TPU v7x, 512 devices: a whole 4x8x8 slice. The times are simulated.
512 devices in a mesh: wave: 64 (over x, y, core), fld: 8 (over z).
Axes of the slice: x: 4, y: 8, z: 8, core: 2. Of those that a mesh axis runs over, the one named last changes fastest.
Arguments:
- spec_coeffs: bfloat16 [640, 2, 641, 1024], P('wave', None, None, 'fld'), may hold values from -6 to 6
- legendre: bfloat16 [640, 2, 641, 128], P('wave', None, None, 'fld'), may hold values from -0.15625 to 0.15625
- pair_lower: int32 [640], replicated, may hold values from 0 to 639, each once
- slot_latitude: int32 [256], replicated, may hold values from 0 to 255, each once
- cycle_points: int32 [128], replicated, may hold values from 20 to 5136, as said below
Outputs:
- fourier_bands: bfloat16 [256, 1280, 1024], P('wave', None, 'fld')
Inputs may be any that keep to these rules, and one draw needn't show every extreme that they name: Pair slot p holds wavenumbers pair_lower[p] and 1279 - pair_lower[p]; every value appears once. Row s holds northern cycle v for v < 128 and southern cycle v - 128 otherwise, v = slot_latitude[s]; every value appears once. `cycle_points`: each entry is 4 j + 16 for a distinct cycle number j from 1 to 1280; cycles 1 and 1280 are always among them.
All inputs are finite; a program needn't handle non-finite values.
Results may differ from a plain program's by a relative error of at most 0.001.
Values may be sent and summed in bfloat16 or wider, within the bound.
No kernel may reach another device: no remote copies, remote signals or barrier semaphores. Data moves between devices by JAX's collectives and lax.ppermute only.
A program may use at most 64 MiB of HBM per device.

v0:
```python
import jax
import jax.numpy as jnp
from jax import lax
from jax.sharding import PartitionSpec as P


def owner_masks(lower_wave, truncation, half_slots):
    slot_index = 2 * lax.broadcasted_iota(jnp.int32, (2, half_slots), 1) + lax.broadcasted_iota(
        jnp.int32, (2, half_slots), 0
    )
    slot_index = slot_index[None]
    length = truncation + 1 - lower_wave
    begin = length + length % 2
    lower_b = lower_wave[:, None, None]
    length_b = length[:, None, None]
    begin_b = begin[:, None, None]
    in_lower = slot_index < length_b
    in_upper = (slot_index >= begin_b) & (slot_index <= begin_b + lower_b)
    return jnp.stack([in_lower, in_upper], axis=3).astype(jnp.bfloat16)


def legendre_sums(table_piece, masked):
    parity_sums = jnp.einsum(
        "pskl,pskhc->slphc", table_piece, masked, preferred_element_type=jnp.float32
    )
    north_part = parity_sums[0] + parity_sums[1]
    south_part = parity_sums[0] - parity_sums[1]
    return jnp.stack([north_part, south_part]).astype(jnp.bfloat16)


def select_bands(fourier, slot_latitude, cycle_points, lower_wave, truncation):
    cycles = fourier.shape[1]
    fourier = fourier.reshape((2 * cycles,) + fourier.shape[2:])
    picked = jnp.take(fourier, slot_latitude, axis=0)
    cycle_limit = jnp.take(cycle_points, slot_latitude % cycles)
    pair_waves = jnp.stack([lower_wave, truncation - lower_wave], axis=1)
    kept_mask = (2 * pair_waves[None] < cycle_limit[:, None, None]).astype(jnp.bfloat16)
    return picked * kept_mask[..., None]


def on_device(spec_coeffs, legendre, pair_lower, slot_latitude, cycle_points):
    pairs_dev = spec_coeffs.shape[0]
    half_slots = spec_coeffs.shape[2]
    columns = spec_coeffs.shape[3]
    truncation = 2 * half_slots - 3
    all_pairs = pair_lower.shape[0]
    n_wave = lax.axis_size("wave")
    lat_dev = slot_latitude.shape[0] // n_wave
    local_lower = lax.dynamic_slice_in_dim(
        pair_lower, lax.axis_index("wave") * pairs_dev, pairs_dev
    )
    masks = owner_masks(local_lower, truncation, half_slots)
    masked = spec_coeffs[:, :, :, None, :] * masks[..., None]
    fourier = legendre_sums(lax.all_gather(legendre, "fld", axis=3, tiled=True), masked)
    picked = select_bands(fourier, slot_latitude, cycle_points, local_lower, truncation)
    received = lax.all_to_all(picked, "wave", split_axis=0, concat_axis=1, tiled=True)
    received = received.reshape(lat_dev, 2 * all_pairs, columns)
    pair_index = jnp.arange(all_pairs, dtype=jnp.int32)
    wave_of = jnp.zeros((truncation + 1,), jnp.int32).at[pair_lower].set(2 * pair_index)
    wave_of = wave_of.at[truncation - pair_lower].set(2 * pair_index + 1)
    return jnp.take(received, wave_of, axis=1)


def solution(mesh):
    placed = (P("wave", None, None, "fld"), P("wave", None, None, "fld"), P(), P(), P())
    return jax.shard_map(
        on_device, mesh=mesh, in_specs=placed, out_specs=P("wave", None, "fld"), check_vma=False
    )
```

profile of v0, /device:TPU:1, one launch (start us, length us, event | category | flops | bytes accessed | tf_op | source)
XLA Modules:
  0.0 160.4 jit_solution(15402695646475738006)
XLA Ops:
  6.5 0.0 copy-start
  6.5 0.0 all-gather.2.cloned.1.call-start
  6.5 1.9 %copy.17 = bf16[10,2,641,16]{2,3,0,1:T(8,128)(2,1)} copy(bf16[10,2,641,16]{2,3,1,0:T(8,128)(2,1)} %param.6) | data formatting | bytes 820480 | tf_op args[1]
  8.4 0.0 all-gather.2.cloned.1.call-update
  8.4 0.0 copy-start.1
  8.4 0.0 copy-start.2
  8.4 2.4 %copy.16 = bf16[10,2,641,128]{3,2,0,1:T(8,128)(2,1)S(1)} copy(bf16[10,2,641,128]{3,1,2,0:T(2,128)(2,1)} %param.5) | data formatting | bytes 6563840 | tf_op args[0]
  10.8 0.0 copy-done.1
  10.8 0.1 subtract_bitcast_fusion
  10.9 0.1 copy.20
  11.0 0.0 copy-done.2
  11.1 1.9 %gather_fusion.1 = s32[256]{0:T(256)S(1)} fusion(s32[128]{0:T(128)S(1)} %copy-done, s32[1024]{0:T(1024)S(1)} %get-tuple-element.18), kind=kCustom, calls=%fused_computation.1 | custom fusion | bytes 3072 | tf_op jit(solution)/shard_map/jit(_take)/gather | solution.py:35
  13.0 0.2 broadcast_compare_fusion
  13.2 0.2 add_convert_fusion.1
  13.4 1.3 compare_convert_fusion
  14.7 56.1 %all-gather.2.cloned.1.call-done = bf16[10,2,641,128]{2,3,0,1:T(8,128)(2,1)} async-done(((bf16[10,2,641,16]{2,3,0,1:T(8,128)(2,1)}), bf16[10,2,641,128]{2,3,0,1:T(8,128)(2,1)}) %all-gather.2.cloned.1.call-update) | async-done | bytes 3281936 | tf_op jit(solution)/shard_map/all_gather | solution.py:54
  70.8 8.7 %fusion.5 = f32[2,128,10,2,128]{4,1,3,2,0:T(8,128)S(1)} fusion(bf16[10,2,641,128]{2,3,0,1:T(8,128)(2,1)} %all-gather.2.cloned.1.call-done, bf16[10,2,641,2]{2,3,0,1:T(2,128)(2,1)S(1)} %add_convert_fusion.1, bf16[10,2,641,128]{3,2,0,1:T(8,128)(2,1)S(1)} %copy.16), kind=kOutput, calls=%fused_computation.12 | convolution fusion | flops 843453440 | bytes 9236560 | tf_op jit(solution)/shard_map/pskl,pskhc->slphc/dot_general | solution.py:23
  79.5 0.3 add_convert_fusion
  79.8 0.1 pad_maximum_fusion
  80.0 0.1 copy.18
  80.1 1.3 copy.19
  81.4 3.3 %gather_fusion = bf16[256,10,2,128]{3,2,1,0:T(2,128)(2,1)S(1)} fusion(bf16[256,10,2,128]{3,2,1,0:T(2,128)(2,1)S(1)} %copy.19, s32[1024]{0:T(1024)S(1)} %get-tuple-element.19), kind=kCustom, calls=%fused_computation | custom fusion | bytes 2622464 | tf_op jit(solution)/shard_map/jit(_take)/gather | solution.py:34
  84.7 6.9 %fusion.10 = bf16[256,10,2,128]{3,2,1,0:T(2,128)(2,1)} fusion(bf16[256,10,2,128]{3,2,1,0:T(2,128)(2,1)S(1)} %gather_fusion, pred[256]{0:T(512)(128)(4,1)S(1)} %compare_and_fusion.2, bf16[256,10,2]{2,1,0:T(8,128)(2,1)} %compare_convert_fusion), kind=kLoop, calls=%fused_computation.17 | loop fusion | flops 1310720 | bytes 2631936 | tf_op jit(solution)/shard_map/mul | solution.py:38
  91.7 10.4 %all-to-all-start = ((bf16[256,10,2,128]{3,2,1,0:T(2,128)(2,1)}), bf16[256,10,2,128]{3,2,1,0:T(2,128)(2,1)S(1)}, u32[]{:S(2)}, u32[]{:S(2)}) async-start(bf16[256,10,2,128]{3,2,1,0:T(2,128)(2,1)} %fusion.10), calls=%async_computation | async-start | bytes 2621440 | tf_op jit(solution)/shard_map/all_to_all | solution.py:56
  102.1 4.1 %scatter_custom_fusion = s32[1280]{0:T(1024)S(1)} fusion(s32[640]{0:T(1024)S(1)} %get-tuple-element.14, s32[640]{0:T(1024)S(1)} %get-tuple-element.20, s32[]{:T(128)} %constant.55.clone.1), kind=kCustom, calls=%fused_computation.31 | custom fusion | bytes 5124 | tf_op jit(solution)/shard_map/scatter | solution.py:59
  106.2 4.3 %scatter_fusion = s32[1280]{0:T(1024)S(1)} fusion(s32[1280]{0:T(1024)S(1)} %scatter_custom_fusion, s32[640]{0:T(1024)S(1)} %get-tuple-element.13, s32[640]{0:T(1024)S(1)} %broadcast_add_fusion), kind=kCustom, calls=%fused_computation.4 | custom fusion | bytes 10240 | tf_op jit(solution)/shard_map/scatter | solution.py:60
  110.5 25.7 %all-to-all-done = bf16[256,10,2,128]{3,2,1,0:T(2,128)(2,1)S(1)} async-done(((bf16[256,10,2,128]{3,2,1,0:T(2,128)(2,1)}), bf16[256,10,2,128]{3,2,1,0:T(2,128)(2,1)S(1)}, u32[]{:S(2)}, u32[]{:S(2)}) %all-to-all-start) | async-done | bytes 1310752 | tf_op jit(solution)/shard_map/all_to_all | solution.py:56
  136.2 0.9 copy.21
  137.1 6.1 %copy.22 = bf16[4,1280,128]{2,0,1:T(4,128)(2,1)S(1)} copy(bf16[4,1280,128]{2,1,0:T(8,128)(2,1)S(1)} %bitcast.21) | data formatting | bytes 2621440 | tf_op jit(solution)/shard_map/reshape | solution.py:57
  143.3 4.4 %gather_fusion.2 = bf16[1280,4,128]{2,1,0:T(4,128)(2,1)S(1)} fusion(bf16[4,1280,128]{2,0,1:T(4,128)(2,1)S(1)} %copy.22, s32[2048]{0:T(1024)S(1)} %pad_clamp_fusion), kind=kCustom, calls=%fused_computation.2 | custom fusion | bytes 2626560 | tf_op jit(solution)/shard_map/jit(_take)/gather | solution.py:61
  147.6 4.7 %select_bitcast_fusion = bf16[4,1280,128]{2,0,1:T(4,128)(2,1)S(1)} fusion(bf16[1280,4,128]{2,1,0:T(4,128)(2,1)S(1)} %gather_fusion.2, pred[1280]{0:T(1024)(128)(4,1)S(1)} %compare_and_fusion.1), kind=kLoop, calls=%fused_computation.14 | loop fusion | flops 655360 | bytes 2622720 | tf_op jit(solution)/shard_map/jit(_take)/select_n | solution.py:61
  152.4 1.2 copy.23
  (14 shorter events, 0.1 us)
Async XLA Ops:
  6.5 4.5 %copy-start = (s32[128]{0:T(128)S(1)}, s32[128]{0:T(128)}, u32[]{:S(2)}) copy-start(s32[128]{0:T(128)} %param.9) | copy-start | bytes 1540
  6.5 64.2 %all-gather.2.cloned.1.call-start = ((), (), s32[]{:S(2)}) async-start(), calls=%async_computation.1 | async-start | bytes 4423680 | tf_op jit(solution)/shard_map/all_gather | solution.py:54
  8.4 2.4 %copy-start.1 = (s32[640]{0:T(1024)S(1)}, s32[640]{0:T(1024)}, u32[]{:S(2)}) copy-start(s32[640]{0:T(1024)} %param.7) | copy-start | bytes 7684
  8.4 2.6 %copy-start.2 = (s32[256]{0:T(256)S(1)}, s32[256]{0:T(256)}, u32[]{:S(2)}) copy-start(s32[256]{0:T(256)} %param.8) | copy-start | bytes 3076
  91.7 44.6 %all-to-all-start = ((bf16[256,10,2,128]{3,2,1,0:T(2,128)(2,1)}), bf16[256,10,2,128]{3,2,1,0:T(2,128)(2,1)S(1)}, u32[]{:S(2)}, u32[]{:S(2)}) async-start(bf16[256,10,2,128]{3,2,1,0:T(2,128)(2,1)} %fusion.10), calls=%async_computation | async-start | bytes 2621440 | tf_op jit(solution)/shard_map/all_to_all | solution.py:56
Sparse Core Ops, SparseCore 0:
  9.4 61.2 all-gather.1
where the time goes:
time: 161 us; the launch traced here: 160 us
  waiting for transfers between devices  81.8 us (51%)
  local copies, waits for them, and re-layouts  32 us (20%)
  other arithmetic  14 us (9%)
  between operations  13.6 us (8%)
  starting transfers between devices  10.4 us (6%)
  matrix products  8.71 us (5%)
    all_gather x1, waiting for transfers between devices, on_device(): lax.all_gather(legendre, 'fld', axis=3, tiled=True)  56.1 us
    all_to_all x1, waiting for transfers between devices, on_device(): lax.all_to_all(picked, 'wave', split_axis=0, concat_axis=1, tiled=True)  25.7 us
    all_to_all x1, starting transfers between devices, on_device(): lax.all_to_all(picked, 'wave', split_axis=0, concat_axis=1, tiled=True)  10.4 us
    dot_general x1, matrix products, legendre_sums(): jnp.einsum('pskl,pskhc->slphc', table_piece, masked, preferred_element_ty...  8.71 us
    mul x1, other arithmetic, select_bands(): return picked * kept_mask[..., None]  6.94 us
    reshape x1, local copies, waits for them, and re-layouts, on_device(): received = received.reshape(lat_dev, 2 * all_pairs, columns)  6.12 us
    select_n x2, other arithmetic, on_device(): return jnp.take(received, wave_of, axis=1)  4.72 us
    gather x1, local copies, waits for them, and re-layouts, on_device(): return jnp.take(received, wave_of, axis=1)  4.36 us
  transfers between devices with their start and end apart: 2, of which 2 were waited for; matrix products, arithmetic and copies ran while one was open for 9% of the time, Pallas kernels for 0%

commit v1 on v0

v1 whole, which is shorter than its diff:
```python
import functools

import jax
import jax.numpy as jnp
from jax import lax
from jax.experimental import pallas as pl
from jax.experimental.pallas import tpu as pltpu
from jax.sharding import PartitionSpec as P

BF = jnp.bfloat16
F32 = jnp.float32
LANES = 128
ROWS = 16
VMEM_LIMIT = 48 * 1024 * 1024


def whole(shape):
    return pl.BlockSpec(shape, lambda *_: (0,) * len(shape))


def pack_kernel(table_ref, *out_refs):
    pairs, _, rows, half_slots = table_ref.shape
    blocks = half_slots // LANES
    group = pairs // len(out_refs)
    lane = lax.broadcasted_iota(jnp.int32, (rows, LANES), 1)
    for g, out_ref in enumerate(out_refs):
        last = jnp.zeros((rows, LANES), F32)
        for i in range(group):
            for r in range(2):
                for b in range(blocks):
                    out_ref[(2 * i + r) * blocks + b] = table_ref[g * group + i, r, :, b * LANES:(b + 1) * LANES]
                tail = table_ref[g * group + i, r, :, half_slots - 1:half_slots].astype(F32)
                last = jnp.where(lane == 2 * i + r, tail, last)
        out_ref[2 * group * blocks] = last.astype(BF)


def pack_table(table, groups):
    pairs, _, rows, half_slots = table.shape
    assert half_slots % LANES == 1
    length = 2 * (pairs // groups) * (half_slots // LANES) + 1
    out = jax.ShapeDtypeStruct((length, rows, LANES), BF)
    return pl.pallas_call(
        pack_kernel,
        out_shape=[out] * groups,
        compiler_params=pltpu.CompilerParams(vmem_limit_bytes=VMEM_LIMIT),
        name="pack_table",
    )(table)


def mask_kernel(truncation, group, place_ref, lower_ref, spec_ref, out_ref):
    _, _, half_slots, columns = spec_ref.shape
    full = half_slots - 1
    i = pl.program_id(0)
    q = lower_ref[place_ref[0] * pl.num_programs(0) + i]
    length = truncation + 1 - q
    begin = length + lax.rem(length, 2)
    for r in range(2):
        slot = 2 * lax.broadcasted_iota(jnp.int32, (full, columns), 0) + r
        coeffs = spec_ref[0, r, :full, :].astype(F32)
        out_ref[0, r, :full, :columns] = jnp.where(slot < length, coeffs, 0.0).astype(BF)
        out_ref[0, r, :full, columns:] = jnp.where((slot >= begin) & (slot <= begin + q), coeffs, 0.0).astype(BF)
        row = lax.broadcasted_iota(jnp.int32, (LANES, columns), 0)
        mine = row == 2 * lax.rem(i, group) + r
        last = 2 * full + r
        tail = spec_ref[0, r, full:, :].astype(F32)
        out_ref[0, r, full:, :columns] = jnp.where(mine & (last < length), tail, 0.0).astype(BF)
        out_ref[0, r, full:, columns:] = jnp.where(mine & (last >= begin) & (last <= begin + q), tail, 0.0).astype(BF)


def mask_coeffs(place, pair_lower, spec, group):
    pairs, _, half_slots, columns = spec.shape
    depth = half_slots - 1 + LANES
    smem = pl.BlockSpec(memory_space=pltpu.SMEM)
    return pl.pallas_call(
        functools.partial(mask_kernel, 2 * half_slots - 3, group),
        grid=(pairs,),
        in_specs=[smem, smem, pl.BlockSpec((1, 2, half_slots, columns), lambda i: (i, 0, 0, 0))],
        out_specs=pl.BlockSpec((1, 2, depth, 2 * columns), lambda i: (i, 0, 0, 0)),
        out_shape=jax.ShapeDtypeStruct((pairs, 2, depth, 2 * columns), BF),
        compiler_params=pltpu.CompilerParams(vmem_limit_bytes=VMEM_LIMIT),
        name="mask_coeffs",
    )(place, pair_lower, spec)


def sums_kernel(truncation, n_wave, groups, place_ref, lower_ref, slots_ref, points_ref, *refs):
    coeff_refs = refs[:groups]
    shard_refs = [refs[groups + 8 * g:groups + 8 * g + 8] for g in range(groups)]
    out_ref, rows_ref, pick_ref, limit_ref = refs[groups + 8 * groups:]
    i = pl.program_id(0)
    steps = pl.num_programs(0)
    pairs = steps * groups
    lats, half = pick_ref.shape[0], pick_ref.shape[0] // 2
    lat_dev = lats // n_wave
    per_dev = out_ref.shape[0] // n_wave
    columns = out_ref.shape[1]
    blocks = coeff_refs[0].shape[2] // LANES - 1

    @pl.when(i == 0)
    def _():
        slots = slots_ref[...]
        cycle = lax.rem(slots, half)
        held = lax.rem(cycle - place_ref[1] * ROWS + half, half) + (slots // half) * half
        index = lax.broadcasted_iota(jnp.int32, (lats, lats), 0)
        pick_ref[...] = jnp.where(index == held, 1.0, 0.0).T.astype(BF)
        index = lax.broadcasted_iota(jnp.int32, (half, lats), 0)
        points = jnp.where(index == cycle, 1.0, 0.0).T * points_ref[...].astype(F32)
        limit_ref[...] = jnp.broadcast_to(jnp.sum(points, axis=1, keepdims=True), limit_ref.shape)

    for g in range(groups):
        pair = i + g * steps
        sums = []
        for r in range(2):
            def block(b):
                return jnp.concatenate([ref[b] for ref in shard_refs[g]], axis=0)

            table = [block((2 * i + r) * blocks + b) for b in range(blocks)] + [block(2 * steps * blocks)]
            sums.append(jnp.dot(jnp.concatenate(table, axis=1), coeff_refs[g][0, r], preferred_element_type=F32))
        both = jnp.concatenate([sums[0] + sums[1], sums[0] - sums[1]], axis=0).astype(BF)
        picked = jnp.dot(pick_ref[...], both, preferred_element_type=F32)
        q = lower_ref[place_ref[0] * pairs + pair]
        for h in range(2):
            wave = (q if h == 0 else truncation - q).astype(F32)
            kept = jnp.where(2.0 * wave < limit_ref[...], picked[:, h * columns:(h + 1) * columns], 0.0)
            for lat in range(lat_dev):
                start = (2 * pair + h) * lat_dev + lat
                rows_ref[pl.ds(start, n_wave, stride=per_dev), :] = kept[lat * n_wave:(lat + 1) * n_wave]

    @pl.when(i == steps - 1)
    def _():
        def body(d, carry):
            at = pl.ds(pl.multiple_of(d * per_dev, per_dev), per_dev)
            out_ref[at, :] = rows_ref[at, :].astype(BF)
            return carry

        lax.fori_loop(0, n_wave, body, 0, unroll=8)


def legendre_sums(place, pair_lower, slots, points, coeffs, shards, n_wave, truncation):
    pairs, _, depth, wide = coeffs.shape
    groups = len(shards)
    steps = pairs // groups
    columns = wide // 2
    lats = slots.shape[1]
    per_dev = 2 * pairs * (lats // n_wave)
    smem = pl.BlockSpec(memory_space=pltpu.SMEM)
    flat = [x for group in shards for x in group]
    return pl.pallas_call(
        functools.partial(sums_kernel, truncation, n_wave, groups),
        grid=(steps,),
        in_specs=[smem, smem, whole(slots.shape), whole(points.shape)]
        + [pl.BlockSpec((1, 2, depth, wide), lambda i, g=g: (i + g * steps, 0, 0, 0)) for g in range(groups)]
        + [whole(x.shape) for x in flat],
        out_specs=whole((n_wave * per_dev, columns)),
        out_shape=jax.ShapeDtypeStruct((n_wave * per_dev, columns), BF),
        scratch_shapes=[
            pltpu.VMEM((n_wave * per_dev, columns), F32),
            pltpu.VMEM((lats, lats), BF),
            pltpu.VMEM((lats, columns), F32),
        ],
        compiler_params=pltpu.CompilerParams(vmem_limit_bytes=VMEM_LIMIT),
        name="legendre_sums",
    )(place, pair_lower, slots, points, *([coeffs] * groups), *flat)


def place_kernel(lat_dev, waves_ref, received_ref, out_ref, rows_ref, held_ref):
    count = waves_ref.shape[1]
    columns = received_ref.shape[1]
    step = received_ref.shape[0] // 64

    def widen(d, carry):
        at = pl.ds(pl.multiple_of(d * step, step), step)
        rows_ref[at, :] = received_ref[at, :].astype(F32)
        return carry

    lax.fori_loop(0, 64, widen, 0, unroll=8)
    for lat in range(lat_dev):
        held_ref[:, lat * columns:(lat + 1) * columns] = rows_ref[pl.ds(lat, count, stride=lat_dev), :].astype(BF)
    tall = 256
    for m in range(0, count, tall):
        index = lax.broadcasted_iota(jnp.int32, (tall, count), 0) + m
        chosen = jnp.where(index == waves_ref[...], 1.0, 0.0).astype(BF)
        placed = jnp.dot(chosen, held_ref[...], preferred_element_type=F32).astype(BF)
        for lat in range(lat_dev):
            out_ref[lat, m:m + tall, :] = placed[:, lat * columns:(lat + 1) * columns]


def place_waves(waves, received, lat_dev):
    count = waves.shape[1]
    columns = received.shape[1]
    return pl.pallas_call(
        functools.partial(place_kernel, lat_dev),
        out_shape=jax.ShapeDtypeStruct((lat_dev, count, columns), BF),
        scratch_shapes=[
            pltpu.VMEM((lat_dev * count, columns), F32),
            pltpu.VMEM((count, lat_dev * columns), BF),
        ],
        compiler_params=pltpu.CompilerParams(vmem_limit_bytes=VMEM_LIMIT),
        name="place_waves",
    )(waves, received)


def gather_ring(groups):
    n = lax.axis_size("fld")
    assert n == 8 and len(groups) == 2

    def up(x):
        return lax.ppermute(x, "fld", [(i, (i + 1) % n) for i in range(n)])

    def down(x):
        return lax.ppermute(x, "fld", [(i, (i - 1) % n) for i in range(n)])

    below, above = [[x] for x in groups], [[x] for x in groups]
    for step in range(n // 2):
        for g in range(2):
            if step < n // 2 - 1 or g == 0:
                below[g].append(up(below[g][-1]))
            if step < n // 2 - 1 or g == 1:
                above[g].append(down(above[g][-1]))
    return [[groups[g]] + above[g][1:] + below[g][:0:-1] for g in range(2)]


def on_device(spec_coeffs, legendre, pair_lower, slot_latitude, cycle_points):
    half_slots = spec_coeffs.shape[2]
    columns = spec_coeffs.shape[3]
    truncation = 2 * half_slots - 3
    n_wave = lax.axis_size("wave")
    lats = slot_latitude.shape[0]
    lat_dev = lats // n_wave
    groups = 2
    place = jnp.stack([lax.axis_index("wave"), lax.axis_index("fld")]).astype(jnp.int32)
    packed = pack_table(jnp.transpose(legendre, (0, 1, 3, 2)), groups)
    shards = gather_ring(packed)
    coeffs = mask_coeffs(place, pair_lower, spec_coeffs, spec_coeffs.shape[0] // groups)
    slots = slot_latitude.reshape(n_wave, lat_dev).T.reshape(1, lats)
    points = cycle_points.reshape(1, lats // 2)
    to_send = legendre_sums(place, pair_lower, slots, points, coeffs, shards, n_wave, truncation)
    to_send = to_send.reshape(n_wave, -1, columns)
    received = lax.all_to_all(to_send, "wave", split_axis=0, concat_axis=0, tiled=True)
    waves = jnp.stack([pair_lower, truncation - pair_lower], axis=1).reshape(1, truncation + 1)
    return place_waves(waves, received.reshape(-1, columns), lat_dev)


def solution(mesh):
    placed = (P("wave", None, None, "fld"), P("wave", None, None, "fld"), P(), P(), P())
    return jax.shard_map(
        on_device, mesh=mesh, in_specs=placed, out_specs=P("wave", None, "fld"), check_vma=False
    )
```

time: 161 us -> 121 us (0.75)
  starting transfers between devices: 10.4 us -> 63.2 us
  waiting for transfers between devices: 81.8 us -> 33.8 us
  local copies, waits for them, and re-layouts: 32 us -> 4.76 us
  Pallas kernels: 0 us -> 18.4 us
  other arithmetic: 14 us -> 0.09 us
  between operations: 13.6 us -> 0.28 us
  matrix products: 8.71 us -> 0 us
    all_gather x1 -> x0, waiting for transfers between devices: 56.1 us -> none  [on_device(): lax.all_gather(legendre, 'fld', axis=3, tiled=True)]
    ppermute x0 -> x14, starting transfers between devices: none -> 48.7 us  [the longest x7 32.4 us: down(): return lax.ppermute(x, 'fld', [(i, (i - 1) % n) for i in range(n)])]
    pallas_call x0 -> x4, Pallas kernels: none -> 18.4 us  [the longest x1 8.22 us: legendre_sums(): pl.pallas_call(functools.partial(sums_kernel, truncation, n_wave, groups)...]
    gather x3 -> x0, local copies, waits for them, and re-layouts: 9.55 us -> none  [the longest x1 4.36 us: on_device(): return jnp.take(received, wave_of, axis=1)]
    dot_general x1 -> x0, matrix products: 8.71 us -> none  [legendre_sums(): jnp.einsum('pskl,pskhc->slphc', table_piece, masked, preferred_element_ty...]
    scatter x2 -> x0, local copies, waits for them, and re-layouts: 8.39 us -> none  [the longest x1 4.29 us: on_device(): wave_of = wave_of.at[truncation - pair_lower].set(2 * pair_index + 1)]
    all_to_all x1, waiting for transfers between devices: 25.7 us -> 33.7 us  [on_device(): lax.all_to_all(to_send, 'wave', split_axis=0, concat_axis=0, tiled=True)]
    mul x3 -> x0, other arithmetic: 6.95 us -> none  [the longest x1 6.94 us: select_bands(): return picked * kept_mask[..., None]]
  transfers between devices with their start and end apart: 2 -> 15, of which waited for: 2 -> 1; matrix products, arithmetic and copies ran while one was open for 9% -> 3% of each run, Pallas kernels for 0% -> 6%
where the time goes in v1:
time: 121 us
  starting transfers between devices  63.2 us (52%)
  waiting for transfers between devices  33.8 us (28%)
  Pallas kernels  18.4 us (15%)
  local copies, waits for them, and re-layouts  4.76 us (4%)
    all_to_all x1, waiting for transfers between devices, on_device(): lax.all_to_all(to_send, 'wave', split_axis=0, concat_axis=0, tiled=True)  33.7 us
    ppermute x7, starting transfers between devices, down(): return lax.ppermute(x, 'fld', [(i, (i - 1) % n) for i in range(n)])  32.4 us
    ppermute x7, starting transfers between devices, up(): return lax.ppermute(x, 'fld', [(i, (i + 1) % n) for i in range(n)])  16.4 us
    all_to_all x1, starting transfers between devices, on_device(): lax.all_to_all(to_send, 'wave', split_axis=0, concat_axis=0, tiled=True)  14.4 us
    pallas_call x1, Pallas kernels, legendre_sums(): pl.pallas_call(functools.partial(sums_kernel, truncation, n_wave, groups)...  8.22 us
    pallas_call x1, Pallas kernels, mask_coeffs(): pl.pallas_call(functools.partial(mask_kernel, 2 * half_slots - 3, group),...  6.91 us
    unnamed x7, local copies, waits for them, and re-layouts  3.42 us
    pallas_call x1, Pallas kernels, place_waves(): pl.pallas_call(functools.partial(place_kernel, lat_dev), out_shape=jax.Sh...  3.2 us
  transfers between devices with their start and end apart: 15, of which 1 were waited for; matrix products, arithmetic and copies ran while one was open for 3% of the time, Pallas kernels for 6%

profile of v1, /device:TPU:1, one launch (start us, length us, event | category | flops | bytes accessed | tf_op | source)
XLA Modules:
  0.0 120.5 jit_solution(10095622705781581036)
XLA Ops:
  0.0 1.0 copy-done
  1.0 0.1 pack_table.1
  1.1 4.8 %collective-permute-start.3 = (bf16[51,16,128]{2,1,0:T(8,128)(2,1)S(1)}, bf16[51,16,128]{2,1,0:T(8,128)(2,1)S(1)}, u32[]{:S(2)}, u32[]{:S(2)}) collective-permute-start(bf16[51,16,128]{2,1,0:T(8,128)(2,1)S(1)} %get-tuple-element.7.refs_2_), channel_id=1, source_target_pairs={{0,1},{1,2},{2,3},{3,4},{4,5},{5,6},{6,7},{7,0},{8,9},{9,10},{10,1... | collective-permute-start | bytes 626696 | tf_op jit(solution)/shard_map/ppermute | solution.py:207
  6.0 8.6 %collective-permute-start.7 = (bf16[51,16,128]{2,1,0:T(8,128)(2,1)S(1)}, bf16[51,16,128]{2,1,0:T(8,128)(2,1)S(1)}, u32[]{:S(2)}, u32[]{:S(2)}) collective-permute-start(bf16[51,16,128]{2,1,0:T(8,128)(2,1)S(1)} %get-tuple-element.8.refs_10_), channel_id=1, source_target_pairs={{0,7},{1,0},{2,1},{3,2},{4,3},{5,4},{6,5},{7,6},{8,15},{9,8},{10,9... | collective-permute-start | bytes 626696 | tf_op jit(solution)/shard_map/ppermute | solution.py:210
  14.6 3.4 %collective-permute-start = (bf16[51,16,128]{2,1,0:T(8,128)(2,1)S(1)}, bf16[51,16,128]{2,1,0:T(8,128)(2,1)S(1)}, u32[]{:S(2)}, u32[]{:S(2)}) collective-permute-start(bf16[51,16,128]{2,1,0:T(8,128)(2,1)S(1)} %get-tuple-element.7.refs_2_), channel_id=1, source_target_pairs={{0,7},{1,0},{2,1},{3,2},{4,3},{5,4},{6,5},{7,6},{8,15},{9,8},{10,9... | collective-permute-start | bytes 626696 | tf_op jit(solution)/shard_map/ppermute | solution.py:210
  17.9 1.9 %collective-permute-start.11 = (bf16[51,16,128]{2,1,0:T(8,128)(2,1)S(1)}, bf16[51,16,128]{2,1,0:T(8,128)(2,1)S(1)}, u32[]{:S(2)}, u32[]{:S(2)}) collective-permute-start(bf16[51,16,128]{2,1,0:T(8,128)(2,1)S(1)} %get-tuple-element.8.refs_10_), channel_id=1, source_target_pairs={{0,1},{1,2},{2,3},{3,4},{4,5},{5,6},{6,7},{7,0},{8,9},{9,10},{10,1... | collective-permute-start | bytes 626696 | tf_op jit(solution)/shard_map/ppermute | solution.py:207
  19.9 1.9 %collective-permute-start.4 = (bf16[51,16,128]{2,1,0:T(8,128)(2,1)S(1)}, bf16[51,16,128]{2,1,0:T(8,128)(2,1)S(1)}, u32[]{:S(2)}, u32[]{:S(2)}) collective-permute-start(bf16[51,16,128]{2,1,0:T(8,128)(2,1)S(1)} %collective-permute-done.3.refs_9_), channel_id=1, source_target_pairs={{0,1},{1,2},{2,3},{3,4},{4,5},{5,6},{6,7},{7,0},{8,9},{9,10},{10,1... | collective-permute-start | bytes 626696 | tf_op jit(solution)/shard_map/ppermute | solution.py:207
  21.8 0.0 collective-permute-done.7.refs_11_
  21.8 4.6 %collective-permute-start.8 = (bf16[51,16,128]{2,1,0:T(8,128)(2,1)S(1)}, bf16[51,16,128]{2,1,0:T(8,128)(2,1)S(1)}, u32[]{:S(2)}, u32[]{:S(2)}) collective-permute-start(bf16[51,16,128]{2,1,0:T(8,128)(2,1)S(1)} %collective-permute-done.7.refs_11_), channel_id=1, source_target_pairs={{0,7},{1,0},{2,1},{3,2},{4,3},{5,4},{6,5},{7,6},{8,15},{9,8},{10,9... | collective-permute-start | bytes 626696 | tf_op jit(solution)/shard_map/ppermute | solution.py:210
  26.4 3.4 %collective-permute-start.1 = (bf16[51,16,128]{2,1,0:T(8,128)(2,1)S(1)}, bf16[51,16,128]{2,1,0:T(8,128)(2,1)S(1)}, u32[]{:S(2)}, u32[]{:S(2)}) collective-permute-start(bf16[51,16,128]{2,1,0:T(8,128)(2,1)S(1)} %collective-permute-done.refs_3_), channel_id=1, source_target_pairs={{0,7},{1,0},{2,1},{3,2},{4,3},{5,4},{6,5},{7,6},{8,15},{9,8},{10,9... | collective-permute-start | bytes 626696 | tf_op jit(solution)/shard_map/ppermute | solution.py:210
  29.8 1.9 %collective-permute-start.12 = (bf16[51,16,128]{2,1,0:T(8,128)(2,1)S(1)}, bf16[51,16,128]{2,1,0:T(8,128)(2,1)S(1)}, u32[]{:S(2)}, u32[]{:S(2)}) collective-permute-start(bf16[51,16,128]{2,1,0:T(8,128)(2,1)S(1)} %collective-permute-done.11.refs_17_), channel_id=1, source_target_pairs={{0,1},{1,2},{2,3},{3,4},{4,5},{5,6},{6,7},{7,0},{8,9},{9,10},{10,1... | collective-permute-start | bytes 626696 | tf_op jit(solution)/shard_map/ppermute | solution.py:207
  31.7 0.0 collective-permute-done.4.refs_8_
  31.7 1.9 %collective-permute-start.5 = (bf16[51,16,128]{2,1,0:T(8,128)(2,1)S(1)}, bf16[51,16,128]{2,1,0:T(8,128)(2,1)S(1)}, u32[]{:S(2)}, u32[]{:S(2)}) collective-permute-start(bf16[51,16,128]{2,1,0:T(8,128)(2,1)S(1)} %collective-permute-done.4.refs_8_), channel_id=1, source_target_pairs={{0,1},{1,2},{2,3},{3,4},{4,5},{5,6},{6,7},{7,0},{8,9},{9,10},{10,1... | collective-permute-start | bytes 626696 | tf_op jit(solution)/shard_map/ppermute | solution.py:207
  33.7 4.6 %collective-permute-start.9 = (bf16[51,16,128]{2,1,0:T(8,128)(2,1)S(1)}, bf16[51,16,128]{2,1,0:T(8,128)(2,1)S(1)}, u32[]{:S(2)}, u32[]{:S(2)}) collective-permute-start(bf16[51,16,128]{2,1,0:T(8,128)(2,1)S(1)} %collective-permute-done.8.refs_12_), channel_id=1, source_target_pairs={{0,7},{1,0},{2,1},{3,2},{4,3},{5,4},{6,5},{7,6},{8,15},{9,8},{10,9... | collective-permute-start | bytes 626696 | tf_op jit(solution)/shard_map/ppermute | solution.py:210
  38.2 0.0 collective-permute-done.1.refs_4_
  38.2 3.4 %collective-permute-start.2 = (bf16[51,16,128]{2,1,0:T(8,128)(2,1)S(1)}, bf16[51,16,128]{2,1,0:T(8,128)(2,1)S(1)}, u32[]{:S(2)}, u32[]{:S(2)}) collective-permute-start(bf16[51,16,128]{2,1,0:T(8,128)(2,1)S(1)} %collective-permute-done.1.refs_4_), channel_id=1, source_target_pairs={{0,7},{1,0},{2,1},{3,2},{4,3},{5,4},{6,5},{7,6},{8,15},{9,8},{10,9... | collective-permute-start | bytes 626696 | tf_op jit(solution)/shard_map/ppermute | solution.py:210
  41.6 1.9 %collective-permute-start.13 = (bf16[51,16,128]{2,1,0:T(8,128)(2,1)S(1)}, bf16[51,16,128]{2,1,0:T(8,128)(2,1)S(1)}, u32[]{:S(2)}, u32[]{:S(2)}) collective-permute-start(bf16[51,16,128]{2,1,0:T(8,128)(2,1)S(1)} %collective-permute-done.12.refs_16_), channel_id=1, source_target_pairs={{0,1},{1,2},{2,3},{3,4},{4,5},{5,6},{6,7},{7,0},{8,9},{9,10},{10,1... | collective-permute-start | bytes 626696 | tf_op jit(solution)/shard_map/ppermute | solution.py:207
  43.6 0.0 collective-permute-done.5.refs_7_
  43.6 1.9 %collective-permute-start.6 = (bf16[51,16,128]{2,1,0:T(8,128)(2,1)S(1)}, bf16[51,16,128]{2,1,0:T(8,128)(2,1)S(1)}, u32[]{:S(2)}, u32[]{:S(2)}) collective-permute-start(bf16[51,16,128]{2,1,0:T(8,128)(2,1)S(1)} %collective-permute-done.5.refs_7_), channel_id=1, source_target_pairs={{0,1},{1,2},{2,3},{3,4},{4,5},{5,6},{6,7},{7,0},{8,9},{9,10},{10,1... | collective-permute-start | bytes 626696 | tf_op jit(solution)/shard_map/ppermute | solution.py:207
  45.5 4.6 %collective-permute-start.10 = (bf16[51,16,128]{2,1,0:T(8,128)(2,1)S(1)}, bf16[51,16,128]{2,1,0:T(8,128)(2,1)S(1)}, u32[]{:S(2)}, u32[]{:S(2)}) collective-permute-start(bf16[51,16,128]{2,1,0:T(8,128)(2,1)S(1)} %collective-permute-done.9.refs_13_), channel_id=1, source_target_pairs={{0,7},{1,0},{2,1},{3,2},{4,3},{5,4},{6,5},{7,6},{8,15},{9,8},{10,9... | collective-permute-start | bytes 626696 | tf_op jit(solution)/shard_map/ppermute | solution.py:210
  50.1 0.8 reshape.19
  50.9 0.1 copy.8
  51.0 0.1 reshape.20.slots_ref
  51.0 2.4 %copy.9.spec_ref = bf16[10,2,641,128]{3,2,1,0:T(8,128)(2,1)S(1)} copy(bf16[10,2,641,128]{3,1,2,0:T(2,128)(2,1)} %param.5) | data formatting | bytes 6563840 | tf_op args[0]
  53.4 0.1 pad_add_fusion.1.place_ref
  53.5 6.9 %mask_coeffs.1.refs_0_.refs_1_ = bf16[10,2,768,256]{3,2,1,0:T(8,128)(2,1)} custom-call(s32[2]{0:T(128)S(1)} %pad_add_fusion.1.place_ref, s32[640]{0:T(1024)S(1)} %copy-done.1, bf16[10,2,641,128]{3,2,1,0:T(8,128)(2,1)S(1)} %copy.9.spec_ref), custom_call_target="tpu_custom_call" | custom-call | tf_op jit(solution)/shard_map/mask_coeffs/pallas_call | solution.py:74
  60.4 8.2 %legendre_sums.1 = bf16[5120,128]{1,0:T(8,128)(2,1)} custom-call(s32[2]{0:T(128)S(1)} %pad_add_fusion.1.place_ref, s32[640]{0:T(1024)S(1)} %copy-done.1, s32[1,256]{1,0:T(1,128)S(1)} %reshape.20.slots_ref, s32[1,128]{1,0:T(1,128)S(1)} %bitcast.9, bf16[10,2,768,256]{3,2,1,0:T(8,128)(2,1)} %mask_coeffs.1.refs_0_.refs_1_, ...), custom_call_target="tpu_custom_call" | custom-call | tf_op jit(solution)/shard_map/legendre_sums/pallas_call | solution.py:147
  68.7 14.4 %all-to-all-start = ((bf16[64,80,128]{2,1,0:T(8,128)(2,1)}), bf16[64,80,128]{2,1,0:T(8,128)(2,1)S(1)}, u32[]{:S(2)}, u32[]{:S(2)}) async-start(bf16[64,80,128]{2,1,0:T(8,128)(2,1)} %bitcast.5), calls=%async_computation | async-start | bytes 2621440 | tf_op jit(solution)/shard_map/all_to_all | solution.py:238
  83.2 0.2 copy.7
  83.4 0.2 reshape.18.waves_ref
  83.6 33.7 %all-to-all-done = bf16[64,80,128]{2,1,0:T(8,128)(2,1)S(1)} async-done(((bf16[64,80,128]{2,1,0:T(8,128)(2,1)}), bf16[64,80,128]{2,1,0:T(8,128)(2,1)S(1)}, u32[]{:S(2)}, u32[]{:S(2)}) %all-to-all-start) | async-done | bytes 1310752 | tf_op jit(solution)/shard_map/all_to_all | solution.py:238
  117.3 3.2 %place_waves.1 = bf16[4,1280,128]{2,1,0:T(8,128)(2,1)} custom-call(s32[1,1280]{1,0:T(1,128)S(1)} %reshape.18.waves_ref, bf16[5120,128]{1,0:T(8,128)(2,1)S(1)} %bitcast.7), custom_call_target="tpu_custom_call" | custom-call | tf_op jit(solution)/shard_map/place_waves/pallas_call | solution.py:190
  (19 shorter events, 0.1 us)
Async XLA Ops:
  0.0 1.0 copy-start
  1.1 18.7 %collective-permute-start.3 = (bf16[51,16,128]{2,1,0:T(8,128)(2,1)S(1)}, bf16[51,16,128]{2,1,0:T(8,128)(2,1)S(1)}, u32[]{:S(2)}, u32[]{:S(2)}) collective-permute-start(bf16[51,16,128]{2,1,0:T(8,128)(2,1)S(1)} %get-tuple-element.7.refs_2_), channel_id=1, source_target_pairs={{0,1},{1,2},{2,3},{3,4},{4,5},{5,6},{6,7},{7,0},{8,9},{9,10},{10,1... | collective-permute-start | bytes 626696 | tf_op jit(solution)/shard_map/ppermute | solution.py:207
  6.0 15.8 %collective-permute-start.7 = (bf16[51,16,128]{2,1,0:T(8,128)(2,1)S(1)}, bf16[51,16,128]{2,1,0:T(8,128)(2,1)S(1)}, u32[]{:S(2)}, u32[]{:S(2)}) collective-permute-start(bf16[51,16,128]{2,1,0:T(8,128)(2,1)S(1)} %get-tuple-element.8.refs_10_), channel_id=1, source_target_pairs={{0,7},{1,0},{2,1},{3,2},{4,3},{5,4},{6,5},{7,6},{8,15},{9,8},{10,9... | collective-permute-start | bytes 626696 | tf_op jit(solution)/shard_map/ppermute | solution.py:210
  14.6 11.8 %collective-permute-start = (bf16[51,16,128]{2,1,0:T(8,128)(2,1)S(1)}, bf16[51,16,128]{2,1,0:T(8,128)(2,1)S(1)}, u32[]{:S(2)}, u32[]{:S(2)}) collective-permute-start(bf16[51,16,128]{2,1,0:T(8,128)(2,1)S(1)} %get-tuple-element.7.refs_2_), channel_id=1, source_target_pairs={{0,7},{1,0},{2,1},{3,2},{4,3},{5,4},{6,5},{7,6},{8,15},{9,8},{10,9... | collective-permute-start | bytes 626696 | tf_op jit(solution)/shard_map/ppermute | solution.py:210
  17.9 11.8 %collective-permute-start.11 = (bf16[51,16,128]{2,1,0:T(8,128)(2,1)S(1)}, bf16[51,16,128]{2,1,0:T(8,128)(2,1)S(1)}, u32[]{:S(2)}, u32[]{:S(2)}) collective-permute-start(bf16[51,16,128]{2,1,0:T(8,128)(2,1)S(1)} %get-tuple-element.8.refs_10_), channel_id=1, source_target_pairs={{0,1},{1,2},{2,3},{3,4},{4,5},{5,6},{6,7},{7,0},{8,9},{9,10},{10,1... | collective-permute-start | bytes 626696 | tf_op jit(solution)/shard_map/ppermute | solution.py:207
  19.9 11.8 %collective-permute-start.4 = (bf16[51,16,128]{2,1,0:T(8,128)(2,1)S(1)}, bf16[51,16,128]{2,1,0:T(8,128)(2,1)S(1)}, u32[]{:S(2)}, u32[]{:S(2)}) collective-permute-start(bf16[51,16,128]{2,1,0:T(8,128)(2,1)S(1)} %collective-permute-done.3.refs_9_), channel_id=1, source_target_pairs={{0,1},{1,2},{2,3},{3,4},{4,5},{5,6},{6,7},{7,0},{8,9},{9,10},{10,1... | collective-permute-start | bytes 626696 | tf_op jit(solution)/shard_map/ppermute | solution.py:207
  21.8 11.8 %collective-permute-start.8 = (bf16[51,16,128]{2,1,0:T(8,128)(2,1)S(1)}, bf16[51,16,128]{2,1,0:T(8,128)(2,1)S(1)}, u32[]{:S(2)}, u32[]{:S(2)}) collective-permute-start(bf16[51,16,128]{2,1,0:T(8,128)(2,1)S(1)} %collective-permute-done.7.refs_11_), channel_id=1, source_target_pairs={{0,7},{1,0},{2,1},{3,2},{4,3},{5,4},{6,5},{7,6},{8,15},{9,8},{10,9... | collective-permute-start | bytes 626696 | tf_op jit(solution)/shard_map/ppermute | solution.py:210
  26.4 11.8 %collective-permute-start.1 = (bf16[51,16,128]{2,1,0:T(8,128)(2,1)S(1)}, bf16[51,16,128]{2,1,0:T(8,128)(2,1)S(1)}, u32[]{:S(2)}, u32[]{:S(2)}) collective-permute-start(bf16[51,16,128]{2,1,0:T(8,128)(2,1)S(1)} %collective-permute-done.refs_3_), channel_id=1, source_target_pairs={{0,7},{1,0},{2,1},{3,2},{4,3},{5,4},{6,5},{7,6},{8,15},{9,8},{10,9... | collective-permute-start | bytes 626696 | tf_op jit(solution)/shard_map/ppermute | solution.py:210
  29.8 11.8 %collective-permute-start.12 = (bf16[51,16,128]{2,1,0:T(8,128)(2,1)S(1)}, bf16[51,16,128]{2,1,0:T(8,128)(2,1)S(1)}, u32[]{:S(2)}, u32[]{:S(2)}) collective-permute-start(bf16[51,16,128]{2,1,0:T(8,128)(2,1)S(1)} %collective-permute-done.11.refs_17_), channel_id=1, source_target_pairs={{0,1},{1,2},{2,3},{3,4},{4,5},{5,6},{6,7},{7,0},{8,9},{9,10},{10,1... | collective-permute-start | bytes 626696 | tf_op jit(solution)/shard_map/ppermute | solution.py:207
  31.7 11.8 %collective-permute-start.5 = (bf16[51,16,128]{2,1,0:T(8,128)(2,1)S(1)}, bf16[51,16,128]{2,1,0:T(8,128)(2,1)S(1)}, u32[]{:S(2)}, u32[]{:S(2)}) collective-permute-start(bf16[51,16,128]{2,1,0:T(8,128)(2,1)S(1)} %collective-permute-done.4.refs_8_), channel_id=1, source_target_pairs={{0,1},{1,2},{2,3},{3,4},{4,5},{5,6},{6,7},{7,0},{8,9},{9,10},{10,1... | collective-permute-start | bytes 626696 | tf_op jit(solution)/shard_map/ppermute | solution.py:207
  33.7 11.8 %collective-permute-start.9 = (bf16[51,16,128]{2,1,0:T(8,128)(2,1)S(1)}, bf16[51,16,128]{2,1,0:T(8,128)(2,1)S(1)}, u32[]{:S(2)}, u32[]{:S(2)}) collective-permute-start(bf16[51,16,128]{2,1,0:T(8,128)(2,1)S(1)} %collective-permute-done.8.refs_12_), channel_id=1, source_target_pairs={{0,7},{1,0},{2,1},{3,2},{4,3},{5,4},{6,5},{7,6},{8,15},{9,8},{10,9... | collective-permute-start | bytes 626696 | tf_op jit(solution)/shard_map/ppermute | solution.py:210
  38.2 22.2 %collective-permute-start.2 = (bf16[51,16,128]{2,1,0:T(8,128)(2,1)S(1)}, bf16[51,16,128]{2,1,0:T(8,128)(2,1)S(1)}, u32[]{:S(2)}, u32[]{:S(2)}) collective-permute-start(bf16[51,16,128]{2,1,0:T(8,128)(2,1)S(1)} %collective-permute-done.1.refs_4_), channel_id=1, source_target_pairs={{0,7},{1,0},{2,1},{3,2},{4,3},{5,4},{6,5},{7,6},{8,15},{9,8},{10,9... | collective-permute-start | bytes 626696 | tf_op jit(solution)/shard_map/ppermute | solution.py:210
  41.6 18.8 %collective-permute-start.13 = (bf16[51,16,128]{2,1,0:T(8,128)(2,1)S(1)}, bf16[51,16,128]{2,1,0:T(8,128)(2,1)S(1)}, u32[]{:S(2)}, u32[]{:S(2)}) collective-permute-start(bf16[51,16,128]{2,1,0:T(8,128)(2,1)S(1)} %collective-permute-done.12.refs_16_), channel_id=1, source_target_pairs={{0,1},{1,2},{2,3},{3,4},{4,5},{5,6},{6,7},{7,0},{8,9},{9,10},{10,1... | collective-permute-start | bytes 626696 | tf_op jit(solution)/shard_map/ppermute | solution.py:207
  43.6 16.9 %collective-permute-start.6 = (bf16[51,16,128]{2,1,0:T(8,128)(2,1)S(1)}, bf16[51,16,128]{2,1,0:T(8,128)(2,1)S(1)}, u32[]{:S(2)}, u32[]{:S(2)}) collective-permute-start(bf16[51,16,128]{2,1,0:T(8,128)(2,1)S(1)} %collective-permute-done.5.refs_7_), channel_id=1, source_target_pairs={{0,1},{1,2},{2,3},{3,4},{4,5},{5,6},{6,7},{7,0},{8,9},{9,10},{10,1... | collective-permute-start | bytes 626696 | tf_op jit(solution)/shard_map/ppermute | solution.py:207
  45.5 14.9 %collective-permute-start.10 = (bf16[51,16,128]{2,1,0:T(8,128)(2,1)S(1)}, bf16[51,16,128]{2,1,0:T(8,128)(2,1)S(1)}, u32[]{:S(2)}, u32[]{:S(2)}) collective-permute-start(bf16[51,16,128]{2,1,0:T(8,128)(2,1)S(1)} %collective-permute-done.9.refs_13_), channel_id=1, source_target_pairs={{0,7},{1,0},{2,1},{3,2},{4,3},{5,4},{6,5},{7,6},{8,15},{9,8},{10,9... | collective-permute-start | bytes 626696 | tf_op jit(solution)/shard_map/ppermute | solution.py:210
  51.0 2.5 %copy-start.1 = (s32[640]{0:T(1024)S(1)}, s32[640]{0:T(1024)}, u32[]{:S(2)}) copy-start(s32[640]{0:T(1024)} %lower_ref.3) | copy-start | bytes 7684
  53.5 6.9 %copy-start.2 = (s32[128]{0:T(128)S(1)}, s32[128]{0:T(128)}, u32[]{:S(2)}) copy-start(s32[128]{0:T(128)} %param.9) | copy-start | bytes 1540
  68.7 48.6 %all-to-all-start = ((bf16[64,80,128]{2,1,0:T(8,128)(2,1)}), bf16[64,80,128]{2,1,0:T(8,128)(2,1)S(1)}, u32[]{:S(2)}, u32[]{:S(2)}) async-start(bf16[64,80,128]{2,1,0:T(8,128)(2,1)} %bitcast.5), calls=%async_computation | async-start | bytes 2621440 | tf_op jit(solution)/shard_map/all_to_all | solution.py:238

commit v2 on v0

v2 whole, which is shorter than its diff:
```python
import functools

import jax
import jax.numpy as jnp
from jax import lax
from jax.experimental import pallas as pl
from jax.experimental.pallas import tpu as pltpu
from jax.sharding import PartitionSpec as P

BF = jnp.bfloat16
F32 = jnp.float32
LANES = 128
ROWS = 16
PLAIN = 2
VMEM = pl.BlockSpec(memory_space=pltpu.VMEM)
SMEM = pl.BlockSpec(memory_space=pltpu.SMEM)
PARAMS = pltpu.CompilerParams(vmem_limit_bytes=24 * 1024 * 1024)


def pack_kernel(table_ref, out_ref):
    pairs, _, rows, half_slots = table_ref.shape
    blocks = half_slots // LANES
    lane = lax.broadcasted_iota(jnp.int32, (rows, LANES), 1)
    last = jnp.zeros((rows, LANES), F32)
    for i in range(pairs):
        for r in range(2):
            for b in range(blocks):
                out_ref[(2 * i + r) * blocks + b] = table_ref[i, r, :, b * LANES:(b + 1) * LANES]
            tail = table_ref[i, r, :, half_slots - 1:half_slots].astype(F32)
            last = jnp.where(lane == 2 * i + r, tail, last)
    out_ref[2 * pairs * blocks] = last.astype(BF)


def pack_table(table):
    pairs, _, rows, half_slots = table.shape
    assert half_slots % LANES == 1
    return pl.pallas_call(
        pack_kernel,
        in_specs=[VMEM],
        out_specs=VMEM,
        out_shape=jax.ShapeDtypeStruct((2 * pairs * (half_slots // LANES) + 1, rows, LANES), BF),
        compiler_params=PARAMS,
        name="pack_table",
    )(table)


def rows_kernel(place_ref, slots_ref, points_ref, pick_ref, limit_ref):
    slots = slots_ref[...]
    lats = slots.shape[1]
    half = lats // 2
    cycle = lax.rem(slots, half)
    held = lax.rem(cycle - place_ref[1] * ROWS + half, half) + (slots // half) * half
    index = lax.broadcasted_iota(jnp.int32, (lats, lats), 0)
    pick_ref[...] = jnp.where(index == held, 1.0, 0.0).T.astype(BF)
    index = lax.broadcasted_iota(jnp.int32, (half, lats), 0)
    points = jnp.where(index == cycle, 1.0, 0.0).T * points_ref[...].astype(F32)
    limit_ref[...] = jnp.broadcast_to(jnp.sum(points, axis=1, keepdims=True), limit_ref.shape)


def row_order(place, slots, points):
    lats = slots.shape[1]
    return pl.pallas_call(
        rows_kernel,
        in_specs=[SMEM, VMEM, VMEM],
        out_specs=[VMEM, VMEM],
        out_shape=[jax.ShapeDtypeStruct((lats, lats), BF), jax.ShapeDtypeStruct((lats, LANES), F32)],
        compiler_params=PARAMS,
        name="row_order",
    )(place, slots, points)


def sums_kernel(truncation, n_wave, place_ref, lower_ref, pick_ref, limit_ref, spec_ref, *refs):
    shard_refs, out_ref, rows_ref = refs[:9], refs[9], refs[10]
    pairs, _, half_slots, columns = spec_ref.shape
    lat_dev = pick_ref.shape[0] // n_wave
    per_dev = out_ref.shape[0] // n_wave
    full = half_slots - 1
    blocks = full // LANES
    plain = PLAIN * LANES
    group = pairs // 2
    split = 2 * group * blocks

    def block(b, g):
        low, high = shard_refs[4], shard_refs[5]
        parts = [ref[g * split + b] for ref in shard_refs[:4]]
        parts.append(low[b] if g == 0 else high[b])
        parts += [ref[g * split + b] for ref in shard_refs[6:]]
        return jnp.concatenate(parts, axis=0)

    tails = block(split, 1)

    def step(i, carry):
        for g in range(2):
            pair = i + g * group
            q = lower_ref[place_ref[0] * pairs + pair]
            length = truncation + 1 - q
            begin = length + lax.rem(length, 2)
            sums = []
            for r in range(2):
                def owned(slot, coeffs, lower):
                    kept = slot < length if lower else (slot >= begin) & (slot <= begin + q)
                    return jnp.where(kept, coeffs, 0.0).astype(BF)

                first = 2 * i * blocks + r * blocks
                table = [block(first + b, g) for b in range(blocks)]
                below = jnp.dot(
                    jnp.concatenate(table[:PLAIN], axis=1), spec_ref[pair, r, :plain, :], preferred_element_type=F32
                )
                coeffs = spec_ref[pair, r, plain:full, :].astype(F32)
                slot = 2 * (lax.broadcasted_iota(jnp.int32, coeffs.shape, 0) + plain) + r
                row = lax.broadcasted_iota(jnp.int32, (LANES, columns), 0)
                tail = jnp.where(row == 2 * pair + r, spec_ref[pair, r, full:, :].astype(F32), 0.0)
                last = jnp.full((LANES, columns), 2 * full + r, jnp.int32)
                both = [
                    jnp.concatenate([owned(slot, coeffs, lower), owned(last, tail, lower)], axis=0)
                    for lower in (True, False)
                ]
                above = jnp.dot(
                    jnp.concatenate(table[PLAIN:] + [tails], axis=1),
                    jnp.concatenate(both, axis=1),
                    preferred_element_type=F32,
                )
                sums.append((above[:, :columns] + below, above[:, columns:]))
            north = jnp.concatenate([sums[0][h] + sums[1][h] for h in range(2)], axis=1)
            south = jnp.concatenate([sums[0][h] - sums[1][h] for h in range(2)], axis=1)
            fourier = jnp.concatenate([north, south], axis=0).astype(BF)
            picked = jnp.dot(pick_ref[...], fourier, preferred_element_type=F32)
            for h in range(2):
                wave = (q if h == 0 else truncation - q).astype(F32)
                kept = jnp.where(2.0 * wave < limit_ref[...], picked[:, h * columns:(h + 1) * columns], 0.0)
                for lat in range(lat_dev):
                    start = (2 * pair + h) * lat_dev + lat
                    rows_ref[pl.ds(start, n_wave, stride=per_dev), :] = kept[lat * n_wave:(lat + 1) * n_wave]
        return carry

    lax.fori_loop(0, group, step, 0)

    def narrow(d, carry):
        at = pl.ds(pl.multiple_of(d * per_dev, per_dev), per_dev)
        out_ref[at, :] = rows_ref[at, :].astype(BF)
        return carry

    lax.fori_loop(0, n_wave, narrow, 0, unroll=8)


def legendre_sums(place, pair_lower, pick, limit, spec, shards, n_wave, truncation):
    pairs, _, _, columns = spec.shape
    sent = 2 * pairs * pick.shape[0]
    return pl.pallas_call(
        functools.partial(sums_kernel, truncation, n_wave),
        in_specs=[SMEM, SMEM] + [VMEM] * (3 + len(shards)),
        out_specs=VMEM,
        out_shape=jax.ShapeDtypeStruct((sent, columns), BF),
        scratch_shapes=[pltpu.VMEM((sent, columns), F32)],
        compiler_params=PARAMS,
        name="legendre_sums",
    )(place, pair_lower, pick, limit, spec, *shards)


def order_kernel(waves_ref, out_ref):
    count, tall = waves_ref.shape[1], 256
    for m in range(0, count, tall):
        index = lax.broadcasted_iota(jnp.int32, (tall, count), 0) + m
        out_ref[m:m + tall, :] = jnp.where(index == waves_ref[...], 1.0, 0.0).astype(BF)


def wave_order(waves):
    count = waves.shape[1]
    return pl.pallas_call(
        order_kernel,
        in_specs=[VMEM],
        out_specs=VMEM,
        out_shape=jax.ShapeDtypeStruct((count, count), BF),
        compiler_params=PARAMS,
        name="wave_order",
    )(waves)


def place_kernel(chosen_ref, received_ref, out_ref, rows_ref, held_ref):
    lat_dev, count, columns = out_ref.shape
    pieces = 64
    step = received_ref.shape[0] // pieces

    def widen(d, carry):
        at = pl.ds(pl.multiple_of(d * step, step), step)
        rows_ref[at, :] = received_ref[at, :].astype(F32)
        return carry

    lax.fori_loop(0, pieces, widen, 0, unroll=8)
    for lat in range(lat_dev):
        held_ref[:, lat * columns:(lat + 1) * columns] = rows_ref[pl.ds(lat, count, stride=lat_dev), :].astype(BF)
    tall = 256
    for m in range(0, count, tall):
        placed = jnp.dot(chosen_ref[m:m + tall, :], held_ref[...], preferred_element_type=F32).astype(BF)
        for lat in range(lat_dev):
            out_ref[lat, m:m + tall, :] = placed[:, lat * columns:(lat + 1) * columns]


def place_waves(chosen, received, lat_dev):
    count = chosen.shape[0]
    columns = received.shape[1]
    return pl.pallas_call(
        place_kernel,
        in_specs=[VMEM, VMEM],
        out_specs=VMEM,
        out_shape=jax.ShapeDtypeStruct((lat_dev, count, columns), BF),
        scratch_shapes=[
            pltpu.VMEM((lat_dev * count, columns), F32),
            pltpu.VMEM((count, lat_dev * columns), BF),
        ],
        compiler_params=PARAMS,
        name="place_waves",
    )(chosen, received)


def on_device(spec_coeffs, legendre, pair_lower, slot_latitude, cycle_points):
    pairs, _, half_slots, columns = spec_coeffs.shape
    truncation = 2 * half_slots - 3
    n_wave, n_fld = lax.axis_size("wave"), lax.axis_size("fld")
    lats = slot_latitude.shape[0]
    lat_dev = lats // n_wave
    assert n_fld == 8

    def up(x):
        return lax.ppermute(x, "fld", [(i, (i + 1) % n_fld) for i in range(n_fld)])

    def down(x):
        return lax.ppermute(x, "fld", [(i, (i - 1) % n_fld) for i in range(n_fld)])

    place = jnp.stack([lax.axis_index("wave"), lax.axis_index("fld")]).astype(jnp.int32)
    slots = slot_latitude.reshape(n_wave, lat_dev).T.reshape(1, lats)
    points = cycle_points.reshape(1, lats // 2)
    waves = jnp.stack([pair_lower, truncation - pair_lower], axis=1).reshape(1, truncation + 1)

    own = pack_table(jnp.transpose(legendre, (0, 1, 3, 2)))
    half = (own.shape[0] - 1) // 2
    below1, above1 = up(own), down(own)
    below1, spec = lax.optimization_barrier((below1, spec_coeffs))
    below2, above2 = up(below1), down(above1)
    pick, limit = row_order(place, slots, points)
    below2, pick, limit, waves = lax.optimization_barrier((below2, pick, limit, waves))
    below3, above3 = up(below2), down(above2)
    low, high = up(below3[:half]), down(above3[half:])
    shards = [own, above1, above2, above3, low, high, below3, below2, below1]
    to_send = legendre_sums(place, pair_lower, pick, limit, spec, shards, n_wave, truncation)
    to_send, waves = lax.optimization_barrier((to_send, waves))
    received = lax.all_to_all(to_send.reshape(n_wave, -1, columns), "wave", split_axis=0, concat_axis=0, tiled=True)
    return place_waves(wave_order(waves), received.reshape(-1, columns), lat_dev)


def solution(mesh):
    placed = (P("wave", None, None, "fld"), P("wave", None, None, "fld"), P(), P(), P())
    return jax.shard_map(
        on_device, mesh=mesh, in_specs=placed, out_specs=P("wave", None, "fld"), check_vma=False
    )
```

time: 161 us -> 121 us (0.75)
  starting transfers between devices: 10.4 us -> 50.2 us
  waiting for transfers between devices: 81.8 us -> 51.3 us
  local copies, waits for them, and re-layouts: 32 us -> 6.12 us
  between operations: 13.6 us -> 0.15 us
  other arithmetic: 14 us -> 0.78 us
  Pallas kernels: 0 us -> 11.9 us
  matrix products: 8.71 us -> 0 us
    all_gather x1 -> x0, waiting for transfers between devices: 56.1 us -> none  [on_device(): lax.all_gather(legendre, 'fld', axis=3, tiled=True)]
    ppermute x0 -> x8, starting transfers between devices: none -> 35.1 us  [the longest x4 27.4 us: down(): return lax.ppermute(x, 'fld', [(i, (i - 1) % n_fld) for i in range(n_fld)])]
    ppermute x0 -> x8, waiting for transfers between devices: none -> 17.8 us  [the longest x4 11.8 us: down(): return lax.ppermute(x, 'fld', [(i, (i - 1) % n_fld) for i in range(n_fld)])]
    pallas_call x0 -> x5, Pallas kernels: none -> 11.9 us  [the longest x1 5.95 us: legendre_sums(): pl.pallas_call(functools.partial(sums_kernel, truncation, n_wave), in_spe...]
    gather x3 -> x0, local copies, waits for them, and re-layouts: 9.55 us -> none  [the longest x1 4.36 us: on_device(): return jnp.take(received, wave_of, axis=1)]
    dot_general x1 -> x0, matrix products: 8.71 us -> none  [legendre_sums(): jnp.einsum('pskl,pskhc->slphc', table_piece, masked, preferred_element_ty...]
    scatter x2 -> x0, local copies, waits for them, and re-layouts: 8.39 us -> none  [the longest x1 4.29 us: on_device(): wave_of = wave_of.at[truncation - pair_lower].set(2 * pair_index + 1)]
    all_to_all x1, waiting for transfers between devices: 25.7 us -> 33.6 us  [on_device(): lax.all_to_all(to_send.reshape(n_wave, -1, columns), 'wave', split_axis=0...]
  transfers between devices with their start and end apart: 2 -> 9, of which waited for: 2 -> 6; matrix products, arithmetic and copies ran while one was open for 9% -> 4% of each run, Pallas kernels for 0% -> 1%
where the time goes in v2:
time: 121 us; the launch traced here: 120 us
  waiting for transfers between devices  51.3 us (42%)
  starting transfers between devices  50.2 us (41%)
  Pallas kernels  11.9 us (10%)
  local copies, waits for them, and re-layouts  6.12 us (5%)
    all_to_all x1, waiting for transfers between devices, on_device(): lax.all_to_all(to_send.reshape(n_wave, -1, columns), 'wave', split_axis=0...  33.6 us
    ppermute x4, starting transfers between devices, down(): return lax.ppermute(x, 'fld', [(i, (i - 1) % n_fld) for i in range(n_fld)])  27.4 us
    all_to_all x1, starting transfers between devices, on_device(): lax.all_to_all(to_send.reshape(n_wave, -1, columns), 'wave', split_axis=0...  15.1 us
    ppermute x4, waiting for transfers between devices, down(): return lax.ppermute(x, 'fld', [(i, (i - 1) % n_fld) for i in range(n_fld)])  11.8 us
    ppermute x4, starting transfers between devices, up(): return lax.ppermute(x, 'fld', [(i, (i + 1) % n_fld) for i in range(n_fld)])  7.67 us
    ppermute x4, waiting for transfers between devices, up(): return lax.ppermute(x, 'fld', [(i, (i + 1) % n_fld) for i in range(n_fld)])  6.02 us
    pallas_call x1, Pallas kernels, legendre_sums(): pl.pallas_call(functools.partial(sums_kernel, truncation, n_wave), in_spe...  5.95 us
    pallas_call x1, Pallas kernels, place_waves(): pl.pallas_call(place_kernel, in_specs=[VMEM, VMEM], out_specs=VMEM, out_s...  4.51 us
  transfers between devices with their start and end apart: 9, of which 6 were waited for; matrix products, arithmetic and copies ran while one was open for 4% of the time, Pallas kernels for 1%

profile of v2, /device:TPU:1, one launch (start us, length us, event | category | flops | bytes accessed | tf_op | source)
XLA Modules:
  0.0 120.5 jit_solution(1636653340901478101)
XLA Ops:
  0.0 1.0 copy-done
  1.0 0.1 pack_table.1.refs_0_
  1.1 11.5 %collective-permute-start.2 = (bf16[101,16,128]{2,1,0:T(8,128)(2,1)S(1)}, bf16[101,16,128]{2,1,0:T(8,128)(2,1)S(1)}, u32[]{:S(2)}, u32[]{:S(2)}) collective-permute-start(bf16[101,16,128]{2,1,0:T(8,128)(2,1)S(1)} %pack_table.1.refs_0_), channel_id=1, source_target_pairs={{0,7},{1,0},{2,1},{3,2},{4,3},{5,4},{6,5},{7,6},{8,15},{9,8},{10,9... | collective-permute-start | bytes 1241096 | tf_op jit(solution)/shard_map/ppermute | solution.py:228
  12.6 1.9 %collective-permute-start = (bf16[101,16,128]{2,1,0:T(8,128)(2,1)S(1)}, bf16[101,16,128]{2,1,0:T(8,128)(2,1)S(1)}, u32[]{:S(2)}, u32[]{:S(2)}) collective-permute-start(bf16[101,16,128]{2,1,0:T(8,128)(2,1)S(1)} %pack_table.1.refs_0_), channel_id=1, source_target_pairs={{0,1},{1,2},{2,3},{3,4},{4,5},{5,6},{6,7},{7,0},{8,9},{9,10},{10,1... | collective-permute-start | bytes 1241096 | tf_op jit(solution)/shard_map/ppermute | solution.py:225
  14.6 6.3 %collective-permute-done.2.refs_1_ = bf16[101,16,128]{2,1,0:T(8,128)(2,1)S(1)} collective-permute-done((bf16[101,16,128]{2,1,0:T(8,128)(2,1)S(1)}, bf16[101,16,128]{2,1,0:T(8,128)(2,1)S(1)}, u32[]{:S(2)}, u32[]{:S(2)}) %collective-permute-start.2) | collective-permute-done | bytes 413728 | tf_op jit(solution)/shard_map/ppermute | solution.py:228
  20.8 5.3 %collective-permute-start.3 = (bf16[101,16,128]{2,1,0:T(8,128)(2,1)S(1)}, bf16[101,16,128]{2,1,0:T(8,128)(2,1)S(1)}, u32[]{:S(2)}, u32[]{:S(2)}) collective-permute-start(bf16[101,16,128]{2,1,0:T(8,128)(2,1)S(1)} %collective-permute-done.2.refs_1_), channel_id=1, source_target_pairs={{0,7},{1,0},{2,1},{3,2},{4,3},{5,4},{6,5},{7,6},{8,15},{9,8},{10,9... | collective-permute-start | bytes 1241096 | tf_op jit(solution)/shard_map/ppermute | solution.py:228
  26.2 0.7 stack.21
  26.8 1.9 %collective-permute-start.1 = (bf16[101,16,128]{2,1,0:T(8,128)(2,1)S(1)}, bf16[101,16,128]{2,1,0:T(8,128)(2,1)S(1)}, u32[]{:S(2)}, u32[]{:S(2)}) collective-permute-start(bf16[101,16,128]{2,1,0:T(8,128)(2,1)S(1)} %collective-permute-done.refs_8_), channel_id=1, source_target_pairs={{0,1},{1,2},{2,3},{3,4},{4,5},{5,6},{6,7},{7,0},{8,9},{9,10},{10,1... | collective-permute-start | bytes 1241096 | tf_op jit(solution)/shard_map/ppermute | solution.py:225
  28.8 0.7 broadcast_subtract_fusion
  29.5 3.9 %collective-permute-done.3.refs_2_ = bf16[101,16,128]{2,1,0:T(8,128)(2,1)S(1)} collective-permute-done((bf16[101,16,128]{2,1,0:T(8,128)(2,1)S(1)}, bf16[101,16,128]{2,1,0:T(8,128)(2,1)S(1)}, u32[]{:S(2)}, u32[]{:S(2)}) %collective-permute-start.3) | collective-permute-done | bytes 413728 | tf_op jit(solution)/shard_map/ppermute | solution.py:228
  33.4 5.3 %collective-permute-start.4 = (bf16[101,16,128]{2,1,0:T(8,128)(2,1)S(1)}, bf16[101,16,128]{2,1,0:T(8,128)(2,1)S(1)}, u32[]{:S(2)}, u32[]{:S(2)}) collective-permute-start(bf16[101,16,128]{2,1,0:T(8,128)(2,1)S(1)} %collective-permute-done.3.refs_2_), channel_id=1, source_target_pairs={{0,7},{1,0},{2,1},{3,2},{4,3},{5,4},{6,5},{7,6},{8,15},{9,8},{10,9... | collective-permute-start | bytes 1241096 | tf_op jit(solution)/shard_map/ppermute | solution.py:228
  38.7 0.1 pad_add_fusion.1.place_ref
  38.8 0.8 reshape.18
  39.6 0.1 copy.7
  39.7 0.1 reshape.19.slots_ref
  39.8 0.2 copy.8
  39.9 0.2 reshape.21.waves_ref
  40.2 0.0 copy-start.2
  40.2 0.6 copy-done.2
  40.8 0.8 row_order.1
  41.6 1.9 %collective-permute-start.5 = (bf16[101,16,128]{2,1,0:T(8,128)(2,1)S(1)}, bf16[101,16,128]{2,1,0:T(8,128)(2,1)S(1)}, u32[]{:S(2)}, u32[]{:S(2)}) collective-permute-start(bf16[101,16,128]{2,1,0:T(8,128)(2,1)S(1)} %collective-permute-done.1.refs_7_), channel_id=1, source_target_pairs={{0,1},{1,2},{2,3},{3,4},{4,5},{5,6},{6,7},{7,0},{8,9},{9,10},{10,1... | collective-permute-start | bytes 1241096 | tf_op jit(solution)/shard_map/ppermute | solution.py:225
  43.6 1.5 %collective-permute-done.4.refs_3_ = bf16[101,16,128]{2,1,0:T(8,128)(2,1)S(1)} collective-permute-done((bf16[101,16,128]{2,1,0:T(8,128)(2,1)S(1)}, bf16[101,16,128]{2,1,0:T(8,128)(2,1)S(1)}, u32[]{:S(2)}, u32[]{:S(2)}) %collective-permute-start.4) | collective-permute-done | bytes 413728 | tf_op jit(solution)/shard_map/ppermute | solution.py:228
  45.1 5.3 %collective-permute-start.7 = (bf16[51,16,128]{2,1,0:T(8,128)(2,1)S(1)}, bf16[51,16,128]{2,1,0:T(8,128)(2,1)S(1)}, u32[]{:S(2)}, u32[]{:S(2)}) collective-permute-start(bf16[51,16,128]{2,1,0:T(8,128)(2,1)S(1)} %slice.9), channel_id=1, source_target_pairs={{0,7},{1,0},{2,1},{3,2},{4,3},{5,4},{6,5},{7,6},{8,15},{9,8},{10,9... | collective-permute-start | bytes 626696 | tf_op jit(solution)/shard_map/ppermute | solution.py:228
  50.4 2.6 %collective-permute-done.5.refs_6_ = bf16[101,16,128]{2,1,0:T(8,128)(2,1)S(1)} collective-permute-done((bf16[101,16,128]{2,1,0:T(8,128)(2,1)S(1)}, bf16[101,16,128]{2,1,0:T(8,128)(2,1)S(1)}, u32[]{:S(2)}, u32[]{:S(2)}) %collective-permute-start.5) | collective-permute-done | bytes 413728 | tf_op jit(solution)/shard_map/ppermute | solution.py:225
  53.1 1.9 %collective-permute-start.6 = (bf16[50,16,128]{2,1,0:T(8,128)(2,1)S(1)}, bf16[50,16,128]{2,1,0:T(8,128)(2,1)S(1)}, u32[]{:S(2)}, u32[]{:S(2)}) collective-permute-start(bf16[50,16,128]{2,1,0:T(8,128)(2,1)S(1)} %slice.8), channel_id=1, source_target_pairs={{0,1},{1,2},{2,3},{3,4},{4,5},{5,6},{6,7},{7,0},{8,9},{9,10},{10,1... | collective-permute-start | bytes 614408 | tf_op jit(solution)/shard_map/ppermute | solution.py:225
  55.0 2.4 %copy.9.spec_ref = bf16[10,2,641,128]{3,2,1,0:T(8,128)(2,1)S(1)} copy(bf16[10,2,641,128]{3,1,2,0:T(2,128)(2,1)} %param.5) | data formatting | bytes 6563840 | tf_op jit(solution)/shard_map/optimization_barrier | solution.py:238
  57.4 3.4 %collective-permute-done.6.refs_4_ = bf16[50,16,128]{2,1,0:T(8,128)(2,1)S(1)} collective-permute-done((bf16[50,16,128]{2,1,0:T(8,128)(2,1)S(1)}, bf16[50,16,128]{2,1,0:T(8,128)(2,1)S(1)}, u32[]{:S(2)}, u32[]{:S(2)}) %collective-permute-start.6) | collective-permute-done | bytes 204832 | tf_op jit(solution)/shard_map/ppermute | solution.py:225
  60.8 6.0 %legendre_sums.1 = bf16[5120,128]{1,0:T(8,128)(2,1)} custom-call(s32[2]{0:T(128)S(1)} %pad_add_fusion.1.place_ref, s32[640]{0:T(1024)S(1)} %copy-done.1, bf16[256,256]{1,0:T(8,128)(2,1)S(1)} %get-tuple-element.18.pick_ref, f32[256,128]{1,0:T(8,128)S(1)} %get-tuple-element.19.limit_ref, bf16[10,2,641,128]{3,2,1,0:T(8,128)(2,1)S(1)} %copy.9.spec_ref, ...), custom_call_target="tpu_custom_call" | custom-call | tf_op jit(solution)/shard_map/legendre_sums/pallas_call | solution.py:149
  66.7 15.1 %all-to-all-start = ((bf16[64,80,128]{2,1,0:T(8,128)(2,1)}), bf16[64,80,128]{2,1,0:T(8,128)(2,1)}, u32[]{:S(2)}, u32[]{:S(2)}) async-start(bf16[64,80,128]{2,1,0:T(8,128)(2,1)} %bitcast.5), calls=%async_computation | async-start | bytes 2621440 | tf_op jit(solution)/shard_map/all_to_all | solution.py:247
  81.8 0.6 wave_order.1.chosen_ref
  82.4 33.6 %all-to-all-done = bf16[64,80,128]{2,1,0:T(8,128)(2,1)} async-done(((bf16[64,80,128]{2,1,0:T(8,128)(2,1)}), bf16[64,80,128]{2,1,0:T(8,128)(2,1)}, u32[]{:S(2)}, u32[]{:S(2)}) %all-to-all-start) | async-done | bytes 1310752 | tf_op jit(solution)/shard_map/all_to_all | solution.py:247
  116.0 4.5 %place_waves.1 = bf16[4,1280,128]{2,1,0:T(8,128)(2,1)} custom-call(bf16[1280,1280]{1,0:T(8,128)(2,1)S(1)} %wave_order.1.chosen_ref, bf16[5120,128]{1,0:T(8,128)(2,1)} %bitcast.6.received_ref), custom_call_target="tpu_custom_call" | custom-call | tf_op jit(solution)/shard_map/place_waves/pallas_call | solution.py:202
  (10 shorter events, 0.1 us)
Async XLA Ops:
  0.0 1.0 copy-start
  1.1 19.7 %collective-permute-start.2 = (bf16[101,16,128]{2,1,0:T(8,128)(2,1)S(1)}, bf16[101,16,128]{2,1,0:T(8,128)(2,1)S(1)}, u32[]{:S(2)}, u32[]{:S(2)}) collective-permute-start(bf16[101,16,128]{2,1,0:T(8,128)(2,1)S(1)} %pack_table.1.refs_0_), channel_id=1, source_target_pairs={{0,7},{1,0},{2,1},{3,2},{4,3},{5,4},{6,5},{7,6},{8,15},{9,8},{10,9... | collective-permute-start | bytes 1241096 | tf_op jit(solution)/shard_map/ppermute | solution.py:228
  12.6 14.2 %collective-permute-start = (bf16[101,16,128]{2,1,0:T(8,128)(2,1)S(1)}, bf16[101,16,128]{2,1,0:T(8,128)(2,1)S(1)}, u32[]{:S(2)}, u32[]{:S(2)}) collective-permute-start(bf16[101,16,128]{2,1,0:T(8,128)(2,1)S(1)} %pack_table.1.refs_0_), channel_id=1, source_target_pairs={{0,1},{1,2},{2,3},{3,4},{4,5},{5,6},{6,7},{7,0},{8,9},{9,10},{10,1... | collective-permute-start | bytes 1241096 | tf_op jit(solution)/shard_map/ppermute | solution.py:225
  20.8 12.6 %collective-permute-start.3 = (bf16[101,16,128]{2,1,0:T(8,128)(2,1)S(1)}, bf16[101,16,128]{2,1,0:T(8,128)(2,1)S(1)}, u32[]{:S(2)}, u32[]{:S(2)}) collective-permute-start(bf16[101,16,128]{2,1,0:T(8,128)(2,1)S(1)} %collective-permute-done.2.refs_1_), channel_id=1, source_target_pairs={{0,7},{1,0},{2,1},{3,2},{4,3},{5,4},{6,5},{7,6},{8,15},{9,8},{10,9... | collective-permute-start | bytes 1241096 | tf_op jit(solution)/shard_map/ppermute | solution.py:228
  26.8 14.8 %collective-permute-start.1 = (bf16[101,16,128]{2,1,0:T(8,128)(2,1)S(1)}, bf16[101,16,128]{2,1,0:T(8,128)(2,1)S(1)}, u32[]{:S(2)}, u32[]{:S(2)}) collective-permute-start(bf16[101,16,128]{2,1,0:T(8,128)(2,1)S(1)} %collective-permute-done.refs_8_), channel_id=1, source_target_pairs={{0,1},{1,2},{2,3},{3,4},{4,5},{5,6},{6,7},{7,0},{8,9},{9,10},{10,1... | collective-permute-start | bytes 1241096 | tf_op jit(solution)/shard_map/ppermute | solution.py:225
  33.4 11.7 %collective-permute-start.4 = (bf16[101,16,128]{2,1,0:T(8,128)(2,1)S(1)}, bf16[101,16,128]{2,1,0:T(8,128)(2,1)S(1)}, u32[]{:S(2)}, u32[]{:S(2)}) collective-permute-start(bf16[101,16,128]{2,1,0:T(8,128)(2,1)S(1)} %collective-permute-done.3.refs_2_), channel_id=1, source_target_pairs={{0,7},{1,0},{2,1},{3,2},{4,3},{5,4},{6,5},{7,6},{8,15},{9,8},{10,9... | collective-permute-start | bytes 1241096 | tf_op jit(solution)/shard_map/ppermute | solution.py:228
  40.2 0.7 copy-start.2
  41.6 11.4 %collective-permute-start.5 = (bf16[101,16,128]{2,1,0:T(8,128)(2,1)S(1)}, bf16[101,16,128]{2,1,0:T(8,128)(2,1)S(1)}, u32[]{:S(2)}, u32[]{:S(2)}) collective-permute-start(bf16[101,16,128]{2,1,0:T(8,128)(2,1)S(1)} %collective-permute-done.1.refs_7_), channel_id=1, source_target_pairs={{0,1},{1,2},{2,3},{3,4},{4,5},{5,6},{6,7},{7,0},{8,9},{9,10},{10,1... | collective-permute-start | bytes 1241096 | tf_op jit(solution)/shard_map/ppermute | solution.py:225
  45.1 15.7 %collective-permute-start.7 = (bf16[51,16,128]{2,1,0:T(8,128)(2,1)S(1)}, bf16[51,16,128]{2,1,0:T(8,128)(2,1)S(1)}, u32[]{:S(2)}, u32[]{:S(2)}) collective-permute-start(bf16[51,16,128]{2,1,0:T(8,128)(2,1)S(1)} %slice.9), channel_id=1, source_target_pairs={{0,7},{1,0},{2,1},{3,2},{4,3},{5,4},{6,5},{7,6},{8,15},{9,8},{10,9... | collective-permute-start | bytes 626696 | tf_op jit(solution)/shard_map/ppermute | solution.py:228
  53.1 7.7 %copy-start.1 = (s32[640]{0:T(1024)S(1)}, s32[640]{0:T(1024)}, u32[]{:S(2)}) copy-start(s32[640]{0:T(1024)} %lower_ref.1) | copy-start | bytes 7684
  53.1 7.7 %collective-permute-start.6 = (bf16[50,16,128]{2,1,0:T(8,128)(2,1)S(1)}, bf16[50,16,128]{2,1,0:T(8,128)(2,1)S(1)}, u32[]{:S(2)}, u32[]{:S(2)}) collective-permute-start(bf16[50,16,128]{2,1,0:T(8,128)(2,1)S(1)} %slice.8), channel_id=1, source_target_pairs={{0,1},{1,2},{2,3},{3,4},{4,5},{5,6},{6,7},{7,0},{8,9},{9,10},{10,1... | collective-permute-start | bytes 614408 | tf_op jit(solution)/shard_map/ppermute | solution.py:225
  66.7 49.2 %all-to-all-start = ((bf16[64,80,128]{2,1,0:T(8,128)(2,1)}), bf16[64,80,128]{2,1,0:T(8,128)(2,1)}, u32[]{:S(2)}, u32[]{:S(2)}) async-start(bf16[64,80,128]{2,1,0:T(8,128)(2,1)} %bitcast.5), calls=%async_computation | async-start | bytes 2621440 | tf_op jit(solution)/shard_map/all_to_all | solution.py:247

commit v3 on v2

v3 whole, which is shorter than its diff:
```python
import functools

import jax
import jax.numpy as jnp
from jax import lax
from jax.experimental import pallas as pl
from jax.experimental.pallas import tpu as pltpu
from jax.sharding import PartitionSpec as P

BF = jnp.bfloat16
F32 = jnp.float32
LANES = 128
ROWS = 16
PLAIN = 2
VMEM = pl.BlockSpec(memory_space=pltpu.VMEM)
SMEM = pl.BlockSpec(memory_space=pltpu.SMEM)
PIECE = 80
UNROLL = True
PARAMS = pltpu.CompilerParams(vmem_limit_bytes=24 * 1024 * 1024)


def pack_kernel(table_ref, *out_refs):
    pairs, _, rows, half_slots = table_ref.shape
    blocks = half_slots // LANES
    group = pairs // len(out_refs)
    lane = lax.broadcasted_iota(jnp.int32, (rows, LANES), 1)
    for g, out_ref in enumerate(out_refs):
        last = jnp.zeros((rows, LANES), F32)
        for i in range(group):
            for r in range(2):
                for b in range(blocks):
                    out_ref[(2 * i + r) * blocks + b] = table_ref[g * group + i, r, :, b * LANES:(b + 1) * LANES]
                tail = table_ref[g * group + i, r, :, half_slots - 1:half_slots].astype(F32)
                last = jnp.where(lane == 2 * i + r, tail, last)
        out_ref[2 * group * blocks] = last.astype(BF)


def pack_table(table, groups):
    pairs, _, rows, half_slots = table.shape
    assert half_slots % LANES == 1
    length = 2 * (pairs // groups) * (half_slots // LANES) + 1
    return pl.pallas_call(
        pack_kernel,
        in_specs=[VMEM],
        out_specs=[VMEM] * groups,
        out_shape=[jax.ShapeDtypeStruct((length, rows, LANES), BF)] * groups,
        compiler_params=PARAMS,
        name="pack_table",
    )(table)


def rows_kernel(lat_dev, place_ref, slots_ref, points_ref, pick_ref, limit_ref):
    lats = slots_ref.shape[1]
    half = lats // 2
    n_wave = lats // lat_dev
    sent = lax.broadcasted_iota(jnp.int32, (lats, lats), 1)
    source = lax.rem(sent, n_wave) * lat_dev + sent // n_wave
    moved = jnp.where(lax.broadcasted_iota(jnp.int32, (lats, lats), 0) == source, 1.0, 0.0).astype(BF)
    slots = jnp.broadcast_to(slots_ref[...].astype(F32), (ROWS, lats)).astype(BF)
    slots = jnp.dot(slots, moved, preferred_element_type=F32)[:1].astype(jnp.int32)
    cycle = lax.rem(slots, half)
    held = lax.rem(cycle - place_ref[1] * ROWS + half, half) + (slots // half) * half
    index = lax.broadcasted_iota(jnp.int32, (lats, lats), 0)
    pick_ref[...] = jnp.where(index == held, 1.0, 0.0).T.astype(BF)
    index = lax.broadcasted_iota(jnp.int32, (half, lats), 0)
    points = jnp.where(index == cycle, 1.0, 0.0).T * points_ref[...].astype(F32)
    limit_ref[...] = jnp.broadcast_to(jnp.sum(points, axis=1, keepdims=True), limit_ref.shape)


def row_order(place, slots, points, lat_dev):
    lats = slots.shape[1]
    assert lats <= 256
    return pl.pallas_call(
        functools.partial(rows_kernel, lat_dev),
        in_specs=[SMEM, VMEM, VMEM],
        out_specs=[VMEM, VMEM],
        out_shape=[jax.ShapeDtypeStruct((lats, lats), BF), jax.ShapeDtypeStruct((lats, LANES), F32)],
        compiler_params=PARAMS,
        name="row_order",
    )(place, slots, points)


def sums_kernel(truncation, n_wave, first_pair, last_group, place_ref, lower_ref, pick_ref, limit_ref, spec_ref, *refs):
    shard_refs, earlier, out_ref = refs[:8], refs[8:-2] if last_group else (), refs[-2] if last_group else refs[-1]
    rows_ref = refs[-1]
    all_pairs, _, half_slots, columns = spec_ref.shape
    lat_dev = pick_ref.shape[0] // n_wave
    per_dev = rows_ref.shape[0] // n_wave
    group = per_dev // (2 * lat_dev)
    full = half_slots - 1
    blocks = full // LANES
    plain = PLAIN * LANES

    def block(b, g):
        return jnp.concatenate([ref[b] for ref in shard_refs], axis=0)

    def step(i, carry):
        for g in range(1):
            local = i
            pair = local + first_pair
            q = lower_ref[place_ref[0] * all_pairs + pair]
            length = truncation + 1 - q
            begin = length + lax.rem(length, 2)
            tails = block(2 * group * blocks, g)
            sums = []
            for r in range(2):
                def owned(slot, coeffs, lower):
                    kept = slot < length if lower else (slot >= begin) & (slot <= begin + q)
                    return jnp.where(kept, coeffs, 0.0).astype(BF)

                table = [block((2 * i + r) * blocks + b, g) for b in range(blocks)]
                below = jnp.dot(
                    jnp.concatenate(table[:PLAIN], axis=1), spec_ref[pair, r, :plain, :], preferred_element_type=F32
                )
                coeffs = spec_ref[pair, r, plain:full, :].astype(F32)
                slot = 2 * (lax.broadcasted_iota(jnp.int32, coeffs.shape, 0) + plain) + r
                row = lax.broadcasted_iota(jnp.int32, (LANES, columns), 0)
                tail = jnp.where(row == 2 * i + r, spec_ref[pair, r, full:, :].astype(F32), 0.0)
                last = jnp.full((LANES, columns), 2 * full + r, jnp.int32)
                both = [
                    jnp.concatenate([owned(slot, coeffs, lower), owned(last, tail, lower)], axis=0)
                    for lower in (True, False)
                ]
                above = jnp.dot(
                    jnp.concatenate(table[PLAIN:] + [tails], axis=1),
                    jnp.concatenate(both, axis=1),
                    preferred_element_type=F32,
                )
                sums.append((above[:, :columns] + below, above[:, columns:]))
            north = jnp.concatenate([sums[0][h] + sums[1][h] for h in range(2)], axis=1)
            south = jnp.concatenate([sums[0][h] - sums[1][h] for h in range(2)], axis=1)
            fourier = jnp.concatenate([north, south], axis=0).astype(BF)
            picked = jnp.dot(pick_ref[...], fourier, preferred_element_type=F32)
            for h in range(2):
                wave = (q if h == 0 else truncation - q).astype(F32)
                kept = jnp.where(2.0 * wave < limit_ref[...], picked[:, h * columns:(h + 1) * columns], 0.0)
                for lat in range(lat_dev):
                    start = (2 * local + h) * lat_dev + lat
                    rows_ref[pl.ds(start, n_wave, stride=per_dev), :] = kept[lat * n_wave:(lat + 1) * n_wave]
        return carry

    lax.fori_loop(0, group, step, 0, unroll=UNROLL)

    def narrow(d, carry):
        at = pl.ds(pl.multiple_of(d * per_dev, per_dev), per_dev)
        parts = [ref[at, :] for ref in earlier + (rows_ref,)]
        sent = per_dev * len(parts)
        out_ref[pl.ds(pl.multiple_of(d * sent, sent), sent), :] = jnp.concatenate(parts, axis=0).astype(BF)
        return carry

    if last_group:
        lax.fori_loop(0, n_wave, narrow, 0, unroll=8)


def legendre_sums(place, pair_lower, pick, limit, spec, shards, earlier, first_pair, group, last, n_wave, truncation):
    columns = spec.shape[3]
    rows = 2 * group * pick.shape[0]
    if last:
        out = jax.ShapeDtypeStruct((rows * (1 + len(earlier)), columns), BF)
    else:
        out, earlier = jax.ShapeDtypeStruct((rows, columns), F32), []
    return pl.pallas_call(
        functools.partial(sums_kernel, truncation, n_wave, first_pair, last),
        in_specs=[SMEM, SMEM] + [VMEM] * (3 + len(shards) + len(earlier)),
        out_specs=VMEM,
        out_shape=out,
        scratch_shapes=[pltpu.VMEM((rows, columns), F32)] if last else [],
        compiler_params=PARAMS,
        name="legendre_sums",
    )(place, pair_lower, pick, limit, spec, *shards, *earlier)


def place_kernel(lat_dev, waves_ref, *refs):
    received_refs, (out_ref, rows_ref, held_ref) = refs[:-3], refs[-3:]
    count = waves_ref.shape[1]
    columns = out_ref.shape[2]
    base = 0
    for received_ref in received_refs:
        rows = received_ref.shape[0]

        def widen(d, carry):
            at = pl.multiple_of(d * PIECE, PIECE)
            rows_ref[pl.ds(at + base * 2 * lat_dev, PIECE), :] = received_ref[pl.ds(at, PIECE), :].astype(F32)
            return carry

        lax.fori_loop(0, rows // PIECE, widen, 0, unroll=8)
        many = rows // (2 * lat_dev)
        for h in range(2):
            for lat in range(lat_dev):
                taken = rows_ref[pl.ds(base * 2 * lat_dev + h * lat_dev + lat, many, stride=2 * lat_dev), :]
                at = 2 * base + h * many
                held_ref[at:at + many, lat * columns:(lat + 1) * columns] = taken.astype(BF)
        base += many
    tall = 256
    for m in range(0, count, tall):
        index = lax.broadcasted_iota(jnp.int32, (tall, count), 0) + m
        chosen = jnp.where(index == waves_ref[...], 1.0, 0.0).astype(BF)
        placed = jnp.dot(chosen, held_ref[...], preferred_element_type=F32).astype(BF)
        for lat in range(lat_dev):
            out_ref[lat, m:m + tall, :] = placed[:, lat * columns:(lat + 1) * columns]


def place_waves(waves, received, lat_dev):
    count = waves.shape[1]
    columns = received[0].shape[1]
    return pl.pallas_call(
        functools.partial(place_kernel, lat_dev),
        out_shape=jax.ShapeDtypeStruct((lat_dev, count, columns), BF),
        scratch_shapes=[
            pltpu.VMEM((lat_dev * count, columns), F32),
            pltpu.VMEM((count, lat_dev * columns), BF),
        ],
        compiler_params=PARAMS,
        name="place_waves",
    )(waves, *received)


def gather_ring(groups):
    n = lax.axis_size("fld")
    assert n == 8 and len(groups) == 2

    def up(x):
        return lax.ppermute(x, "fld", [(i, (i + 1) % n) for i in range(n)])

    def down(x):
        return lax.ppermute(x, "fld", [(i, (i - 1) % n) for i in range(n)])

    below, above = [[x] for x in groups], [[x] for x in groups]
    for step in range(n // 2):
        for g in range(2):
            if step < n // 2 - 1 or g == 0:
                below[g].append(up(below[g][-1]))
            if step < n // 2 - 1 or g == 1:
                above[g].append(down(above[g][-1]))
    return [[groups[g]] + above[g][1:] + below[g][:0:-1] for g in range(2)]


def on_device(spec_coeffs, legendre, pair_lower, slot_latitude, cycle_points):
    pairs, _, half_slots, columns = spec_coeffs.shape
    truncation = 2 * half_slots - 3
    n_wave = lax.axis_size("wave")
    lats = slot_latitude.shape[0]
    lat_dev = lats // n_wave
    group = pairs // 2
    place = jnp.stack([lax.axis_index("wave"), lax.axis_index("fld")]).astype(jnp.int32)
    shards = gather_ring(pack_table(jnp.transpose(legendre, (0, 1, 3, 2)), 2))
    pick, limit = row_order(place, slot_latitude.reshape(1, lats), cycle_points.reshape(1, lats // 2), lat_dev)
    rows = []
    for g in range(2):
        sums = legendre_sums(
            place, pair_lower, pick, limit, spec_coeffs, shards[g], rows, g * group, group, g == 1, n_wave, truncation
        )
        rows.append(sums)
    sent = rows[-1].reshape(n_wave, -1, columns)
    received = [lax.all_to_all(sent, "wave", split_axis=0, concat_axis=0, tiled=True).reshape(-1, columns)]
    lower = pair_lower.reshape(1, -1)
    waves = jnp.concatenate([lower, truncation - lower], axis=1)
    return place_waves(waves, received, lat_dev)


def solution(mesh):
    placed = (P("wave", None, None, "fld"), P("wave", None, None, "fld"), P(), P(), P())
    return jax.shard_map(
        on_device, mesh=mesh, in_specs=placed, out_specs=P("wave", None, "fld"), check_vma=False
    )
```

time: 121 us -> 112 us (0.926)
  waiting for transfers between devices: 51.3 us -> 34.2 us
  starting transfers between devices: 50.2 us -> 63.2 us
  local copies, waits for them, and re-layouts: 6.12 us -> 3.43 us
  Pallas kernels: 11.9 us -> 10.2 us
    ppermute x8 -> x14, waiting for transfers between devices: 17.8 us -> 0.04 us  [the longest x7 0.02 us: down(): return lax.ppermute(x, 'fld', [(i, (i - 1) % n) for i in range(n)])]
    ppermute x8 -> x14, starting transfers between devices: 35.1 us -> 48.7 us  [the longest x7 32.4 us: down(): return lax.ppermute(x, 'fld', [(i, (i - 1) % n) for i in range(n)])]
    optimization_barrier x1 -> x0, local copies, waits for them, and re-layouts: 2.36 us -> none  [on_device(): below1, spec = lax.optimization_barrier((below1, spec_coeffs))]
    unnamed x6 -> x9, local copies, waits for them, and re-layouts: 1.69 us -> 3.42 us
    pallas_call x5, Pallas kernels: 11.9 us -> 10.2 us  [the longest x2 5.67 us: legendre_sums(): pl.pallas_call(functools.partial(sums_kernel, truncation, n_wave, first_p...]
  transfers between devices with their start and end apart: 9 -> 15, of which waited for: 6 -> 1; matrix products, arithmetic and copies ran while one was open for 4% -> 2% of each run, Pallas kernels for 1% -> 3%
where the time goes in v3:
time: 112 us; the launch traced here: 111 us
  starting transfers between devices  63.2 us (56%)
  waiting for transfers between devices  34.2 us (31%)
  Pallas kernels  10.2 us (9%)
  local copies, waits for them, and re-layouts  3.43 us (3%)
    all_to_all x1, waiting for transfers between devices, on_device(): lax.all_to_all(sent, 'wave', split_axis=0, concat_axis=0, tiled=True)  34.1 us
    ppermute x7, starting transfers between devices, down(): return lax.ppermute(x, 'fld', [(i, (i - 1) % n) for i in range(n)])  32.4 us
    ppermute x7, starting transfers between devices, up(): return lax.ppermute(x, 'fld', [(i, (i + 1) % n) for i in range(n)])  16.4 us
    all_to_all x1, starting transfers between devices, on_device(): lax.all_to_all(sent, 'wave', split_axis=0, concat_axis=0, tiled=True)  14.4 us
    pallas_call x2, Pallas kernels, legendre_sums(): pl.pallas_call(functools.partial(sums_kernel, truncation, n_wave, first_p...  5.67 us
    pallas_call x1, Pallas kernels, place_waves(): pl.pallas_call(functools.partial(place_kernel, lat_dev), out_shape=jax.Sh...  3.58 us
    unnamed x9, local copies, waits for them, and re-layouts  3.42 us
  transfers between devices with their start and end apart: 15, of which 1 were waited for; matrix products, arithmetic and copies ran while one was open for 2% of the time, Pallas kernels for 3%

profile of v3, /device:TPU:1, one launch (start us, length us, event | category | flops | bytes accessed | tf_op | source)
XLA Modules:
  0.0 111.4 jit_solution(5509168657961399492)
XLA Ops:
  0.0 1.0 copy-done
  1.0 0.1 pack_table.1
  1.1 4.8 %collective-permute-start.10 = (bf16[51,16,128]{2,1,0:T(8,128)(2,1)S(1)}, bf16[51,16,128]{2,1,0:T(8,128)(2,1)S(1)}, u32[]{:S(2)}, u32[]{:S(2)}) collective-permute-start(bf16[51,16,128]{2,1,0:T(8,128)(2,1)S(1)} %get-tuple-element.12.refs_0_), channel_id=1, source_target_pairs={{0,1},{1,2},{2,3},{3,4},{4,5},{5,6},{6,7},{7,0},{8,9},{9,10},{10,1... | collective-permute-start | bytes 626696 | tf_op jit(solution)/shard_map/ppermute | solution.py:223
  6.0 8.6 %collective-permute-start = (bf16[51,16,128]{2,1,0:T(8,128)(2,1)S(1)}, bf16[51,16,128]{2,1,0:T(8,128)(2,1)S(1)}, u32[]{:S(2)}, u32[]{:S(2)}) collective-permute-start(bf16[51,16,128]{2,1,0:T(8,128)(2,1)S(1)} %get-tuple-element.11.refs_0_), channel_id=1, source_target_pairs={{0,7},{1,0},{2,1},{3,2},{4,3},{5,4},{6,5},{7,6},{8,15},{9,8},{10,9... | collective-permute-start | bytes 626696 | tf_op jit(solution)/shard_map/ppermute | solution.py:226
  14.6 3.4 %collective-permute-start.7 = (bf16[51,16,128]{2,1,0:T(8,128)(2,1)S(1)}, bf16[51,16,128]{2,1,0:T(8,128)(2,1)S(1)}, u32[]{:S(2)}, u32[]{:S(2)}) collective-permute-start(bf16[51,16,128]{2,1,0:T(8,128)(2,1)S(1)} %get-tuple-element.12.refs_0_), channel_id=1, source_target_pairs={{0,7},{1,0},{2,1},{3,2},{4,3},{5,4},{6,5},{7,6},{8,15},{9,8},{10,9... | collective-permute-start | bytes 626696 | tf_op jit(solution)/shard_map/ppermute | solution.py:226
  17.9 1.9 %collective-permute-start.11 = (bf16[51,16,128]{2,1,0:T(8,128)(2,1)S(1)}, bf16[51,16,128]{2,1,0:T(8,128)(2,1)S(1)}, u32[]{:S(2)}, u32[]{:S(2)}) collective-permute-start(bf16[51,16,128]{2,1,0:T(8,128)(2,1)S(1)} %collective-permute-done.10.refs_7_), channel_id=1, source_target_pairs={{0,1},{1,2},{2,3},{3,4},{4,5},{5,6},{6,7},{7,0},{8,9},{9,10},{10,1... | collective-permute-start | bytes 626696 | tf_op jit(solution)/shard_map/ppermute | solution.py:223
  19.9 1.9 %collective-permute-start.4 = (bf16[51,16,128]{2,1,0:T(8,128)(2,1)S(1)}, bf16[51,16,128]{2,1,0:T(8,128)(2,1)S(1)}, u32[]{:S(2)}, u32[]{:S(2)}) collective-permute-start(bf16[51,16,128]{2,1,0:T(8,128)(2,1)S(1)} %get-tuple-element.11.refs_0_), channel_id=1, source_target_pairs={{0,1},{1,2},{2,3},{3,4},{4,5},{5,6},{6,7},{7,0},{8,9},{9,10},{10,1... | collective-permute-start | bytes 626696 | tf_op jit(solution)/shard_map/ppermute | solution.py:223
  21.8 0.0 collective-permute-done.refs_1_
  21.8 4.6 %collective-permute-start.1 = (bf16[51,16,128]{2,1,0:T(8,128)(2,1)S(1)}, bf16[51,16,128]{2,1,0:T(8,128)(2,1)S(1)}, u32[]{:S(2)}, u32[]{:S(2)}) collective-permute-start(bf16[51,16,128]{2,1,0:T(8,128)(2,1)S(1)} %collective-permute-done.refs_1_), channel_id=1, source_target_pairs={{0,7},{1,0},{2,1},{3,2},{4,3},{5,4},{6,5},{7,6},{8,15},{9,8},{10,9... | collective-permute-start | bytes 626696 | tf_op jit(solution)/shard_map/ppermute | solution.py:226
  26.4 3.4 %collective-permute-start.8 = (bf16[51,16,128]{2,1,0:T(8,128)(2,1)S(1)}, bf16[51,16,128]{2,1,0:T(8,128)(2,1)S(1)}, u32[]{:S(2)}, u32[]{:S(2)}) collective-permute-start(bf16[51,16,128]{2,1,0:T(8,128)(2,1)S(1)} %collective-permute-done.7.refs_1_), channel_id=1, source_target_pairs={{0,7},{1,0},{2,1},{3,2},{4,3},{5,4},{6,5},{7,6},{8,15},{9,8},{10,9... | collective-permute-start | bytes 626696 | tf_op jit(solution)/shard_map/ppermute | solution.py:226
  29.8 1.9 %collective-permute-start.12 = (bf16[51,16,128]{2,1,0:T(8,128)(2,1)S(1)}, bf16[51,16,128]{2,1,0:T(8,128)(2,1)S(1)}, u32[]{:S(2)}, u32[]{:S(2)}) collective-permute-start(bf16[51,16,128]{2,1,0:T(8,128)(2,1)S(1)} %collective-permute-done.11.refs_6_), channel_id=1, source_target_pairs={{0,1},{1,2},{2,3},{3,4},{4,5},{5,6},{6,7},{7,0},{8,9},{9,10},{10,1... | collective-permute-start | bytes 626696 | tf_op jit(solution)/shard_map/ppermute | solution.py:223
  31.7 0.0 collective-permute-done.4.refs_7_
  31.7 1.9 %collective-permute-start.5 = (bf16[51,16,128]{2,1,0:T(8,128)(2,1)S(1)}, bf16[51,16,128]{2,1,0:T(8,128)(2,1)S(1)}, u32[]{:S(2)}, u32[]{:S(2)}) collective-permute-start(bf16[51,16,128]{2,1,0:T(8,128)(2,1)S(1)} %collective-permute-done.4.refs_7_), channel_id=1, source_target_pairs={{0,1},{1,2},{2,3},{3,4},{4,5},{5,6},{6,7},{7,0},{8,9},{9,10},{10,1... | collective-permute-start | bytes 626696 | tf_op jit(solution)/shard_map/ppermute | solution.py:223
  33.7 4.6 %collective-permute-start.2 = (bf16[51,16,128]{2,1,0:T(8,128)(2,1)S(1)}, bf16[51,16,128]{2,1,0:T(8,128)(2,1)S(1)}, u32[]{:S(2)}, u32[]{:S(2)}) collective-permute-start(bf16[51,16,128]{2,1,0:T(8,128)(2,1)S(1)} %collective-permute-done.1.refs_2_), channel_id=1, source_target_pairs={{0,7},{1,0},{2,1},{3,2},{4,3},{5,4},{6,5},{7,6},{8,15},{9,8},{10,9... | collective-permute-start | bytes 626696 | tf_op jit(solution)/shard_map/ppermute | solution.py:226
  38.2 0.0 collective-permute-done.8.refs_2_
  38.2 3.4 %collective-permute-start.9 = (bf16[51,16,128]{2,1,0:T(8,128)(2,1)S(1)}, bf16[51,16,128]{2,1,0:T(8,128)(2,1)S(1)}, u32[]{:S(2)}, u32[]{:S(2)}) collective-permute-start(bf16[51,16,128]{2,1,0:T(8,128)(2,1)S(1)} %collective-permute-done.8.refs_2_), channel_id=1, source_target_pairs={{0,7},{1,0},{2,1},{3,2},{4,3},{5,4},{6,5},{7,6},{8,15},{9,8},{10,9... | collective-permute-start | bytes 626696 | tf_op jit(solution)/shard_map/ppermute | solution.py:226
  41.6 1.9 %collective-permute-start.13 = (bf16[51,16,128]{2,1,0:T(8,128)(2,1)S(1)}, bf16[51,16,128]{2,1,0:T(8,128)(2,1)S(1)}, u32[]{:S(2)}, u32[]{:S(2)}) collective-permute-start(bf16[51,16,128]{2,1,0:T(8,128)(2,1)S(1)} %collective-permute-done.12.refs_5_), channel_id=1, source_target_pairs={{0,1},{1,2},{2,3},{3,4},{4,5},{5,6},{6,7},{7,0},{8,9},{9,10},{10,1... | collective-permute-start | bytes 626696 | tf_op jit(solution)/shard_map/ppermute | solution.py:223
  43.6 0.0 collective-permute-done.5.refs_6_
  43.6 1.9 %collective-permute-start.6 = (bf16[51,16,128]{2,1,0:T(8,128)(2,1)S(1)}, bf16[51,16,128]{2,1,0:T(8,128)(2,1)S(1)}, u32[]{:S(2)}, u32[]{:S(2)}) collective-permute-start(bf16[51,16,128]{2,1,0:T(8,128)(2,1)S(1)} %collective-permute-done.5.refs_6_), channel_id=1, source_target_pairs={{0,1},{1,2},{2,3},{3,4},{4,5},{5,6},{6,7},{7,0},{8,9},{9,10},{10,1... | collective-permute-start | bytes 626696 | tf_op jit(solution)/shard_map/ppermute | solution.py:223
  45.5 0.0 collective-permute-done.2.refs_3_
  45.5 4.6 %collective-permute-start.3 = (bf16[51,16,128]{2,1,0:T(8,128)(2,1)S(1)}, bf16[51,16,128]{2,1,0:T(8,128)(2,1)S(1)}, u32[]{:S(2)}, u32[]{:S(2)}) collective-permute-start(bf16[51,16,128]{2,1,0:T(8,128)(2,1)S(1)} %collective-permute-done.2.refs_3_), channel_id=1, source_target_pairs={{0,7},{1,0},{2,1},{3,2},{4,3},{5,4},{6,5},{7,6},{8,15},{9,8},{10,9... | collective-permute-start | bytes 626696 | tf_op jit(solution)/shard_map/ppermute | solution.py:226
  50.1 0.0 copy-start.2
  50.1 0.0 copy-start.3
  50.1 0.0 copy-start.1
  50.1 2.4 %copy.7.spec_ref = bf16[10,2,641,128]{3,2,1,0:T(8,128)(2,1)S(1)} copy(bf16[10,2,641,128]{3,1,2,0:T(2,128)(2,1)} %param.5) | data formatting | bytes 6563840 | tf_op args[0]
  52.5 0.1 pad_add_fusion.1.place_ref
  52.6 0.9 row_order.1
  53.5 2.2 %legendre_sums.2.refs_8_ = f32[2560,128]{1,0:T(8,128)S(1)} custom-call(s32[2]{0:T(128)S(1)} %pad_add_fusion.1.place_ref, s32[640]{0:T(1024)S(1)} %copy-done.1, bf16[256,256]{1,0:T(8,128)(2,1)S(1)} %get-tuple-element.9.pick_ref, f32[256,128]{1,0:T(8,128)S(1)} %get-tuple-element.10.limit_ref, bf16[10,2,641,128]{3,2,1,0:T(8,128)(2,1)S(1)} %copy.7.spec_ref, ...), custom_call_target="tpu_custom_call" | custom-call | tf_op jit(solution)/shard_map/legendre_sums/pallas_call | solution.py:162
  55.8 3.4 %legendre_sums.3 = bf16[5120,128]{1,0:T(8,128)(2,1)} custom-call(s32[2]{0:T(128)S(1)} %pad_add_fusion.1.place_ref, s32[640]{0:T(1024)S(1)} %copy-done.1, bf16[256,256]{1,0:T(8,128)(2,1)S(1)} %get-tuple-element.9.pick_ref, f32[256,128]{1,0:T(8,128)S(1)} %get-tuple-element.10.limit_ref, bf16[10,2,641,128]{3,2,1,0:T(8,128)(2,1)S(1)} %copy.7.spec_ref, ...), custom_call_target="tpu_custom_call" | custom-call | tf_op jit(solution)/shard_map/legendre_sums/pallas_call | solution.py:162
  59.2 14.4 %all-to-all-start = ((bf16[64,80,128]{2,1,0:T(8,128)(2,1)}), bf16[64,80,128]{2,1,0:T(8,128)(2,1)S(1)}, u32[]{:S(2)}, u32[]{:S(2)}) async-start(bf16[64,80,128]{2,1,0:T(8,128)(2,1)} %bitcast.5), calls=%async_computation | async-start | bytes 2621440 | tf_op jit(solution)/shard_map/all_to_all | solution.py:255
  73.7 34.1 %all-to-all-done = bf16[64,80,128]{2,1,0:T(8,128)(2,1)S(1)} async-done(((bf16[64,80,128]{2,1,0:T(8,128)(2,1)}), bf16[64,80,128]{2,1,0:T(8,128)(2,1)S(1)}, u32[]{:S(2)}, u32[]{:S(2)}) %all-to-all-start) | async-done | bytes 1310752 | tf_op jit(solution)/shard_map/all_to_all | solution.py:255
  107.8 3.6 %place_waves.1 = bf16[4,1280,128]{2,1,0:T(8,128)(2,1)} custom-call(s32[1,1280]{1,0:T(1,128)S(1)} %pad_add_fusion.waves_ref, bf16[5120,128]{1,0:T(8,128)(2,1)S(1)} %bitcast.7), custom_call_target="tpu_custom_call" | custom-call | tf_op jit(solution)/shard_map/place_waves/pallas_call | solution.py:206
  (17 shorter events, 0.0 us)
Async XLA Ops:
  0.0 1.0 copy-start
  1.1 16.8 %collective-permute-start.10 = (bf16[51,16,128]{2,1,0:T(8,128)(2,1)S(1)}, bf16[51,16,128]{2,1,0:T(8,128)(2,1)S(1)}, u32[]{:S(2)}, u32[]{:S(2)}) collective-permute-start(bf16[51,16,128]{2,1,0:T(8,128)(2,1)S(1)} %get-tuple-element.12.refs_0_), channel_id=1, source_target_pairs={{0,1},{1,2},{2,3},{3,4},{4,5},{5,6},{6,7},{7,0},{8,9},{9,10},{10,1... | collective-permute-start | bytes 626696 | tf_op jit(solution)/shard_map/ppermute | solution.py:223
  6.0 15.8 %collective-permute-start = (bf16[51,16,128]{2,1,0:T(8,128)(2,1)S(1)}, bf16[51,16,128]{2,1,0:T(8,128)(2,1)S(1)}, u32[]{:S(2)}, u32[]{:S(2)}) collective-permute-start(bf16[51,16,128]{2,1,0:T(8,128)(2,1)S(1)} %get-tuple-element.11.refs_0_), channel_id=1, source_target_pairs={{0,7},{1,0},{2,1},{3,2},{4,3},{5,4},{6,5},{7,6},{8,15},{9,8},{10,9... | collective-permute-start | bytes 626696 | tf_op jit(solution)/shard_map/ppermute | solution.py:226
  14.6 11.8 %collective-permute-start.7 = (bf16[51,16,128]{2,1,0:T(8,128)(2,1)S(1)}, bf16[51,16,128]{2,1,0:T(8,128)(2,1)S(1)}, u32[]{:S(2)}, u32[]{:S(2)}) collective-permute-start(bf16[51,16,128]{2,1,0:T(8,128)(2,1)S(1)} %get-tuple-element.12.refs_0_), channel_id=1, source_target_pairs={{0,7},{1,0},{2,1},{3,2},{4,3},{5,4},{6,5},{7,6},{8,15},{9,8},{10,9... | collective-permute-start | bytes 626696 | tf_op jit(solution)/shard_map/ppermute | solution.py:226
  17.9 11.8 %collective-permute-start.11 = (bf16[51,16,128]{2,1,0:T(8,128)(2,1)S(1)}, bf16[51,16,128]{2,1,0:T(8,128)(2,1)S(1)}, u32[]{:S(2)}, u32[]{:S(2)}) collective-permute-start(bf16[51,16,128]{2,1,0:T(8,128)(2,1)S(1)} %collective-permute-done.10.refs_7_), channel_id=1, source_target_pairs={{0,1},{1,2},{2,3},{3,4},{4,5},{5,6},{6,7},{7,0},{8,9},{9,10},{10,1... | collective-permute-start | bytes 626696 | tf_op jit(solution)/shard_map/ppermute | solution.py:223
  19.9 11.8 %collective-permute-start.4 = (bf16[51,16,128]{2,1,0:T(8,128)(2,1)S(1)}, bf16[51,16,128]{2,1,0:T(8,128)(2,1)S(1)}, u32[]{:S(2)}, u32[]{:S(2)}) collective-permute-start(bf16[51,16,128]{2,1,0:T(8,128)(2,1)S(1)} %get-tuple-element.11.refs_0_), channel_id=1, source_target_pairs={{0,1},{1,2},{2,3},{3,4},{4,5},{5,6},{6,7},{7,0},{8,9},{9,10},{10,1... | collective-permute-start | bytes 626696 | tf_op jit(solution)/shard_map/ppermute | solution.py:223
  21.8 11.8 %collective-permute-start.1 = (bf16[51,16,128]{2,1,0:T(8,128)(2,1)S(1)}, bf16[51,16,128]{2,1,0:T(8,128)(2,1)S(1)}, u32[]{:S(2)}, u32[]{:S(2)}) collective-permute-start(bf16[51,16,128]{2,1,0:T(8,128)(2,1)S(1)} %collective-permute-done.refs_1_), channel_id=1, source_target_pairs={{0,7},{1,0},{2,1},{3,2},{4,3},{5,4},{6,5},{7,6},{8,15},{9,8},{10,9... | collective-permute-start | bytes 626696 | tf_op jit(solution)/shard_map/ppermute | solution.py:226
  26.4 11.8 %collective-permute-start.8 = (bf16[51,16,128]{2,1,0:T(8,128)(2,1)S(1)}, bf16[51,16,128]{2,1,0:T(8,128)(2,1)S(1)}, u32[]{:S(2)}, u32[]{:S(2)}) collective-permute-start(bf16[51,16,128]{2,1,0:T(8,128)(2,1)S(1)} %collective-permute-done.7.refs_1_), channel_id=1, source_target_pairs={{0,7},{1,0},{2,1},{3,2},{4,3},{5,4},{6,5},{7,6},{8,15},{9,8},{10,9... | collective-permute-start | bytes 626696 | tf_op jit(solution)/shard_map/ppermute | solution.py:226
  29.8 11.8 %collective-permute-start.12 = (bf16[51,16,128]{2,1,0:T(8,128)(2,1)S(1)}, bf16[51,16,128]{2,1,0:T(8,128)(2,1)S(1)}, u32[]{:S(2)}, u32[]{:S(2)}) collective-permute-start(bf16[51,16,128]{2,1,0:T(8,128)(2,1)S(1)} %collective-permute-done.11.refs_6_), channel_id=1, source_target_pairs={{0,1},{1,2},{2,3},{3,4},{4,5},{5,6},{6,7},{7,0},{8,9},{9,10},{10,1... | collective-permute-start | bytes 626696 | tf_op jit(solution)/shard_map/ppermute | solution.py:223
  31.7 11.8 %collective-permute-start.5 = (bf16[51,16,128]{2,1,0:T(8,128)(2,1)S(1)}, bf16[51,16,128]{2,1,0:T(8,128)(2,1)S(1)}, u32[]{:S(2)}, u32[]{:S(2)}) collective-permute-start(bf16[51,16,128]{2,1,0:T(8,128)(2,1)S(1)} %collective-permute-done.4.refs_7_), channel_id=1, source_target_pairs={{0,1},{1,2},{2,3},{3,4},{4,5},{5,6},{6,7},{7,0},{8,9},{9,10},{10,1... | collective-permute-start | bytes 626696 | tf_op jit(solution)/shard_map/ppermute | solution.py:223
  33.7 11.8 %collective-permute-start.2 = (bf16[51,16,128]{2,1,0:T(8,128)(2,1)S(1)}, bf16[51,16,128]{2,1,0:T(8,128)(2,1)S(1)}, u32[]{:S(2)}, u32[]{:S(2)}) collective-permute-start(bf16[51,16,128]{2,1,0:T(8,128)(2,1)S(1)} %collective-permute-done.1.refs_2_), channel_id=1, source_target_pairs={{0,7},{1,0},{2,1},{3,2},{4,3},{5,4},{6,5},{7,6},{8,15},{9,8},{10,9... | collective-permute-start | bytes 626696 | tf_op jit(solution)/shard_map/ppermute | solution.py:226
  38.2 15.2 %collective-permute-start.9 = (bf16[51,16,128]{2,1,0:T(8,128)(2,1)S(1)}, bf16[51,16,128]{2,1,0:T(8,128)(2,1)S(1)}, u32[]{:S(2)}, u32[]{:S(2)}) collective-permute-start(bf16[51,16,128]{2,1,0:T(8,128)(2,1)S(1)} %collective-permute-done.8.refs_2_), channel_id=1, source_target_pairs={{0,7},{1,0},{2,1},{3,2},{4,3},{5,4},{6,5},{7,6},{8,15},{9,8},{10,9... | collective-permute-start | bytes 626696 | tf_op jit(solution)/shard_map/ppermute | solution.py:226
  41.6 11.9 %collective-permute-start.13 = (bf16[51,16,128]{2,1,0:T(8,128)(2,1)S(1)}, bf16[51,16,128]{2,1,0:T(8,128)(2,1)S(1)}, u32[]{:S(2)}, u32[]{:S(2)}) collective-permute-start(bf16[51,16,128]{2,1,0:T(8,128)(2,1)S(1)} %collective-permute-done.12.refs_5_), channel_id=1, source_target_pairs={{0,1},{1,2},{2,3},{3,4},{4,5},{5,6},{6,7},{7,0},{8,9},{9,10},{10,1... | collective-permute-start | bytes 626696 | tf_op jit(solution)/shard_map/ppermute | solution.py:223
  43.6 12.2 %collective-permute-start.6 = (bf16[51,16,128]{2,1,0:T(8,128)(2,1)S(1)}, bf16[51,16,128]{2,1,0:T(8,128)(2,1)S(1)}, u32[]{:S(2)}, u32[]{:S(2)}) collective-permute-start(bf16[51,16,128]{2,1,0:T(8,128)(2,1)S(1)} %collective-permute-done.5.refs_6_), channel_id=1, source_target_pairs={{0,1},{1,2},{2,3},{3,4},{4,5},{5,6},{6,7},{7,0},{8,9},{9,10},{10,1... | collective-permute-start | bytes 626696 | tf_op jit(solution)/shard_map/ppermute | solution.py:223
  45.5 10.3 %collective-permute-start.3 = (bf16[51,16,128]{2,1,0:T(8,128)(2,1)S(1)}, bf16[51,16,128]{2,1,0:T(8,128)(2,1)S(1)}, u32[]{:S(2)}, u32[]{:S(2)}) collective-permute-start(bf16[51,16,128]{2,1,0:T(8,128)(2,1)S(1)} %collective-permute-done.2.refs_3_), channel_id=1, source_target_pairs={{0,7},{1,0},{2,1},{3,2},{4,3},{5,4},{6,5},{7,6},{8,15},{9,8},{10,9... | collective-permute-start | bytes 626696 | tf_op jit(solution)/shard_map/ppermute | solution.py:226
  50.1 2.5 %copy-start.2 = (s32[256]{0:T(256)S(1)}, s32[256]{0:T(256)}, u32[]{:S(2)}) copy-start(s32[256]{0:T(256)} %param.8) | copy-start | bytes 3076
  50.1 2.5 %copy-start.3 = (s32[128]{0:T(128)S(1)}, s32[128]{0:T(128)}, u32[]{:S(2)}) copy-start(s32[128]{0:T(128)} %param.9) | copy-start | bytes 1540
  50.1 3.4 %copy-start.1 = (s32[640]{0:T(1024)S(1)}, s32[640]{0:T(1024)}, u32[]{:S(2)}) copy-start(s32[640]{0:T(1024)} %lower_ref.3) | copy-start | bytes 7684
  59.2 48.6 %all-to-all-start = ((bf16[64,80,128]{2,1,0:T(8,128)(2,1)}), bf16[64,80,128]{2,1,0:T(8,128)(2,1)S(1)}, u32[]{:S(2)}, u32[]{:S(2)}) async-start(bf16[64,80,128]{2,1,0:T(8,128)(2,1)} %bitcast.5), calls=%async_computation | async-start | bytes 2621440 | tf_op jit(solution)/shard_map/all_to_all | solution.py:255

commit v4 on v3

--- a/solution.py
+++ b/solution.py
@@ -49,7 +49,30 @@
     )(table)
 
 
-def rows_kernel(lat_dev, place_ref, slots_ref, points_ref, pick_ref, limit_ref):
+def even_partner(z):
+    return z + 1 - 2 * (z % 2)
+
+
+def odd_partner(z, n):
+    return (z + n - 1 + 2 * (z % 2)) % n
+
+
+def held_order(z, n, first):
+    partners = [even_partner, lambda i: odd_partner(i, n)]
+    near, far = partners[first], partners[1 - first]
+    pairs, via = [(z, near(z))], z
+    for step in range(1, n // 2):
+        origin, path = z, []
+        for k in range(step):
+            path.append(far if (step - k) % 2 else near)
+        for move in path:
+            origin = move(origin)
+        pairs.append((origin, near(origin)))
+    return [i for pair in pairs for i in pair]
+
+
+def rows_kernel(lat_dev, place_ref, slots_ref, points_ref, *out_refs):
+    pick_refs, limit_ref = out_refs[:-1], out_refs[-1]
     lats = slots_ref.shape[1]
     half = lats // 2
     n_wave = lats // lat_dev
@@ -59,9 +82,12 @@
     slots = jnp.broadcast_to(slots_ref[...].astype(F32), (ROWS, lats)).astype(BF)
     slots = jnp.dot(slots, moved, preferred_element_type=F32)[:1].astype(jnp.int32)
     cycle = lax.rem(slots, half)
-    held = lax.rem(cycle - place_ref[1] * ROWS + half, half) + (slots // half) * half
     index = lax.broadcasted_iota(jnp.int32, (lats, lats), 0)
-    pick_ref[...] = jnp.where(index == held, 1.0, 0.0).T.astype(BF)
+    for first, pick_ref in enumerate(pick_refs):
+        held = lax.rem(cycle, ROWS) + (slots // half) * half
+        for at, z in enumerate(held_order(place_ref[1], half // ROWS, first)):
+            held = held + jnp.where(cycle // ROWS == z, at * ROWS, 0)
+        pick_ref[...] = jnp.where(index == held, 1.0, 0.0).T.astype(BF)
     index = lax.broadcasted_iota(jnp.int32, (half, lats), 0)
     points = jnp.where(index == cycle, 1.0, 0.0).T * points_ref[...].astype(F32)
     limit_ref[...] = jnp.broadcast_to(jnp.sum(points, axis=1, keepdims=True), limit_ref.shape)
@@ -73,15 +99,15 @@
     return pl.pallas_call(
         functools.partial(rows_kernel, lat_dev),
         in_specs=[SMEM, VMEM, VMEM],
-        out_specs=[VMEM, VMEM],
-        out_shape=[jax.ShapeDtypeStruct((lats, lats), BF), jax.ShapeDtypeStruct((lats, LANES), F32)],
+        out_specs=[VMEM] * 3,
+        out_shape=[jax.ShapeDtypeStruct((lats, lats), BF)] * 2 + [jax.ShapeDtypeStruct((lats, LANES), F32)],
         compiler_params=PARAMS,
         name="row_order",
     )(place, slots, points)
 
 
 def sums_kernel(truncation, n_wave, first_pair, last_group, place_ref, lower_ref, pick_ref, limit_ref, spec_ref, *refs):
-    shard_refs, earlier, out_ref = refs[:8], refs[8:-2] if last_group else (), refs[-2] if last_group else refs[-1]
+    shard_refs, earlier, out_ref = refs[:5], refs[5:-2] if last_group else (), refs[-2] if last_group else refs[-1]
     rows_ref = refs[-1]
     all_pairs, _, half_slots, columns = spec_ref.shape
     lat_dev = pick_ref.shape[0] // n_wave
@@ -92,7 +118,9 @@
     plain = PLAIN * LANES
 
     def block(b, g):
-        return jnp.concatenate([ref[b] for ref in shard_refs], axis=0)
+        length = shard_refs[0].shape[0]
+        parts = [ref[b + at] for ref in shard_refs for at in range(0, ref.shape[0], length)]
+        return jnp.concatenate(parts, axis=0)
 
     def step(i, carry):
         for g in range(1):
@@ -215,24 +243,18 @@
     )(waves, *received)
 
 
-def gather_ring(groups):
+def gather_table(groups):
     n = lax.axis_size("fld")
-    assert n == 8 and len(groups) == 2
-
-    def up(x):
-        return lax.ppermute(x, "fld", [(i, (i + 1) % n) for i in range(n)])
-
-    def down(x):
-        return lax.ppermute(x, "fld", [(i, (i - 1) % n) for i in range(n)])
-
-    below, above = [[x] for x in groups], [[x] for x in groups]
+    kinds = [
+        [(i, even_partner(i)) for i in range(n)],
+        [(i, odd_partner(i, n)) for i in range(n)],
+    ]
+    held = [[x] for x in groups]
     for step in range(n // 2):
-        for g in range(2):
-            if step < n // 2 - 1 or g == 0:
-                below[g].append(up(below[g][-1]))
-            if step < n // 2 - 1 or g == 1:
-                above[g].append(down(above[g][-1]))
-    return [[groups[g]] + above[g][1:] + below[g][:0:-1] for g in range(2)]
+        for first, parts in enumerate(held):
+            sent = jnp.concatenate(parts, axis=0) if step == 1 else parts[-1]
+            parts.append(lax.ppermute(sent, "fld", kinds[(first + step) % 2]))
+    return held
 
 
 def on_device(spec_coeffs, legendre, pair_lower, slot_latitude, cycle_points):
@@ -243,12 +265,12 @@
     lat_dev = lats // n_wave
     group = pairs // 2
     place = jnp.stack([lax.axis_index("wave"), lax.axis_index("fld")]).astype(jnp.int32)
-    shards = gather_ring(pack_table(jnp.transpose(legendre, (0, 1, 3, 2)), 2))
-    pick, limit = row_order(place, slot_latitude.reshape(1, lats), cycle_points.reshape(1, lats // 2), lat_dev)
+    shards = gather_table(pack_table(jnp.transpose(legendre, (0, 1, 3, 2)), 2))
+    *picks, limit = row_order(place, slot_latitude.reshape(1, lats), cycle_points.reshape(1, lats // 2), lat_dev)
     rows = []
     for g in range(2):
         sums = legendre_sums(
-            place, pair_lower, pick, limit, spec_coeffs, shards[g], rows, g * group, group, g == 1, n_wave, truncation
+            place, pair_lower, picks[g], limit, spec_coeffs, shards[g], rows, g * group, group, g == 1, n_wave, truncation
         )
         rows.append(sums)
     sent = rows[-1].reshape(n_wave, -1, columns)

time: 112 us -> 110 us (0.982)
  starting transfers between devices: 63.2 us -> 44.7 us
  waiting for transfers between devices: 34.2 us -> 51 us
    ppermute x14 -> x8, starting transfers between devices: 48.7 us -> 31.2 us  [gather_table(): parts.append(lax.ppermute(sent, 'fld', kinds[(first + step) % 2]))]
    ppermute x14 -> x8, waiting for transfers between devices: 0.04 us -> 16.8 us  [gather_table(): parts.append(lax.ppermute(sent, 'fld', kinds[(first + step) % 2]))]
  transfers between devices with their start and end apart: 15 -> 9, of which waited for: 1 -> 5; matrix products, arithmetic and copies ran while one was open for 2% -> 2% of each run, Pallas kernels for 3% -> 3%
where the time goes in v4:
time: 110 us
  waiting for transfers between devices  51 us (46%)
  starting transfers between devices  44.7 us (41%)
  Pallas kernels  10.3 us (9%)
  local copies, waits for them, and re-layouts  3.43 us (3%)
    all_to_all x1, waiting for transfers between devices, on_device(): lax.all_to_all(sent, 'wave', split_axis=0, concat_axis=0, tiled=True)  34.1 us
    ppermute x8, starting transfers between devices, gather_table(): parts.append(lax.ppermute(sent, 'fld', kinds[(first + step) % 2]))  31.2 us
    ppermute x8, waiting for transfers between devices, gather_table(): parts.append(lax.ppermute(sent, 'fld', kinds[(first + step) % 2]))  16.8 us
    all_to_all x1, starting transfers between devices, on_device(): lax.all_to_all(sent, 'wave', split_axis=0, concat_axis=0, tiled=True)  13.5 us
    pallas_call x2, Pallas kernels, legendre_sums(): pl.pallas_call(functools.partial(sums_kernel, truncation, n_wave, first_p...  5.66 us
    pallas_call x1, Pallas kernels, place_waves(): pl.pallas_call(functools.partial(place_kernel, lat_dev), out_shape=jax.Sh...  3.58 us
    unnamed x9, local copies, waits for them, and re-layouts  3.42 us
  transfers between devices with their start and end apart: 9, of which 5 were waited for; matrix products, arithmetic and copies ran while one was open for 2% of the time, Pallas kernels for 3%

profile of v4, /device:TPU:1, one launch (start us, length us, event | category | flops | bytes accessed | tf_op | source)
XLA Modules:
  0.0 109.8 jit_solution(7567447969520885182)
XLA Ops:
  0.0 1.0 copy-done
  1.0 0.1 pack_table.1
  1.1 4.8 %collective-permute-start.4 = (bf16[51,16,128]{2,1,0:T(8,128)(2,1)S(1)}, bf16[51,16,128]{2,1,0:T(8,128)(2,1)S(1)}, u32[]{:S(2)}, u32[]{:S(2)}) collective-permute-start(bf16[51,16,128]{2,1,0:T(8,128)(2,1)S(1)} %get-tuple-element.14.refs_0_), channel_id=1, source_target_pairs={{0,1},{1,0},{2,3},{3,2},{4,5},{5,4},{6,7},{7,6},{8,9},{9,8},{10,11... | collective-permute-start | bytes 626696 | tf_op jit(solution)/shard_map/ppermute | solution.py:256
  6.0 8.8 %collective-permute-start = (bf16[51,16,128]{2,1,0:T(8,128)(2,1)S(1)}, bf16[51,16,128]{2,1,0:T(8,128)(2,1)S(1)}, u32[]{:S(2)}, u32[]{:S(2)}) collective-permute-start(bf16[51,16,128]{2,1,0:T(8,128)(2,1)S(1)} %get-tuple-element.12.refs_0_), channel_id=1, source_target_pairs={{0,7},{1,2},{2,1},{3,4},{4,3},{5,6},{6,5},{7,0},{8,15},{9,10},{10,... | collective-permute-start | bytes 626696 | tf_op jit(solution)/shard_map/ppermute | solution.py:256
  14.8 0.0 collective-permute-done.4.refs_1_
  14.9 5.7 %collective-permute-start.5 = (bf16[102,16,128]{2,1,0:T(8,128)(2,1)S(1)}, bf16[102,16,128]{2,1,0:T(8,128)(2,1)S(1)}, u32[]{:S(2)}, u32[]{:S(2)}) collective-permute-start(bf16[102,16,128]{2,1,0:T(8,128)(2,1)S(1)} %pad_maximum_fusion.1), channel_id=1, source_target_pairs={{0,7},{1,2},{2,1},{3,4},{4,3},{5,6},{6,5},{7,0},{8,15},{9,10},{10,... | collective-permute-start | bytes 1253384 | tf_op jit(solution)/shard_map/ppermute | solution.py:256
  20.6 0.0 collective-permute-done.refs_1_
  20.7 1.9 %collective-permute-start.1 = (bf16[102,16,128]{2,1,0:T(8,128)(2,1)S(1)}, bf16[102,16,128]{2,1,0:T(8,128)(2,1)S(1)}, u32[]{:S(2)}, u32[]{:S(2)}) collective-permute-start(bf16[102,16,128]{2,1,0:T(8,128)(2,1)S(1)} %pad_maximum_fusion), channel_id=1, source_target_pairs={{0,1},{1,0},{2,3},{3,2},{4,5},{5,4},{6,7},{7,6},{8,9},{9,8},{10,11... | collective-permute-start | bytes 1253384 | tf_op jit(solution)/shard_map/ppermute | solution.py:256
  22.6 6.4 %collective-permute-done.5.refs_2_ = bf16[102,16,128]{2,1,0:T(8,128)(2,1)S(1)} collective-permute-done((bf16[102,16,128]{2,1,0:T(8,128)(2,1)S(1)}, bf16[102,16,128]{2,1,0:T(8,128)(2,1)S(1)}, u32[]{:S(2)}, u32[]{:S(2)}) %collective-permute-start.5) | collective-permute-done | bytes 417824 | tf_op jit(solution)/shard_map/ppermute | solution.py:256
  29.0 1.9 %collective-permute-start.6 = (bf16[102,16,128]{2,1,0:T(8,128)(2,1)S(1)}, bf16[102,16,128]{2,1,0:T(8,128)(2,1)S(1)}, u32[]{:S(2)}, u32[]{:S(2)}) collective-permute-start(bf16[102,16,128]{2,1,0:T(8,128)(2,1)S(1)} %collective-permute-done.5.refs_2_), channel_id=1, source_target_pairs={{0,1},{1,0},{2,3},{3,2},{4,5},{5,4},{6,7},{7,6},{8,9},{9,8},{10,11... | collective-permute-start | bytes 1253384 | tf_op jit(solution)/shard_map/ppermute | solution.py:256
  30.9 1.0 collective-permute-done.1.refs_2_
  31.9 3.4 %collective-permute-start.2 = (bf16[102,16,128]{2,1,0:T(8,128)(2,1)S(1)}, bf16[102,16,128]{2,1,0:T(8,128)(2,1)S(1)}, u32[]{:S(2)}, u32[]{:S(2)}) collective-permute-start(bf16[102,16,128]{2,1,0:T(8,128)(2,1)S(1)} %collective-permute-done.1.refs_2_), channel_id=1, source_target_pairs={{0,7},{1,2},{2,1},{3,4},{4,3},{5,6},{6,5},{7,0},{8,15},{9,10},{10,... | collective-permute-start | bytes 1253384 | tf_op jit(solution)/shard_map/ppermute | solution.py:256
  35.2 5.9 %collective-permute-done.6.refs_3_ = bf16[102,16,128]{2,1,0:T(8,128)(2,1)S(1)} collective-permute-done((bf16[102,16,128]{2,1,0:T(8,128)(2,1)S(1)}, bf16[102,16,128]{2,1,0:T(8,128)(2,1)S(1)}, u32[]{:S(2)}, u32[]{:S(2)}) %collective-permute-start.6) | collective-permute-done | bytes 417824 | tf_op jit(solution)/shard_map/ppermute | solution.py:256
  41.1 2.7 %collective-permute-start.7 = (bf16[102,16,128]{2,1,0:T(8,128)(2,1)S(1)}, bf16[102,16,128]{2,1,0:T(8,128)(2,1)S(1)}, u32[]{:S(2)}, u32[]{:S(2)}) collective-permute-start(bf16[102,16,128]{2,1,0:T(8,128)(2,1)S(1)} %collective-permute-done.6.refs_3_), channel_id=1, source_target_pairs={{0,7},{1,2},{2,1},{3,4},{4,3},{5,6},{6,5},{7,0},{8,15},{9,10},{10,... | collective-permute-start | bytes 1253384 | tf_op jit(solution)/shard_map/ppermute | solution.py:256
  43.8 0.0 collective-permute-done.2.refs_3_
  43.8 1.9 %collective-permute-start.3 = (bf16[102,16,128]{2,1,0:T(8,128)(2,1)S(1)}, bf16[102,16,128]{2,1,0:T(8,128)(2,1)S(1)}, u32[]{:S(2)}, u32[]{:S(2)}) collective-permute-start(bf16[102,16,128]{2,1,0:T(8,128)(2,1)S(1)} %collective-permute-done.2.refs_3_), channel_id=1, source_target_pairs={{0,1},{1,0},{2,3},{3,2},{4,5},{5,4},{6,7},{7,6},{8,9},{9,8},{10,11... | collective-permute-start | bytes 1253384 | tf_op jit(solution)/shard_map/ppermute | solution.py:256
  45.8 0.0 copy-start.2
  45.8 0.0 copy-start.3
  45.8 0.0 copy-start.1
  45.8 2.4 %copy.7.spec_ref = bf16[10,2,641,128]{3,2,1,0:T(8,128)(2,1)S(1)} copy(bf16[10,2,641,128]{3,1,2,0:T(2,128)(2,1)} %param.5) | data formatting | bytes 6563840 | tf_op args[0]
  48.2 0.1 pad_add_fusion.1.place_ref
  48.3 0.0 copy-done.2
  48.3 0.0 copy-done.3
  48.3 0.9 row_order.1
  49.2 3.6 %collective-permute-done.7.refs_4_ = bf16[102,16,128]{2,1,0:T(8,128)(2,1)S(1)} collective-permute-done((bf16[102,16,128]{2,1,0:T(8,128)(2,1)S(1)}, bf16[102,16,128]{2,1,0:T(8,128)(2,1)S(1)}, u32[]{:S(2)}, u32[]{:S(2)}) %collective-permute-start.7) | collective-permute-done | bytes 417824 | tf_op jit(solution)/shard_map/ppermute | solution.py:256
  52.8 0.0 copy-done.1
  52.8 2.2 %legendre_sums.2.refs_5_ = f32[2560,128]{1,0:T(8,128)S(1)} custom-call(s32[2]{0:T(128)S(1)} %pad_add_fusion.1.place_ref, s32[640]{0:T(1024)S(1)} %copy-done.1, bf16[256,256]{1,0:T(8,128)(2,1)S(1)} %get-tuple-element.13.pick_ref, f32[256,128]{1,0:T(8,128)S(1)} %get-tuple-element.11.limit_ref, bf16[10,2,641,128]{3,2,1,0:T(8,128)(2,1)S(1)} %copy.7.spec_ref, ...), custom_call_target="tpu_custom_call" | custom-call | tf_op jit(solution)/shard_map/legendre_sums/pallas_call | solution.py:190
  55.1 0.0 collective-permute-done.3.refs_4_
  55.1 3.4 %legendre_sums.3 = bf16[5120,128]{1,0:T(8,128)(2,1)} custom-call(s32[2]{0:T(128)S(1)} %pad_add_fusion.1.place_ref, s32[640]{0:T(1024)S(1)} %copy-done.1, bf16[256,256]{1,0:T(8,128)(2,1)S(1)} %get-tuple-element.10.pick_ref, f32[256,128]{1,0:T(8,128)S(1)} %get-tuple-element.11.limit_ref, bf16[10,2,641,128]{3,2,1,0:T(8,128)(2,1)S(1)} %copy.7.spec_ref, ...), custom_call_target="tpu_custom_call" | custom-call | tf_op jit(solution)/shard_map/legendre_sums/pallas_call | solution.py:190
  58.5 13.5 %all-to-all-start = ((bf16[64,80,128]{2,1,0:T(8,128)(2,1)}), bf16[64,80,128]{2,1,0:T(8,128)(2,1)S(1)}, u32[]{:S(2)}, u32[]{:S(2)}) async-start(bf16[64,80,128]{2,1,0:T(8,128)(2,1)} %bitcast.5), calls=%async_computation | async-start | bytes 2621440 | tf_op jit(solution)/shard_map/all_to_all | solution.py:277
  72.1 34.1 %all-to-all-done = bf16[64,80,128]{2,1,0:T(8,128)(2,1)S(1)} async-done(((bf16[64,80,128]{2,1,0:T(8,128)(2,1)}), bf16[64,80,128]{2,1,0:T(8,128)(2,1)S(1)}, u32[]{:S(2)}, u32[]{:S(2)}) %all-to-all-start) | async-done | bytes 1310752 | tf_op jit(solution)/shard_map/all_to_all | solution.py:277
  106.2 3.6 %place_waves.1 = bf16[4,1280,128]{2,1,0:T(8,128)(2,1)} custom-call(s32[1,1280]{1,0:T(1,128)S(1)} %pad_add_fusion.waves_ref, bf16[5120,128]{1,0:T(8,128)(2,1)S(1)} %bitcast.7), custom_call_target="tpu_custom_call" | custom-call | tf_op jit(solution)/shard_map/place_waves/pallas_call | solution.py:234
  (7 shorter events, 0.1 us)
Async XLA Ops:
  0.0 1.0 copy-start
  1.1 13.7 %collective-permute-start.4 = (bf16[51,16,128]{2,1,0:T(8,128)(2,1)S(1)}, bf16[51,16,128]{2,1,0:T(8,128)(2,1)S(1)}, u32[]{:S(2)}, u32[]{:S(2)}) collective-permute-start(bf16[51,16,128]{2,1,0:T(8,128)(2,1)S(1)} %get-tuple-element.14.refs_0_), channel_id=1, source_target_pairs={{0,1},{1,0},{2,3},{3,2},{4,5},{5,4},{6,7},{7,6},{8,9},{9,8},{10,11... | collective-permute-start | bytes 626696 | tf_op jit(solution)/shard_map/ppermute | solution.py:256
  6.0 14.6 %collective-permute-start = (bf16[51,16,128]{2,1,0:T(8,128)(2,1)S(1)}, bf16[51,16,128]{2,1,0:T(8,128)(2,1)S(1)}, u32[]{:S(2)}, u32[]{:S(2)}) collective-permute-start(bf16[51,16,128]{2,1,0:T(8,128)(2,1)S(1)} %get-tuple-element.12.refs_0_), channel_id=1, source_target_pairs={{0,7},{1,2},{2,1},{3,4},{4,3},{5,6},{6,5},{7,0},{8,15},{9,10},{10,... | collective-permute-start | bytes 626696 | tf_op jit(solution)/shard_map/ppermute | solution.py:256
  14.9 14.1 %collective-permute-start.5 = (bf16[102,16,128]{2,1,0:T(8,128)(2,1)S(1)}, bf16[102,16,128]{2,1,0:T(8,128)(2,1)S(1)}, u32[]{:S(2)}, u32[]{:S(2)}) collective-permute-start(bf16[102,16,128]{2,1,0:T(8,128)(2,1)S(1)} %pad_maximum_fusion.1), channel_id=1, source_target_pairs={{0,7},{1,2},{2,1},{3,4},{4,3},{5,6},{6,5},{7,0},{8,15},{9,10},{10,... | collective-permute-start | bytes 1253384 | tf_op jit(solution)/shard_map/ppermute | solution.py:256
  20.7 11.2 %collective-permute-start.1 = (bf16[102,16,128]{2,1,0:T(8,128)(2,1)S(1)}, bf16[102,16,128]{2,1,0:T(8,128)(2,1)S(1)}, u32[]{:S(2)}, u32[]{:S(2)}) collective-permute-start(bf16[102,16,128]{2,1,0:T(8,128)(2,1)S(1)} %pad_maximum_fusion), channel_id=1, source_target_pairs={{0,1},{1,0},{2,3},{3,2},{4,5},{5,4},{6,7},{7,6},{8,9},{9,8},{10,11... | collective-permute-start | bytes 1253384 | tf_op jit(solution)/shard_map/ppermute | solution.py:256
  29.0 12.1 %collective-permute-start.6 = (bf16[102,16,128]{2,1,0:T(8,128)(2,1)S(1)}, bf16[102,16,128]{2,1,0:T(8,128)(2,1)S(1)}, u32[]{:S(2)}, u32[]{:S(2)}) collective-permute-start(bf16[102,16,128]{2,1,0:T(8,128)(2,1)S(1)} %collective-permute-done.5.refs_2_), channel_id=1, source_target_pairs={{0,1},{1,0},{2,3},{3,2},{4,5},{5,4},{6,7},{7,6},{8,9},{9,8},{10,11... | collective-permute-start | bytes 1253384 | tf_op jit(solution)/shard_map/ppermute | solution.py:256
  31.9 12.0 %collective-permute-start.2 = (bf16[102,16,128]{2,1,0:T(8,128)(2,1)S(1)}, bf16[102,16,128]{2,1,0:T(8,128)(2,1)S(1)}, u32[]{:S(2)}, u32[]{:S(2)}) collective-permute-start(bf16[102,16,128]{2,1,0:T(8,128)(2,1)S(1)} %collective-permute-done.1.refs_2_), channel_id=1, source_target_pairs={{0,7},{1,2},{2,1},{3,4},{4,3},{5,6},{6,5},{7,0},{8,15},{9,10},{10,... | collective-permute-start | bytes 1253384 | tf_op jit(solution)/shard_map/ppermute | solution.py:256
  41.1 11.7 %collective-permute-start.7 = (bf16[102,16,128]{2,1,0:T(8,128)(2,1)S(1)}, bf16[102,16,128]{2,1,0:T(8,128)(2,1)S(1)}, u32[]{:S(2)}, u32[]{:S(2)}) collective-permute-start(bf16[102,16,128]{2,1,0:T(8,128)(2,1)S(1)} %collective-permute-done.6.refs_3_), channel_id=1, source_target_pairs={{0,7},{1,2},{2,1},{3,4},{4,3},{5,6},{6,5},{7,0},{8,15},{9,10},{10,... | collective-permute-start | bytes 1253384 | tf_op jit(solution)/shard_map/ppermute | solution.py:256
  43.8 11.2 %collective-permute-start.3 = (bf16[102,16,128]{2,1,0:T(8,128)(2,1)S(1)}, bf16[102,16,128]{2,1,0:T(8,128)(2,1)S(1)}, u32[]{:S(2)}, u32[]{:S(2)}) collective-permute-start(bf16[102,16,128]{2,1,0:T(8,128)(2,1)S(1)} %collective-permute-done.2.refs_3_), channel_id=1, source_target_pairs={{0,1},{1,0},{2,3},{3,2},{4,5},{5,4},{6,7},{7,6},{8,9},{9,8},{10,11... | collective-permute-start | bytes 1253384 | tf_op jit(solution)/shard_map/ppermute | solution.py:256
  45.8 2.5 %copy-start.2 = (s32[256]{0:T(256)S(1)}, s32[256]{0:T(256)}, u32[]{:S(2)}) copy-start(s32[256]{0:T(256)} %param.8) | copy-start | bytes 3076
  45.8 2.5 %copy-start.3 = (s32[128]{0:T(128)S(1)}, s32[128]{0:T(128)}, u32[]{:S(2)}) copy-start(s32[128]{0:T(128)} %param.9) | copy-start | bytes 1540
  45.8 7.0 %copy-start.1 = (s32[640]{0:T(1024)S(1)}, s32[640]{0:T(1024)}, u32[]{:S(2)}) copy-start(s32[640]{0:T(1024)} %lower_ref.3) | copy-start | bytes 7684
  58.5 47.7 %all-to-all-start = ((bf16[64,80,128]{2,1,0:T(8,128)(2,1)}), bf16[64,80,128]{2,1,0:T(8,128)(2,1)S(1)}, u32[]{:S(2)}, u32[]{:S(2)}) async-start(bf16[64,80,128]{2,1,0:T(8,128)(2,1)} %bitcast.5), calls=%async_computation | async-start | bytes 2621440 | tf_op jit(solution)/shard_map/all_to_all | solution.py:277

commit v5 on v4

--- a/solution.py
+++ b/solution.py
@@ -14,8 +14,7 @@
 PLAIN = 2
 VMEM = pl.BlockSpec(memory_space=pltpu.VMEM)
 SMEM = pl.BlockSpec(memory_space=pltpu.SMEM)
-PIECE = 80
-UNROLL = True
+LEFT = 4
 PARAMS = pltpu.CompilerParams(vmem_limit_bytes=24 * 1024 * 1024)
 
 
@@ -106,37 +105,40 @@
     )(place, slots, points)
 
 
+def sent_row(pair, h, lat, lat_dev):
+    row = 2 * pair + h
+    return lat * ROWS + row if row < ROWS else lat_dev * ROWS + lat * LEFT + row - ROWS
+
+
 def sums_kernel(truncation, n_wave, first_pair, last_group, place_ref, lower_ref, pick_ref, limit_ref, spec_ref, *refs):
     shard_refs, earlier, out_ref = refs[:5], refs[5:-2] if last_group else (), refs[-2] if last_group else refs[-1]
     rows_ref = refs[-1]
     all_pairs, _, half_slots, columns = spec_ref.shape
     lat_dev = pick_ref.shape[0] // n_wave
     per_dev = rows_ref.shape[0] // n_wave
-    group = per_dev // (2 * lat_dev)
+    group = all_pairs // 2
     full = half_slots - 1
     blocks = full // LANES
     plain = PLAIN * LANES
 
-    def block(b, g):
+    def block(b):
         length = shard_refs[0].shape[0]
         parts = [ref[b + at] for ref in shard_refs for at in range(0, ref.shape[0], length)]
         return jnp.concatenate(parts, axis=0)
 
-    def step(i, carry):
-        for g in range(1):
-            local = i
-            pair = local + first_pair
+    def step(i):
+        for pair in (i + first_pair,):
             q = lower_ref[place_ref[0] * all_pairs + pair]
             length = truncation + 1 - q
             begin = length + lax.rem(length, 2)
-            tails = block(2 * group * blocks, g)
+            tails = block(2 * group * blocks)
             sums = []
             for r in range(2):
                 def owned(slot, coeffs, lower):
                     kept = slot < length if lower else (slot >= begin) & (slot <= begin + q)
                     return jnp.where(kept, coeffs, 0.0).astype(BF)
 
-                table = [block((2 * i + r) * blocks + b, g) for b in range(blocks)]
+                table = [block((2 * i + r) * blocks + b) for b in range(blocks)]
                 below = jnp.dot(
                     jnp.concatenate(table[:PLAIN], axis=1), spec_ref[pair, r, :plain, :], preferred_element_type=F32
                 )
@@ -163,30 +165,36 @@
                 wave = (q if h == 0 else truncation - q).astype(F32)
                 kept = jnp.where(2.0 * wave < limit_ref[...], picked[:, h * columns:(h + 1) * columns], 0.0)
                 for lat in range(lat_dev):
-                    start = (2 * local + h) * lat_dev + lat
-                    rows_ref[pl.ds(start, n_wave, stride=per_dev), :] = kept[lat * n_wave:(lat + 1) * n_wave]
+                    at = pl.ds(sent_row(pair, h, lat, lat_dev), n_wave, stride=per_dev)
+                    rows_ref[at, :] = kept[lat * n_wave:(lat + 1) * n_wave]
+
+    for i in range(group):
+        step(i)
+
+    def narrow(d, carry):
+        base = pl.multiple_of(d * per_dev, per_dev)
+        parts = []
+        for at in range(0, per_dev, 8):
+            there = 2 * group - at % ROWS if at < lat_dev * ROWS else 0
+            rows = pl.ds(base + at, 8)
+            if there <= 0:
+                parts.append(rows_ref[rows, :])
+            elif there >= 8:
+                parts.append(earlier[0][rows, :])
+            else:
+                row = lax.broadcasted_iota(jnp.int32, (8, columns), 0)
+                parts.append(jnp.where(row < there, earlier[0][rows, :], rows_ref[rows, :]))
+        out_ref[pl.ds(base, per_dev), :] = jnp.concatenate(parts, axis=0).astype(BF)
         return carry
 
-    lax.fori_loop(0, group, step, 0, unroll=UNROLL)
-
-    def narrow(d, carry):
-        at = pl.ds(pl.multiple_of(d * per_dev, per_dev), per_dev)
-        parts = [ref[at, :] for ref in earlier + (rows_ref,)]
-        sent = per_dev * len(parts)
-        out_ref[pl.ds(pl.multiple_of(d * sent, sent), sent), :] = jnp.concatenate(parts, axis=0).astype(BF)
-        return carry
-
     if last_group:
-        lax.fori_loop(0, n_wave, narrow, 0, unroll=8)
+        lax.fori_loop(0, n_wave, narrow, 0, unroll=16)
 
 
 def legendre_sums(place, pair_lower, pick, limit, spec, shards, earlier, first_pair, group, last, n_wave, truncation):
     columns = spec.shape[3]
-    rows = 2 * group * pick.shape[0]
-    if last:
-        out = jax.ShapeDtypeStruct((rows * (1 + len(earlier)), columns), BF)
-    else:
-        out, earlier = jax.ShapeDtypeStruct((rows, columns), F32), []
+    rows = 4 * group * pick.shape[0]
+    out = jax.ShapeDtypeStruct((rows, columns), BF if last else F32)
     return pl.pallas_call(
         functools.partial(sums_kernel, truncation, n_wave, first_pair, last),
         in_specs=[SMEM, SMEM] + [VMEM] * (3 + len(shards) + len(earlier)),
@@ -198,49 +206,48 @@
     )(place, pair_lower, pick, limit, spec, *shards, *earlier)
 
 
-def place_kernel(lat_dev, waves_ref, *refs):
-    received_refs, (out_ref, rows_ref, held_ref) = refs[:-3], refs[-3:]
-    count = waves_ref.shape[1]
-    columns = out_ref.shape[2]
-    base = 0
-    for received_ref in received_refs:
-        rows = received_ref.shape[0]
-
-        def widen(d, carry):
-            at = pl.multiple_of(d * PIECE, PIECE)
-            rows_ref[pl.ds(at + base * 2 * lat_dev, PIECE), :] = received_ref[pl.ds(at, PIECE), :].astype(F32)
-            return carry
-
-        lax.fori_loop(0, rows // PIECE, widen, 0, unroll=8)
-        many = rows // (2 * lat_dev)
-        for h in range(2):
-            for lat in range(lat_dev):
-                taken = rows_ref[pl.ds(base * 2 * lat_dev + h * lat_dev + lat, many, stride=2 * lat_dev), :]
-                at = 2 * base + h * many
-                held_ref[at:at + many, lat * columns:(lat + 1) * columns] = taken.astype(BF)
-        base += many
-    tall = 256
-    for m in range(0, count, tall):
-        index = lax.broadcasted_iota(jnp.int32, (tall, count), 0) + m
+def place_kernel(waves_ref, received_ref, out_ref, rows_ref, left_ref, placed_ref, sems):
+    lat_dev, count, columns = placed_ref.shape
+    n_wave = received_ref.shape[0]
+    main = n_wave * ROWS
+    rows_ref[...] = received_ref[:, lat_dev * ROWS:, :].astype(F32).reshape(rows_ref.shape)
+    for lat in range(lat_dev):
+        for i in range(LEFT):
+            rows = rows_ref[pl.ds(lat * LEFT + i, n_wave, stride=lat_dev * LEFT), :]
+            left_ref[i * n_wave:(i + 1) * n_wave, lat * columns:(lat + 1) * columns] = rows.astype(BF)
+    held = [received_ref[:, lat * ROWS:(lat + 1) * ROWS, :].reshape(main, columns) for lat in range(lat_dev)]
+    held = jnp.concatenate([jnp.concatenate(held, axis=1), left_ref[...]], axis=0)
+    tall = count // 4
+    copies = []
+    for n in range(4):
+        index = lax.broadcasted_iota(jnp.int32, (tall, count), 0) + n * tall
         chosen = jnp.where(index == waves_ref[...], 1.0, 0.0).astype(BF)
-        placed = jnp.dot(chosen, held_ref[...], preferred_element_type=F32).astype(BF)
+        placed = jnp.dot(chosen, held, preferred_element_type=F32).astype(BF)
+        at = pl.ds(n * tall, tall)
         for lat in range(lat_dev):
-            out_ref[lat, m:m + tall, :] = placed[:, lat * columns:(lat + 1) * columns]
+            placed_ref[lat, n * tall:(n + 1) * tall, :] = placed[:, lat * columns:(lat + 1) * columns]
+        copies.append(pltpu.make_async_copy(placed_ref.at[:, at, :], out_ref.at[:, at, :], sems.at[n]))
+        copies[-1].start()
+    for copy in copies:
+        copy.wait()
 
 
 def place_waves(waves, received, lat_dev):
     count = waves.shape[1]
-    columns = received[0].shape[1]
-    return pl.pallas_call(
-        functools.partial(place_kernel, lat_dev),
+    n_wave, _, columns = received.shape
+    return pl.pallas_call(
+        place_kernel,
+        out_specs=pl.BlockSpec(memory_space=pltpu.HBM),
         out_shape=jax.ShapeDtypeStruct((lat_dev, count, columns), BF),
         scratch_shapes=[
-            pltpu.VMEM((lat_dev * count, columns), F32),
-            pltpu.VMEM((count, lat_dev * columns), BF),
+            pltpu.VMEM((n_wave * lat_dev * LEFT, columns), F32),
+            pltpu.VMEM((n_wave * LEFT, lat_dev * columns), BF),
+            pltpu.VMEM((lat_dev, count, columns), BF),
+            pltpu.SemaphoreType.DMA((4,)),
         ],
         compiler_params=PARAMS,
         name="place_waves",
-    )(waves, *received)
+    )(waves, received)
 
 
 def gather_table(groups):
@@ -267,16 +274,18 @@
     place = jnp.stack([lax.axis_index("wave"), lax.axis_index("fld")]).astype(jnp.int32)
     shards = gather_table(pack_table(jnp.transpose(legendre, (0, 1, 3, 2)), 2))
     *picks, limit = row_order(place, slot_latitude.reshape(1, lats), cycle_points.reshape(1, lats // 2), lat_dev)
+    assert 2 * pairs == ROWS + LEFT and lat_dev * LEFT == ROWS
     rows = []
     for g in range(2):
         sums = legendre_sums(
             place, pair_lower, picks[g], limit, spec_coeffs, shards[g], rows, g * group, group, g == 1, n_wave, truncation
         )
         rows.append(sums)
-    sent = rows[-1].reshape(n_wave, -1, columns)
-    received = [lax.all_to_all(sent, "wave", split_axis=0, concat_axis=0, tiled=True).reshape(-1, columns)]
-    lower = pair_lower.reshape(1, -1)
-    waves = jnp.concatenate([lower, truncation - lower], axis=1)
+    sent, lower = lax.optimization_barrier((rows[-1].reshape(n_wave, -1, columns), pair_lower))
+    received = lax.all_to_all(sent, "wave", split_axis=0, concat_axis=0, tiled=True)
+    lower = lower.reshape(n_wave, pairs)
+    held = jnp.stack([lower, truncation - lower], axis=2).reshape(n_wave, 2 * pairs)
+    waves = jnp.concatenate([held[:, :ROWS].reshape(-1), held[:, ROWS:].T.reshape(-1)]).reshape(1, truncation + 1)
     return place_waves(waves, received, lat_dev)
 
 

time: 110 us -> 110 us (level)
  transfers between devices with their start and end apart: 9 -> 9, of which waited for: 5 -> 5; matrix products, arithmetic and copies ran while one was open for 2% -> 3% of each run, Pallas kernels for 3% -> 3%
where the time goes in v5:
time: 110 us; the launch traced here: 109 us
  waiting for transfers between devices  50.4 us (46%)
  starting transfers between devices  44.8 us (41%)
  Pallas kernels  9.75 us (9%)
  local copies, waits for them, and re-layouts  3.97 us (4%)
    all_to_all x1, waiting for transfers between devices, on_device(): lax.all_to_all(sent, 'wave', split_axis=0, concat_axis=0, tiled=True)  33.6 us
    ppermute x8, starting transfers between devices, gather_table(): parts.append(lax.ppermute(sent, 'fld', kinds[(first + step) % 2]))  31.2 us
    ppermute x8, waiting for transfers between devices, gather_table(): parts.append(lax.ppermute(sent, 'fld', kinds[(first + step) % 2]))  16.8 us
    all_to_all x1, starting transfers between devices, on_device(): lax.all_to_all(sent, 'wave', split_axis=0, concat_axis=0, tiled=True)  13.5 us
    pallas_call x2, Pallas kernels, legendre_sums(): pl.pallas_call(functools.partial(sums_kernel, truncation, n_wave, first_p...  5.93 us
    unnamed x9, local copies, waits for them, and re-layouts  3.42 us
    pallas_call x1, Pallas kernels, place_waves(): pl.pallas_call(place_kernel, out_specs=pl.BlockSpec(memory_space=pltpu.HB...  2.78 us
  transfers between devices with their start and end apart: 9, of which 5 were waited for; matrix products, arithmetic and copies ran while one was open for 3% of the time, Pallas kernels for 3%

profile of v5, /device:TPU:1, one launch (start us, length us, event | category | flops | bytes accessed | tf_op | source)
XLA Modules:
  0.0 109.3 jit_solution(8542197105234650404)
XLA Ops:
  0.0 1.0 copy-done
  1.0 0.1 pack_table.1
  1.1 4.8 %collective-permute-start.4 = (bf16[51,16,128]{2,1,0:T(8,128)(2,1)S(1)}, bf16[51,16,128]{2,1,0:T(8,128)(2,1)S(1)}, u32[]{:S(2)}, u32[]{:S(2)}) collective-permute-start(bf16[51,16,128]{2,1,0:T(8,128)(2,1)S(1)} %get-tuple-element.16.refs_0_), channel_id=1, source_target_pairs={{0,1},{1,0},{2,3},{3,2},{4,5},{5,4},{6,7},{7,6},{8,9},{9,8},{10,11... | collective-permute-start | bytes 626696 | tf_op jit(solution)/shard_map/ppermute | solution.py:263
  6.0 8.8 %collective-permute-start = (bf16[51,16,128]{2,1,0:T(8,128)(2,1)S(1)}, bf16[51,16,128]{2,1,0:T(8,128)(2,1)S(1)}, u32[]{:S(2)}, u32[]{:S(2)}) collective-permute-start(bf16[51,16,128]{2,1,0:T(8,128)(2,1)S(1)} %get-tuple-element.14.refs_0_), channel_id=1, source_target_pairs={{0,7},{1,2},{2,1},{3,4},{4,3},{5,6},{6,5},{7,0},{8,15},{9,10},{10,... | collective-permute-start | bytes 626696 | tf_op jit(solution)/shard_map/ppermute | solution.py:263
  14.8 0.0 collective-permute-done.4.refs_1_
  14.9 5.7 %collective-permute-start.5 = (bf16[102,16,128]{2,1,0:T(8,128)(2,1)S(1)}, bf16[102,16,128]{2,1,0:T(8,128)(2,1)S(1)}, u32[]{:S(2)}, u32[]{:S(2)}) collective-permute-start(bf16[102,16,128]{2,1,0:T(8,128)(2,1)S(1)} %pad_maximum_fusion.1), channel_id=1, source_target_pairs={{0,7},{1,2},{2,1},{3,4},{4,3},{5,6},{6,5},{7,0},{8,15},{9,10},{10,... | collective-permute-start | bytes 1253384 | tf_op jit(solution)/shard_map/ppermute | solution.py:263
  20.7 1.9 %collective-permute-start.1 = (bf16[102,16,128]{2,1,0:T(8,128)(2,1)S(1)}, bf16[102,16,128]{2,1,0:T(8,128)(2,1)S(1)}, u32[]{:S(2)}, u32[]{:S(2)}) collective-permute-start(bf16[102,16,128]{2,1,0:T(8,128)(2,1)S(1)} %pad_maximum_fusion), channel_id=1, source_target_pairs={{0,1},{1,0},{2,3},{3,2},{4,5},{5,4},{6,7},{7,6},{8,9},{9,8},{10,11... | collective-permute-start | bytes 1253384 | tf_op jit(solution)/shard_map/ppermute | solution.py:263
  22.6 6.4 %collective-permute-done.5.refs_2_ = bf16[102,16,128]{2,1,0:T(8,128)(2,1)S(1)} collective-permute-done((bf16[102,16,128]{2,1,0:T(8,128)(2,1)S(1)}, bf16[102,16,128]{2,1,0:T(8,128)(2,1)S(1)}, u32[]{:S(2)}, u32[]{:S(2)}) %collective-permute-start.5) | collective-permute-done | bytes 417824 | tf_op jit(solution)/shard_map/ppermute | solution.py:263
  29.0 1.9 %collective-permute-start.6 = (bf16[102,16,128]{2,1,0:T(8,128)(2,1)S(1)}, bf16[102,16,128]{2,1,0:T(8,128)(2,1)S(1)}, u32[]{:S(2)}, u32[]{:S(2)}) collective-permute-start(bf16[102,16,128]{2,1,0:T(8,128)(2,1)S(1)} %collective-permute-done.5.refs_2_), channel_id=1, source_target_pairs={{0,1},{1,0},{2,3},{3,2},{4,5},{5,4},{6,7},{7,6},{8,9},{9,8},{10,11... | collective-permute-start | bytes 1253384 | tf_op jit(solution)/shard_map/ppermute | solution.py:263
  30.9 1.0 collective-permute-done.1.refs_2_
  31.9 3.4 %collective-permute-start.2 = (bf16[102,16,128]{2,1,0:T(8,128)(2,1)S(1)}, bf16[102,16,128]{2,1,0:T(8,128)(2,1)S(1)}, u32[]{:S(2)}, u32[]{:S(2)}) collective-permute-start(bf16[102,16,128]{2,1,0:T(8,128)(2,1)S(1)} %collective-permute-done.1.refs_2_), channel_id=1, source_target_pairs={{0,7},{1,2},{2,1},{3,4},{4,3},{5,6},{6,5},{7,0},{8,15},{9,10},{10,... | collective-permute-start | bytes 1253384 | tf_op jit(solution)/shard_map/ppermute | solution.py:263
  35.2 5.9 %collective-permute-done.6.refs_3_ = bf16[102,16,128]{2,1,0:T(8,128)(2,1)S(1)} collective-permute-done((bf16[102,16,128]{2,1,0:T(8,128)(2,1)S(1)}, bf16[102,16,128]{2,1,0:T(8,128)(2,1)S(1)}, u32[]{:S(2)}, u32[]{:S(2)}) %collective-permute-start.6) | collective-permute-done | bytes 417824 | tf_op jit(solution)/shard_map/ppermute | solution.py:263
  41.1 2.7 %collective-permute-start.7 = (bf16[102,16,128]{2,1,0:T(8,128)(2,1)S(1)}, bf16[102,16,128]{2,1,0:T(8,128)(2,1)S(1)}, u32[]{:S(2)}, u32[]{:S(2)}) collective-permute-start(bf16[102,16,128]{2,1,0:T(8,128)(2,1)S(1)} %collective-permute-done.6.refs_3_), channel_id=1, source_target_pairs={{0,7},{1,2},{2,1},{3,4},{4,3},{5,6},{6,5},{7,0},{8,15},{9,10},{10,... | collective-permute-start | bytes 1253384 | tf_op jit(solution)/shard_map/ppermute | solution.py:263
  43.8 1.9 %collective-permute-start.3 = (bf16[102,16,128]{2,1,0:T(8,128)(2,1)S(1)}, bf16[102,16,128]{2,1,0:T(8,128)(2,1)S(1)}, u32[]{:S(2)}, u32[]{:S(2)}) collective-permute-start(bf16[102,16,128]{2,1,0:T(8,128)(2,1)S(1)} %collective-permute-done.2.refs_3_), channel_id=1, source_target_pairs={{0,1},{1,0},{2,3},{3,2},{4,5},{5,4},{6,7},{7,6},{8,9},{9,8},{10,11... | collective-permute-start | bytes 1253384 | tf_op jit(solution)/shard_map/ppermute | solution.py:263
  45.8 0.0 copy-start.2
  45.8 0.0 copy-start.3
  45.8 0.0 copy-start.1
  45.8 2.4 %copy.13.spec_ref = bf16[10,2,641,128]{3,2,1,0:T(8,128)(2,1)S(1)} copy(bf16[10,2,641,128]{3,1,2,0:T(2,128)(2,1)} %param.5) | data formatting | bytes 6563840 | tf_op args[0]
  48.2 0.1 pad_add_fusion.2.place_ref
  48.3 0.9 row_order.1
  49.2 3.6 %collective-permute-done.7.refs_4_ = bf16[102,16,128]{2,1,0:T(8,128)(2,1)S(1)} collective-permute-done((bf16[102,16,128]{2,1,0:T(8,128)(2,1)S(1)}, bf16[102,16,128]{2,1,0:T(8,128)(2,1)S(1)}, u32[]{:S(2)}, u32[]{:S(2)}) %collective-permute-start.7) | collective-permute-done | bytes 417824 | tf_op jit(solution)/shard_map/ppermute | solution.py:263
  52.8 2.3 %legendre_sums.2.refs_5_ = f32[5120,128]{1,0:T(8,128)S(1)} custom-call(s32[2]{0:T(128)S(1)} %pad_add_fusion.2.place_ref, s32[640]{0:T(1024)S(1)} %copy-done.1, bf16[256,256]{1,0:T(8,128)(2,1)S(1)} %get-tuple-element.15.pick_ref, f32[256,128]{1,0:T(8,128)S(1)} %get-tuple-element.13.limit_ref, bf16[10,2,641,128]{3,2,1,0:T(8,128)(2,1)S(1)} %copy.13.spec_ref, ...), custom_call_target="tpu_custom_call" | custom-call | tf_op jit(solution)/shard_map/legendre_sums/pallas_call | solution.py:198
  55.2 3.6 %legendre_sums.3 = bf16[5120,128]{1,0:T(8,128)(2,1)} custom-call(s32[2]{0:T(128)S(1)} %pad_add_fusion.2.place_ref, s32[640]{0:T(1024)S(1)} %copy-done.1, bf16[256,256]{1,0:T(8,128)(2,1)S(1)} %get-tuple-element.12.pick_ref, f32[256,128]{1,0:T(8,128)S(1)} %get-tuple-element.13.limit_ref, bf16[10,2,641,128]{3,2,1,0:T(8,128)(2,1)S(1)} %copy.13.spec_ref, ...), custom_call_target="tpu_custom_call" | custom-call | tf_op jit(solution)/shard_map/legendre_sums/pallas_call | solution.py:198
  58.8 13.5 %all-to-all-start = ((bf16[64,80,128]{2,1,0:T(8,128)(2,1)}), bf16[64,80,128]{2,1,0:T(8,128)(2,1)S(1)}, u32[]{:S(2)}, u32[]{:S(2)}) async-start(bf16[64,80,128]{2,1,0:T(8,128)(2,1)} %bitcast.5), calls=%async_computation | async-start | bytes 2621440 | tf_op jit(solution)/shard_map/all_to_all | solution.py:285
  72.3 0.1 stack_reshape.3
  72.4 0.1 copy.14
  72.5 0.1 copy.15
  72.7 0.1 copy.16
  72.8 0.1 reshape.36
  72.8 0.1 reshape.37
  72.9 33.6 %all-to-all-done.received_ref = bf16[64,80,128]{2,1,0:T(8,128)(2,1)S(1)} async-done(((bf16[64,80,128]{2,1,0:T(8,128)(2,1)}), bf16[64,80,128]{2,1,0:T(8,128)(2,1)S(1)}, u32[]{:S(2)}, u32[]{:S(2)}) %all-to-all-start) | async-done | bytes 1310752 | tf_op jit(solution)/shard_map/all_to_all | solution.py:285
  106.5 2.8 %place_waves.1 = bf16[4,1280,128]{2,1,0:T(8,128)(2,1)} custom-call(s32[1,1280]{1,0:T(1,128)S(1)} %reshape.38.waves_ref, bf16[64,80,128]{2,1,0:T(8,128)(2,1)S(1)} %all-to-all-done.received_ref), custom_call_target="tpu_custom_call" | custom-call | tf_op jit(solution)/shard_map/place_waves/pallas_call | solution.py:238
  (16 shorter events, 0.2 us)
Async XLA Ops:
  0.0 1.0 copy-start
  1.1 13.7 %collective-permute-start.4 = (bf16[51,16,128]{2,1,0:T(8,128)(2,1)S(1)}, bf16[51,16,128]{2,1,0:T(8,128)(2,1)S(1)}, u32[]{:S(2)}, u32[]{:S(2)}) collective-permute-start(bf16[51,16,128]{2,1,0:T(8,128)(2,1)S(1)} %get-tuple-element.16.refs_0_), channel_id=1, source_target_pairs={{0,1},{1,0},{2,3},{3,2},{4,5},{5,4},{6,7},{7,6},{8,9},{9,8},{10,11... | collective-permute-start | bytes 626696 | tf_op jit(solution)/shard_map/ppermute | solution.py:263
  6.0 14.6 %collective-permute-start = (bf16[51,16,128]{2,1,0:T(8,128)(2,1)S(1)}, bf16[51,16,128]{2,1,0:T(8,128)(2,1)S(1)}, u32[]{:S(2)}, u32[]{:S(2)}) collective-permute-start(bf16[51,16,128]{2,1,0:T(8,128)(2,1)S(1)} %get-tuple-element.14.refs_0_), channel_id=1, source_target_pairs={{0,7},{1,2},{2,1},{3,4},{4,3},{5,6},{6,5},{7,0},{8,15},{9,10},{10,... | collective-permute-start | bytes 626696 | tf_op jit(solution)/shard_map/ppermute | solution.py:263
  14.9 14.1 %collective-permute-start.5 = (bf16[102,16,128]{2,1,0:T(8,128)(2,1)S(1)}, bf16[102,16,128]{2,1,0:T(8,128)(2,1)S(1)}, u32[]{:S(2)}, u32[]{:S(2)}) collective-permute-start(bf16[102,16,128]{2,1,0:T(8,128)(2,1)S(1)} %pad_maximum_fusion.1), channel_id=1, source_target_pairs={{0,7},{1,2},{2,1},{3,4},{4,3},{5,6},{6,5},{7,0},{8,15},{9,10},{10,... | collective-permute-start | bytes 1253384 | tf_op jit(solution)/shard_map/ppermute | solution.py:263
  20.7 11.2 %collective-permute-start.1 = (bf16[102,16,128]{2,1,0:T(8,128)(2,1)S(1)}, bf16[102,16,128]{2,1,0:T(8,128)(2,1)S(1)}, u32[]{:S(2)}, u32[]{:S(2)}) collective-permute-start(bf16[102,16,128]{2,1,0:T(8,128)(2,1)S(1)} %pad_maximum_fusion), channel_id=1, source_target_pairs={{0,1},{1,0},{2,3},{3,2},{4,5},{5,4},{6,7},{7,6},{8,9},{9,8},{10,11... | collective-permute-start | bytes 1253384 | tf_op jit(solution)/shard_map/ppermute | solution.py:263
  29.0 12.1 %collective-permute-start.6 = (bf16[102,16,128]{2,1,0:T(8,128)(2,1)S(1)}, bf16[102,16,128]{2,1,0:T(8,128)(2,1)S(1)}, u32[]{:S(2)}, u32[]{:S(2)}) collective-permute-start(bf16[102,16,128]{2,1,0:T(8,128)(2,1)S(1)} %collective-permute-done.5.refs_2_), channel_id=1, source_target_pairs={{0,1},{1,0},{2,3},{3,2},{4,5},{5,4},{6,7},{7,6},{8,9},{9,8},{10,11... | collective-permute-start | bytes 1253384 | tf_op jit(solution)/shard_map/ppermute | solution.py:263
  31.9 12.0 %collective-permute-start.2 = (bf16[102,16,128]{2,1,0:T(8,128)(2,1)S(1)}, bf16[102,16,128]{2,1,0:T(8,128)(2,1)S(1)}, u32[]{:S(2)}, u32[]{:S(2)}) collective-permute-start(bf16[102,16,128]{2,1,0:T(8,128)(2,1)S(1)} %collective-permute-done.1.refs_2_), channel_id=1, source_target_pairs={{0,7},{1,2},{2,1},{3,4},{4,3},{5,6},{6,5},{7,0},{8,15},{9,10},{10,... | collective-permute-start | bytes 1253384 | tf_op jit(solution)/shard_map/ppermute | solution.py:263
  41.1 11.7 %collective-permute-start.7 = (bf16[102,16,128]{2,1,0:T(8,128)(2,1)S(1)}, bf16[102,16,128]{2,1,0:T(8,128)(2,1)S(1)}, u32[]{:S(2)}, u32[]{:S(2)}) collective-permute-start(bf16[102,16,128]{2,1,0:T(8,128)(2,1)S(1)} %collective-permute-done.6.refs_3_), channel_id=1, source_target_pairs={{0,7},{1,2},{2,1},{3,4},{4,3},{5,6},{6,5},{7,0},{8,15},{9,10},{10,... | collective-permute-start | bytes 1253384 | tf_op jit(solution)/shard_map/ppermute | solution.py:263
  43.8 11.3 %collective-permute-start.3 = (bf16[102,16,128]{2,1,0:T(8,128)(2,1)S(1)}, bf16[102,16,128]{2,1,0:T(8,128)(2,1)S(1)}, u32[]{:S(2)}, u32[]{:S(2)}) collective-permute-start(bf16[102,16,128]{2,1,0:T(8,128)(2,1)S(1)} %collective-permute-done.2.refs_3_), channel_id=1, source_target_pairs={{0,1},{1,0},{2,3},{3,2},{4,5},{5,4},{6,7},{7,6},{8,9},{9,8},{10,11... | collective-permute-start | bytes 1253384 | tf_op jit(solution)/shard_map/ppermute | solution.py:263
  45.8 2.5 %copy-start.2 = (s32[256]{0:T(256)S(1)}, s32[256]{0:T(256)}, u32[]{:S(2)}) copy-start(s32[256]{0:T(256)} %param.8) | copy-start | bytes 3076
  45.8 2.5 %copy-start.3 = (s32[128]{0:T(128)S(1)}, s32[128]{0:T(128)}, u32[]{:S(2)}) copy-start(s32[128]{0:T(128)} %param.9) | copy-start | bytes 1540
  45.8 7.0 %copy-start.1 = (s32[640]{0:T(1024)S(1)}, s32[640]{0:T(1024)}, u32[]{:S(2)}) copy-start(s32[640]{0:T(1024)} %lower_ref.3) | copy-start | bytes 7684
  58.8 47.7 %all-to-all-start = ((bf16[64,80,128]{2,1,0:T(8,128)(2,1)}), bf16[64,80,128]{2,1,0:T(8,128)(2,1)S(1)}, u32[]{:S(2)}, u32[]{:S(2)}) async-start(bf16[64,80,128]{2,1,0:T(8,128)(2,1)} %bitcast.5), calls=%async_computation | async-start | bytes 2621440 | tf_op jit(solution)/shard_map/all_to_all | solution.py:285

commit v6 on v5

--- a/solution.py
+++ b/solution.py
@@ -18,34 +18,40 @@
 PARAMS = pltpu.CompilerParams(vmem_limit_bytes=24 * 1024 * 1024)
 
 
-def pack_kernel(table_ref, *out_refs):
-    pairs, _, rows, half_slots = table_ref.shape
+def pack_kernel(first, table_ref, out_ref, held_ref, sem):
+    group, _, rows, half_slots = held_ref.shape
     blocks = half_slots // LANES
-    group = pairs // len(out_refs)
+    fetch = pltpu.make_async_copy(table_ref.at[pl.ds(first, group)], held_ref, sem)
+    fetch.start()
+    fetch.wait()
     lane = lax.broadcasted_iota(jnp.int32, (rows, LANES), 1)
-    for g, out_ref in enumerate(out_refs):
-        last = jnp.zeros((rows, LANES), F32)
-        for i in range(group):
-            for r in range(2):
-                for b in range(blocks):
-                    out_ref[(2 * i + r) * blocks + b] = table_ref[g * group + i, r, :, b * LANES:(b + 1) * LANES]
-                tail = table_ref[g * group + i, r, :, half_slots - 1:half_slots].astype(F32)
-                last = jnp.where(lane == 2 * i + r, tail, last)
-        out_ref[2 * group * blocks] = last.astype(BF)
+    last = jnp.zeros((rows, LANES), F32)
+    for i in range(group):
+        for r in range(2):
+            for b in range(blocks):
+                out_ref[(2 * i + r) * blocks + b] = held_ref[i, r, :, b * LANES:(b + 1) * LANES]
+            tail = held_ref[i, r, :, half_slots - 1:half_slots].astype(F32)
+            last = jnp.where(lane == 2 * i + r, tail, last)
+    out_ref[2 * group * blocks] = last.astype(BF)
 
 
 def pack_table(table, groups):
     pairs, _, rows, half_slots = table.shape
     assert half_slots % LANES == 1
-    length = 2 * (pairs // groups) * (half_slots // LANES) + 1
-    return pl.pallas_call(
-        pack_kernel,
-        in_specs=[VMEM],
-        out_specs=[VMEM] * groups,
-        out_shape=[jax.ShapeDtypeStruct((length, rows, LANES), BF)] * groups,
-        compiler_params=PARAMS,
-        name="pack_table",
-    )(table)
+    group = pairs // groups
+    length = 2 * group * (half_slots // LANES) + 1
+    return [
+        pl.pallas_call(
+            functools.partial(pack_kernel, g * group),
+            in_specs=[pl.BlockSpec(memory_space=pltpu.HBM)],
+            out_specs=VMEM,
+            out_shape=jax.ShapeDtypeStruct((length, rows, LANES), BF),
+            scratch_shapes=[pltpu.VMEM((group, 2, rows, half_slots), BF), pltpu.SemaphoreType.DMA],
+            compiler_params=pltpu.CompilerParams(vmem_limit_bytes=60 * 1024 * 1024),
+            name="pack_table",
+        )(table)
+        for g in range(groups)
+    ]
 
 
 def even_partner(z):

time: 110 us -> 113 us (1.027)
  Pallas kernels: 9.75 us -> 13.1 us
  other arithmetic: 0.2 us -> 2.06 us
    pallas_call x1 -> x2, Pallas kernels: 0.09 us -> 3.43 us  [pack_table(): pl.pallas_call(functools.partial(pack_kernel, g * group), in_specs=[pl.Bl...]
    concatenate x2, other arithmetic: 0.08 us -> 1.94 us  [gather_table(): sent = jnp.concatenate(parts, axis=0) if step == 1 else parts[-1]]
    unnamed x9 -> x11, local copies, waits for them, and re-layouts: 3.42 us -> 2.43 us
  transfers between devices with their start and end apart: 9 -> 9, of which waited for: 5 -> 5; matrix products, arithmetic and copies ran while one was open for 3% -> 4% of each run, Pallas kernels for 3% -> 4%
where the time goes in v6:
time: 113 us
  waiting for transfers between devices  50.4 us (45%)
  starting transfers between devices  43.8 us (39%)
  Pallas kernels  13.1 us (12%)
  local copies, waits for them, and re-layouts  2.98 us (3%)
  other arithmetic  2.06 us (2%)
    all_to_all x1, waiting for transfers between devices, on_device(): lax.all_to_all(sent, 'wave', split_axis=0, concat_axis=0, tiled=True)  33.6 us
    ppermute x8, starting transfers between devices, gather_table(): parts.append(lax.ppermute(sent, 'fld', kinds[(first + step) % 2]))  30.8 us
    ppermute x8, waiting for transfers between devices, gather_table(): parts.append(lax.ppermute(sent, 'fld', kinds[(first + step) % 2]))  16.8 us
    all_to_all x1, starting transfers between devices, on_device(): lax.all_to_all(sent, 'wave', split_axis=0, concat_axis=0, tiled=True)  13 us
    pallas_call x2, Pallas kernels, legendre_sums(): pl.pallas_call(functools.partial(sums_kernel, truncation, n_wave, first_p...  5.96 us
    pallas_call x2, Pallas kernels, pack_table(): pl.pallas_call(functools.partial(pack_kernel, g * group), in_specs=[pl.Bl...  3.43 us
    pallas_call x1, Pallas kernels, place_waves(): pl.pallas_call(place_kernel, out_specs=pl.BlockSpec(memory_space=pltpu.HB...  2.76 us
    unnamed x11, local copies, waits for them, and re-layouts  2.43 us
  transfers between devices with their start and end apart: 9, of which 5 were waited for; matrix products, arithmetic and copies ran while one was open for 4% of the time, Pallas kernels for 4%

profile of v6, /device:TPU:1, one launch (start us, length us, event | category | flops | bytes accessed | tf_op | source)
XLA Modules:
  0.0 112.5 jit_solution(13661718727113500225)
XLA Ops:
  0.0 1.7 %pack_table.3.refs_0_ = bf16[51,16,128]{2,1,0:T(8,128)(2,1)} custom-call(bf16[10,2,16,641]{3,2,1,0:T(8,128)(2,1)} %bitcast.12), custom_call_target="tpu_custom_call" | custom-call | tf_op jit(solution)/shard_map/pack_table/pallas_call | solution.py:44
  1.7 4.8 %collective-permute-start.4 = (bf16[51,16,128]{2,1,0:T(8,128)(2,1)}, bf16[51,16,128]{2,1,0:T(8,128)(2,1)S(1)}, u32[]{:S(2)}, u32[]{:S(2)}) collective-permute-start(bf16[51,16,128]{2,1,0:T(8,128)(2,1)} %pack_table.3.refs_0_), channel_id=1, source_target_pairs={{0,1},{1,0},{2,3},{3,2},{4,5},{5,4},{6,7},{7,6},{8,9},{9,8},{10,11... | collective-permute-start | bytes 626696 | tf_op jit(solution)/shard_map/ppermute | solution.py:269
  6.6 1.7 %pack_table.2.refs_0_ = bf16[51,16,128]{2,1,0:T(8,128)(2,1)} custom-call(bf16[10,2,16,641]{3,2,1,0:T(8,128)(2,1)} %bitcast.13), custom_call_target="tpu_custom_call" | custom-call | tf_op jit(solution)/shard_map/pack_table/pallas_call | solution.py:44
  8.3 8.8 %collective-permute-start = (bf16[51,16,128]{2,1,0:T(8,128)(2,1)}, bf16[51,16,128]{2,1,0:T(8,128)(2,1)S(1)}, u32[]{:S(2)}, u32[]{:S(2)}) collective-permute-start(bf16[51,16,128]{2,1,0:T(8,128)(2,1)} %pack_table.2.refs_0_), channel_id=1, source_target_pairs={{0,7},{1,2},{2,1},{3,4},{4,3},{5,6},{6,5},{7,0},{8,15},{9,10},{10,... | collective-permute-start | bytes 626696 | tf_op jit(solution)/shard_map/ppermute | solution.py:269
  17.2 1.0 pad_maximum_fusion.1
  18.1 4.2 %collective-permute-start.5 = (bf16[102,16,128]{2,1,0:T(8,128)(2,1)S(1)}, bf16[102,16,128]{2,1,0:T(8,128)(2,1)S(1)}, u32[]{:S(2)}, u32[]{:S(2)}) collective-permute-start(bf16[102,16,128]{2,1,0:T(8,128)(2,1)S(1)} %pad_maximum_fusion.1), channel_id=1, source_target_pairs={{0,7},{1,2},{2,1},{3,4},{4,3},{5,6},{6,5},{7,0},{8,15},{9,10},{10,... | collective-permute-start | bytes 1253384 | tf_op jit(solution)/shard_map/ppermute | solution.py:269
  22.3 1.0 pad_maximum_fusion
  23.3 1.9 %collective-permute-start.1 = (bf16[102,16,128]{2,1,0:T(8,128)(2,1)S(1)}, bf16[102,16,128]{2,1,0:T(8,128)(2,1)S(1)}, u32[]{:S(2)}, u32[]{:S(2)}) collective-permute-start(bf16[102,16,128]{2,1,0:T(8,128)(2,1)S(1)} %pad_maximum_fusion), channel_id=1, source_target_pairs={{0,1},{1,0},{2,3},{3,2},{4,5},{5,4},{6,7},{7,6},{8,9},{9,8},{10,11... | collective-permute-start | bytes 1253384 | tf_op jit(solution)/shard_map/ppermute | solution.py:269
  25.3 5.9 %collective-permute-done.5.refs_2_ = bf16[102,16,128]{2,1,0:T(8,128)(2,1)S(1)} collective-permute-done((bf16[102,16,128]{2,1,0:T(8,128)(2,1)S(1)}, bf16[102,16,128]{2,1,0:T(8,128)(2,1)S(1)}, u32[]{:S(2)}, u32[]{:S(2)}) %collective-permute-start.5) | collective-permute-done | bytes 417824 | tf_op jit(solution)/shard_map/ppermute | solution.py:269
  31.1 1.9 %collective-permute-start.6 = (bf16[102,16,128]{2,1,0:T(8,128)(2,1)S(1)}, bf16[102,16,128]{2,1,0:T(8,128)(2,1)S(1)}, u32[]{:S(2)}, u32[]{:S(2)}) collective-permute-start(bf16[102,16,128]{2,1,0:T(8,128)(2,1)S(1)} %collective-permute-done.5.refs_2_), channel_id=1, source_target_pairs={{0,1},{1,0},{2,3},{3,2},{4,5},{5,4},{6,7},{7,6},{8,9},{9,8},{10,11... | collective-permute-start | bytes 1253384 | tf_op jit(solution)/shard_map/ppermute | solution.py:269
  33.0 1.5 %collective-permute-done.1.refs_2_ = bf16[102,16,128]{2,1,0:T(8,128)(2,1)S(1)} collective-permute-done((bf16[102,16,128]{2,1,0:T(8,128)(2,1)S(1)}, bf16[102,16,128]{2,1,0:T(8,128)(2,1)S(1)}, u32[]{:S(2)}, u32[]{:S(2)}) %collective-permute-start.1) | collective-permute-done | bytes 417824 | tf_op jit(solution)/shard_map/ppermute | solution.py:269
  34.5 3.8 %collective-permute-start.2 = (bf16[102,16,128]{2,1,0:T(8,128)(2,1)S(1)}, bf16[102,16,128]{2,1,0:T(8,128)(2,1)S(1)}, u32[]{:S(2)}, u32[]{:S(2)}) collective-permute-start(bf16[102,16,128]{2,1,0:T(8,128)(2,1)S(1)} %collective-permute-done.1.refs_2_), channel_id=1, source_target_pairs={{0,7},{1,2},{2,1},{3,4},{4,3},{5,6},{6,5},{7,0},{8,15},{9,10},{10,... | collective-permute-start | bytes 1253384 | tf_op jit(solution)/shard_map/ppermute | solution.py:269
  38.3 6.0 %collective-permute-done.6.refs_3_ = bf16[102,16,128]{2,1,0:T(8,128)(2,1)S(1)} collective-permute-done((bf16[102,16,128]{2,1,0:T(8,128)(2,1)S(1)}, bf16[102,16,128]{2,1,0:T(8,128)(2,1)S(1)}, u32[]{:S(2)}, u32[]{:S(2)}) %collective-permute-start.6) | collective-permute-done | bytes 417824 | tf_op jit(solution)/shard_map/ppermute | solution.py:269
  44.3 3.4 %collective-permute-start.7 = (bf16[102,16,128]{2,1,0:T(8,128)(2,1)S(1)}, bf16[102,16,128]{2,1,0:T(8,128)(2,1)S(1)}, u32[]{:S(2)}, u32[]{:S(2)}) collective-permute-start(bf16[102,16,128]{2,1,0:T(8,128)(2,1)S(1)} %collective-permute-done.6.refs_3_), channel_id=1, source_target_pairs={{0,7},{1,2},{2,1},{3,4},{4,3},{5,6},{6,5},{7,0},{8,15},{9,10},{10,... | collective-permute-start | bytes 1253384 | tf_op jit(solution)/shard_map/ppermute | solution.py:269
  47.7 1.9 %collective-permute-start.3 = (bf16[102,16,128]{2,1,0:T(8,128)(2,1)S(1)}, bf16[102,16,128]{2,1,0:T(8,128)(2,1)S(1)}, u32[]{:S(2)}, u32[]{:S(2)}) collective-permute-start(bf16[102,16,128]{2,1,0:T(8,128)(2,1)S(1)} %collective-permute-done.2.refs_3_), channel_id=1, source_target_pairs={{0,1},{1,0},{2,3},{3,2},{4,5},{5,4},{6,7},{7,6},{8,9},{9,8},{10,11... | collective-permute-start | bytes 1253384 | tf_op jit(solution)/shard_map/ppermute | solution.py:269
  49.7 0.0 copy-start.3
  49.7 0.0 copy-start.2
  49.7 2.4 %copy.13.spec_ref = bf16[10,2,641,128]{3,2,1,0:T(8,128)(2,1)S(1)} copy(bf16[10,2,641,128]{3,1,2,0:T(2,128)(2,1)} %param.5) | data formatting | bytes 6563840 | tf_op args[0]
  52.1 0.1 pad_add_fusion.2.place_ref
  52.2 0.9 row_order.1
  53.1 3.5 %collective-permute-done.7.refs_4_ = bf16[102,16,128]{2,1,0:T(8,128)(2,1)S(1)} collective-permute-done((bf16[102,16,128]{2,1,0:T(8,128)(2,1)S(1)}, bf16[102,16,128]{2,1,0:T(8,128)(2,1)S(1)}, u32[]{:S(2)}, u32[]{:S(2)}) %collective-permute-start.7) | collective-permute-done | bytes 417824 | tf_op jit(solution)/shard_map/ppermute | solution.py:269
  56.6 2.3 %legendre_sums.2.refs_5_ = f32[5120,128]{1,0:T(8,128)S(1)} custom-call(s32[2]{0:T(128)S(1)} %pad_add_fusion.2.place_ref, s32[640]{0:T(1024)S(1)} %copy-done.2, bf16[256,256]{1,0:T(8,128)(2,1)S(1)} %get-tuple-element.12.pick_ref, f32[256,128]{1,0:T(8,128)S(1)} %get-tuple-element.11.limit_ref, bf16[10,2,641,128]{3,2,1,0:T(8,128)(2,1)S(1)} %copy.13.spec_ref, ...), custom_call_target="tpu_custom_call" | custom-call | tf_op jit(solution)/shard_map/legendre_sums/pallas_call | solution.py:204
  59.0 3.6 %legendre_sums.3 = bf16[5120,128]{1,0:T(8,128)(2,1)} custom-call(s32[2]{0:T(128)S(1)} %pad_add_fusion.2.place_ref, s32[640]{0:T(1024)S(1)} %copy-done.2, bf16[256,256]{1,0:T(8,128)(2,1)S(1)} %get-tuple-element.10.pick_ref, f32[256,128]{1,0:T(8,128)S(1)} %get-tuple-element.11.limit_ref, bf16[10,2,641,128]{3,2,1,0:T(8,128)(2,1)S(1)} %copy.13.spec_ref, ...), custom_call_target="tpu_custom_call" | custom-call | tf_op jit(solution)/shard_map/legendre_sums/pallas_call | solution.py:204
  62.6 13.0 %all-to-all-start = ((bf16[64,80,128]{2,1,0:T(8,128)(2,1)}), bf16[64,80,128]{2,1,0:T(8,128)(2,1)S(1)}, u32[]{:S(2)}, u32[]{:S(2)}) async-start(bf16[64,80,128]{2,1,0:T(8,128)(2,1)} %bitcast.5), calls=%async_computation | async-start | bytes 2621440 | tf_op jit(solution)/shard_map/all_to_all | solution.py:291
  75.6 0.1 stack_reshape.3
  75.7 0.1 copy.14
  75.8 0.1 copy.15
  75.9 0.1 copy.16
  76.0 0.1 reshape.36
  76.1 0.1 reshape.37
  76.2 33.6 %all-to-all-done.received_ref = bf16[64,80,128]{2,1,0:T(8,128)(2,1)S(1)} async-done(((bf16[64,80,128]{2,1,0:T(8,128)(2,1)}), bf16[64,80,128]{2,1,0:T(8,128)(2,1)S(1)}, u32[]{:S(2)}, u32[]{:S(2)}) %all-to-all-start) | async-done | bytes 1310752 | tf_op jit(solution)/shard_map/all_to_all | solution.py:291
  109.7 2.8 %place_waves.1 = bf16[4,1280,128]{2,1,0:T(8,128)(2,1)} custom-call(s32[1,1280]{1,0:T(1,128)S(1)} %reshape.38.waves_ref, bf16[64,80,128]{2,1,0:T(8,128)(2,1)S(1)} %all-to-all-done.received_ref), custom_call_target="tpu_custom_call" | custom-call | tf_op jit(solution)/shard_map/place_waves/pallas_call | solution.py:244
  (19 shorter events, 0.1 us)
Async XLA Ops:
  1.7 15.4 %collective-permute-start.4 = (bf16[51,16,128]{2,1,0:T(8,128)(2,1)}, bf16[51,16,128]{2,1,0:T(8,128)(2,1)S(1)}, u32[]{:S(2)}, u32[]{:S(2)}) collective-permute-start(bf16[51,16,128]{2,1,0:T(8,128)(2,1)} %pack_table.3.refs_0_), channel_id=1, source_target_pairs={{0,1},{1,0},{2,3},{3,2},{4,5},{5,4},{6,7},{7,6},{8,9},{9,8},{10,11... | collective-permute-start | bytes 626696 | tf_op jit(solution)/shard_map/ppermute | solution.py:269
  8.3 14.1 %collective-permute-start = (bf16[51,16,128]{2,1,0:T(8,128)(2,1)}, bf16[51,16,128]{2,1,0:T(8,128)(2,1)S(1)}, u32[]{:S(2)}, u32[]{:S(2)}) collective-permute-start(bf16[51,16,128]{2,1,0:T(8,128)(2,1)} %pack_table.2.refs_0_), channel_id=1, source_target_pairs={{0,7},{1,2},{2,1},{3,4},{4,3},{5,6},{6,5},{7,0},{8,15},{9,10},{10,... | collective-permute-start | bytes 626696 | tf_op jit(solution)/shard_map/ppermute | solution.py:269
  18.1 13.0 %collective-permute-start.5 = (bf16[102,16,128]{2,1,0:T(8,128)(2,1)S(1)}, bf16[102,16,128]{2,1,0:T(8,128)(2,1)S(1)}, u32[]{:S(2)}, u32[]{:S(2)}) collective-permute-start(bf16[102,16,128]{2,1,0:T(8,128)(2,1)S(1)} %pad_maximum_fusion.1), channel_id=1, source_target_pairs={{0,7},{1,2},{2,1},{3,4},{4,3},{5,6},{6,5},{7,0},{8,15},{9,10},{10,... | collective-permute-start | bytes 1253384 | tf_op jit(solution)/shard_map/ppermute | solution.py:269
  23.3 11.2 %collective-permute-start.1 = (bf16[102,16,128]{2,1,0:T(8,128)(2,1)S(1)}, bf16[102,16,128]{2,1,0:T(8,128)(2,1)S(1)}, u32[]{:S(2)}, u32[]{:S(2)}) collective-permute-start(bf16[102,16,128]{2,1,0:T(8,128)(2,1)S(1)} %pad_maximum_fusion), channel_id=1, source_target_pairs={{0,1},{1,0},{2,3},{3,2},{4,5},{5,4},{6,7},{7,6},{8,9},{9,8},{10,11... | collective-permute-start | bytes 1253384 | tf_op jit(solution)/shard_map/ppermute | solution.py:269
  31.1 13.2 %collective-permute-start.6 = (bf16[102,16,128]{2,1,0:T(8,128)(2,1)S(1)}, bf16[102,16,128]{2,1,0:T(8,128)(2,1)S(1)}, u32[]{:S(2)}, u32[]{:S(2)}) collective-permute-start(bf16[102,16,128]{2,1,0:T(8,128)(2,1)S(1)} %collective-permute-done.5.refs_2_), channel_id=1, source_target_pairs={{0,1},{1,0},{2,3},{3,2},{4,5},{5,4},{6,7},{7,6},{8,9},{9,8},{10,11... | collective-permute-start | bytes 1253384 | tf_op jit(solution)/shard_map/ppermute | solution.py:269
  34.5 13.2 %collective-permute-start.2 = (bf16[102,16,128]{2,1,0:T(8,128)(2,1)S(1)}, bf16[102,16,128]{2,1,0:T(8,128)(2,1)S(1)}, u32[]{:S(2)}, u32[]{:S(2)}) collective-permute-start(bf16[102,16,128]{2,1,0:T(8,128)(2,1)S(1)} %collective-permute-done.1.refs_2_), channel_id=1, source_target_pairs={{0,7},{1,2},{2,1},{3,4},{4,3},{5,6},{6,5},{7,0},{8,15},{9,10},{10,... | collective-permute-start | bytes 1253384 | tf_op jit(solution)/shard_map/ppermute | solution.py:269
  44.3 12.3 %collective-permute-start.7 = (bf16[102,16,128]{2,1,0:T(8,128)(2,1)S(1)}, bf16[102,16,128]{2,1,0:T(8,128)(2,1)S(1)}, u32[]{:S(2)}, u32[]{:S(2)}) collective-permute-start(bf16[102,16,128]{2,1,0:T(8,128)(2,1)S(1)} %collective-permute-done.6.refs_3_), channel_id=1, source_target_pairs={{0,7},{1,2},{2,1},{3,4},{4,3},{5,6},{6,5},{7,0},{8,15},{9,10},{10,... | collective-permute-start | bytes 1253384 | tf_op jit(solution)/shard_map/ppermute | solution.py:269
  47.7 11.2 %collective-permute-start.3 = (bf16[102,16,128]{2,1,0:T(8,128)(2,1)S(1)}, bf16[102,16,128]{2,1,0:T(8,128)(2,1)S(1)}, u32[]{:S(2)}, u32[]{:S(2)}) collective-permute-start(bf16[102,16,128]{2,1,0:T(8,128)(2,1)S(1)} %collective-permute-done.2.refs_3_), channel_id=1, source_target_pairs={{0,1},{1,0},{2,3},{3,2},{4,5},{5,4},{6,7},{7,6},{8,9},{9,8},{10,11... | collective-permute-start | bytes 1253384 | tf_op jit(solution)/shard_map/ppermute | solution.py:269
  49.7 2.5 %copy-start.3 = (s32[256]{0:T(256)S(1)}, s32[256]{0:T(256)}, u32[]{:S(2)}) copy-start(s32[256]{0:T(256)} %param.8) | copy-start | bytes 3076
  49.7 2.5 %copy-start.4 = (s32[128]{0:T(128)S(1)}, s32[128]{0:T(128)}, u32[]{:S(2)}) copy-start(s32[128]{0:T(128)} %param.9) | copy-start | bytes 1540
  49.7 6.9 %copy-start.1 = (bf16[51,16,128]{2,1,0:T(8,128)(2,1)S(1)}, bf16[51,16,128]{2,1,0:T(8,128)(2,1)}, u32[]{:S(2)}) copy-start(bf16[51,16,128]{2,1,0:T(8,128)(2,1)} %pack_table.3.refs_0_) | copy-start | bytes 626692
  49.7 6.9 %copy-start.2 = (s32[640]{0:T(1024)S(1)}, s32[640]{0:T(1024)}, u32[]{:S(2)}) copy-start(s32[640]{0:T(1024)} %lower_ref.3) | copy-start | bytes 7684
  56.6 2.4 %copy-start = (bf16[51,16,128]{2,1,0:T(8,128)(2,1)S(1)}, bf16[51,16,128]{2,1,0:T(8,128)(2,1)}, u32[]{:S(2)}) copy-start(bf16[51,16,128]{2,1,0:T(8,128)(2,1)} %pack_table.2.refs_0_) | copy-start | bytes 626692
  62.6 47.1 %all-to-all-start = ((bf16[64,80,128]{2,1,0:T(8,128)(2,1)}), bf16[64,80,128]{2,1,0:T(8,128)(2,1)S(1)}, u32[]{:S(2)}, u32[]{:S(2)}) async-start(bf16[64,80,128]{2,1,0:T(8,128)(2,1)} %bitcast.5), calls=%async_computation | async-start | bytes 2621440 | tf_op jit(solution)/shard_map/all_to_all | solution.py:291

commit v7 on v5

--- a/solution.py
+++ b/solution.py
@@ -133,15 +133,18 @@
             begin = length + lax.rem(length, 2)
             tails = block(2 * group * blocks)
             sums = []
+            first = [
+                jnp.concatenate([block((2 * i + r) * blocks + b) for b in range(PLAIN)], axis=1) for r in range(2)
+            ]
+            plain_coeffs = jnp.concatenate([spec_ref[pair, r, :plain, :] for r in range(2)], axis=1)
+            below = jnp.dot(jnp.concatenate(first, axis=0), plain_coeffs, preferred_element_type=F32)
+            below = [below[:first[0].shape[0], :columns], below[first[0].shape[0]:, columns:]]
             for r in range(2):
                 def owned(slot, coeffs, lower):
                     kept = slot < length if lower else (slot >= begin) & (slot <= begin + q)
                     return jnp.where(kept, coeffs, 0.0).astype(BF)
 
-                table = [block((2 * i + r) * blocks + b) for b in range(blocks)]
-                below = jnp.dot(
-                    jnp.concatenate(table[:PLAIN], axis=1), spec_ref[pair, r, :plain, :], preferred_element_type=F32
-                )
+                table = [block((2 * i + r) * blocks + b) for b in range(PLAIN, blocks)]
                 coeffs = spec_ref[pair, r, plain:full, :].astype(F32)
                 slot = 2 * (lax.broadcasted_iota(jnp.int32, coeffs.shape, 0) + plain) + r
                 row = lax.broadcasted_iota(jnp.int32, (LANES, columns), 0)
@@ -152,11 +155,11 @@
                     for lower in (True, False)
                 ]
                 above = jnp.dot(
-                    jnp.concatenate(table[PLAIN:] + [tails], axis=1),
+                    jnp.concatenate(table + [tails], axis=1),
                     jnp.concatenate(both, axis=1),
                     preferred_element_type=F32,
                 )
-                sums.append((above[:, :columns] + below, above[:, columns:]))
+                sums.append((above[:, :columns] + below[r], above[:, columns:]))
             north = jnp.concatenate([sums[0][h] + sums[1][h] for h in range(2)], axis=1)
             south = jnp.concatenate([sums[0][h] - sums[1][h] for h in range(2)], axis=1)
             fourier = jnp.concatenate([north, south], axis=0).astype(BF)

time: 110 us -> 110 us (level)
  no operation moved by 1% of the time
where the time goes in v7:
time: 110 us; the launch traced here: 109 us
  waiting for transfers between devices  50.4 us (46%)
  starting transfers between devices  44.8 us (41%)
  Pallas kernels  9.73 us (9%)
  local copies, waits for them, and re-layouts  3.97 us (4%)
    all_to_all x1, waiting for transfers between devices, on_device(): lax.all_to_all(sent, 'wave', split_axis=0, concat_axis=0, tiled=True)  33.6 us
    ppermute x8, starting transfers between devices, gather_table(): parts.append(lax.ppermute(sent, 'fld', kinds[(first + step) % 2]))  31.2 us
    ppermute x8, waiting for transfers between devices, gather_table(): parts.append(lax.ppermute(sent, 'fld', kinds[(first + step) % 2]))  16.8 us
    all_to_all x1, starting transfers between devices, on_device(): lax.all_to_all(sent, 'wave', split_axis=0, concat_axis=0, tiled=True)  13.5 us
    pallas_call x2, Pallas kernels, legendre_sums(): pl.pallas_call(functools.partial(sums_kernel, truncation, n_wave, first_p...  5.91 us
    unnamed x9, local copies, waits for them, and re-layouts  3.42 us
    pallas_call x1, Pallas kernels, place_waves(): pl.pallas_call(place_kernel, out_specs=pl.BlockSpec(memory_space=pltpu.HB...  2.78 us
  transfers between devices with their start and end apart: 9, of which 5 were waited for; matrix products, arithmetic and copies ran while one was open for 3% of the time, Pallas kernels for 3%

profile of v7, /device:TPU:1, one launch (start us, length us, event | category | flops | bytes accessed | tf_op | source)
XLA Modules:
  0.0 109.2 jit_solution(289533535236416410)
XLA Ops:
  0.0 1.0 copy-done
  1.0 0.1 pack_table.1
  1.1 4.8 %collective-permute-start.4 = (bf16[51,16,128]{2,1,0:T(8,128)(2,1)S(1)}, bf16[51,16,128]{2,1,0:T(8,128)(2,1)S(1)}, u32[]{:S(2)}, u32[]{:S(2)}) collective-permute-start(bf16[51,16,128]{2,1,0:T(8,128)(2,1)S(1)} %get-tuple-element.16.refs_0_), channel_id=1, source_target_pairs={{0,1},{1,0},{2,3},{3,2},{4,5},{5,4},{6,7},{7,6},{8,9},{9,8},{10,11... | collective-permute-start | bytes 626696 | tf_op jit(solution)/shard_map/ppermute | solution.py:266
  6.0 8.8 %collective-permute-start = (bf16[51,16,128]{2,1,0:T(8,128)(2,1)S(1)}, bf16[51,16,128]{2,1,0:T(8,128)(2,1)S(1)}, u32[]{:S(2)}, u32[]{:S(2)}) collective-permute-start(bf16[51,16,128]{2,1,0:T(8,128)(2,1)S(1)} %get-tuple-element.14.refs_0_), channel_id=1, source_target_pairs={{0,7},{1,2},{2,1},{3,4},{4,3},{5,6},{6,5},{7,0},{8,15},{9,10},{10,... | collective-permute-start | bytes 626696 | tf_op jit(solution)/shard_map/ppermute | solution.py:266
  14.9 5.7 %collective-permute-start.5 = (bf16[102,16,128]{2,1,0:T(8,128)(2,1)S(1)}, bf16[102,16,128]{2,1,0:T(8,128)(2,1)S(1)}, u32[]{:S(2)}, u32[]{:S(2)}) collective-permute-start(bf16[102,16,128]{2,1,0:T(8,128)(2,1)S(1)} %pad_maximum_fusion.1), channel_id=1, source_target_pairs={{0,7},{1,2},{2,1},{3,4},{4,3},{5,6},{6,5},{7,0},{8,15},{9,10},{10,... | collective-permute-start | bytes 1253384 | tf_op jit(solution)/shard_map/ppermute | solution.py:266
  20.6 0.0 collective-permute-done.refs_1_
  20.7 1.9 %collective-permute-start.1 = (bf16[102,16,128]{2,1,0:T(8,128)(2,1)S(1)}, bf16[102,16,128]{2,1,0:T(8,128)(2,1)S(1)}, u32[]{:S(2)}, u32[]{:S(2)}) collective-permute-start(bf16[102,16,128]{2,1,0:T(8,128)(2,1)S(1)} %pad_maximum_fusion), channel_id=1, source_target_pairs={{0,1},{1,0},{2,3},{3,2},{4,5},{5,4},{6,7},{7,6},{8,9},{9,8},{10,11... | collective-permute-start | bytes 1253384 | tf_op jit(solution)/shard_map/ppermute | solution.py:266
  22.6 6.4 %collective-permute-done.5.refs_2_ = bf16[102,16,128]{2,1,0:T(8,128)(2,1)S(1)} collective-permute-done((bf16[102,16,128]{2,1,0:T(8,128)(2,1)S(1)}, bf16[102,16,128]{2,1,0:T(8,128)(2,1)S(1)}, u32[]{:S(2)}, u32[]{:S(2)}) %collective-permute-start.5) | collective-permute-done | bytes 417824 | tf_op jit(solution)/shard_map/ppermute | solution.py:266
  29.0 1.9 %collective-permute-start.6 = (bf16[102,16,128]{2,1,0:T(8,128)(2,1)S(1)}, bf16[102,16,128]{2,1,0:T(8,128)(2,1)S(1)}, u32[]{:S(2)}, u32[]{:S(2)}) collective-permute-start(bf16[102,16,128]{2,1,0:T(8,128)(2,1)S(1)} %collective-permute-done.5.refs_2_), channel_id=1, source_target_pairs={{0,1},{1,0},{2,3},{3,2},{4,5},{5,4},{6,7},{7,6},{8,9},{9,8},{10,11... | collective-permute-start | bytes 1253384 | tf_op jit(solution)/shard_map/ppermute | solution.py:266
  30.9 1.0 collective-permute-done.1.refs_2_
  31.9 3.4 %collective-permute-start.2 = (bf16[102,16,128]{2,1,0:T(8,128)(2,1)S(1)}, bf16[102,16,128]{2,1,0:T(8,128)(2,1)S(1)}, u32[]{:S(2)}, u32[]{:S(2)}) collective-permute-start(bf16[102,16,128]{2,1,0:T(8,128)(2,1)S(1)} %collective-permute-done.1.refs_2_), channel_id=1, source_target_pairs={{0,7},{1,2},{2,1},{3,4},{4,3},{5,6},{6,5},{7,0},{8,15},{9,10},{10,... | collective-permute-start | bytes 1253384 | tf_op jit(solution)/shard_map/ppermute | solution.py:266
  35.2 5.9 %collective-permute-done.6.refs_3_ = bf16[102,16,128]{2,1,0:T(8,128)(2,1)S(1)} collective-permute-done((bf16[102,16,128]{2,1,0:T(8,128)(2,1)S(1)}, bf16[102,16,128]{2,1,0:T(8,128)(2,1)S(1)}, u32[]{:S(2)}, u32[]{:S(2)}) %collective-permute-start.6) | collective-permute-done | bytes 417824 | tf_op jit(solution)/shard_map/ppermute | solution.py:266
  41.1 2.7 %collective-permute-start.7 = (bf16[102,16,128]{2,1,0:T(8,128)(2,1)S(1)}, bf16[102,16,128]{2,1,0:T(8,128)(2,1)S(1)}, u32[]{:S(2)}, u32[]{:S(2)}) collective-permute-start(bf16[102,16,128]{2,1,0:T(8,128)(2,1)S(1)} %collective-permute-done.6.refs_3_), channel_id=1, source_target_pairs={{0,7},{1,2},{2,1},{3,4},{4,3},{5,6},{6,5},{7,0},{8,15},{9,10},{10,... | collective-permute-start | bytes 1253384 | tf_op jit(solution)/shard_map/ppermute | solution.py:266
  43.8 1.9 %collective-permute-start.3 = (bf16[102,16,128]{2,1,0:T(8,128)(2,1)S(1)}, bf16[102,16,128]{2,1,0:T(8,128)(2,1)S(1)}, u32[]{:S(2)}, u32[]{:S(2)}) collective-permute-start(bf16[102,16,128]{2,1,0:T(8,128)(2,1)S(1)} %collective-permute-done.2.refs_3_), channel_id=1, source_target_pairs={{0,1},{1,0},{2,3},{3,2},{4,5},{5,4},{6,7},{7,6},{8,9},{9,8},{10,11... | collective-permute-start | bytes 1253384 | tf_op jit(solution)/shard_map/ppermute | solution.py:266
  45.8 0.0 copy-start.2
  45.8 0.0 copy-start.3
  45.8 0.0 copy-start.1
  45.8 2.4 %copy.13.spec_ref = bf16[10,2,641,128]{3,2,1,0:T(8,128)(2,1)S(1)} copy(bf16[10,2,641,128]{3,1,2,0:T(2,128)(2,1)} %param.5) | data formatting | bytes 6563840 | tf_op args[0]
  48.2 0.1 pad_add_fusion.2.place_ref
  48.3 0.9 row_order.1
  49.2 3.6 %collective-permute-done.7.refs_4_ = bf16[102,16,128]{2,1,0:T(8,128)(2,1)S(1)} collective-permute-done((bf16[102,16,128]{2,1,0:T(8,128)(2,1)S(1)}, bf16[102,16,128]{2,1,0:T(8,128)(2,1)S(1)}, u32[]{:S(2)}, u32[]{:S(2)}) %collective-permute-start.7) | collective-permute-done | bytes 417824 | tf_op jit(solution)/shard_map/ppermute | solution.py:266
  52.8 2.3 %legendre_sums.2.refs_5_ = f32[5120,128]{1,0:T(8,128)S(1)} custom-call(s32[2]{0:T(128)S(1)} %pad_add_fusion.2.place_ref, s32[640]{0:T(1024)S(1)} %copy-done.1, bf16[256,256]{1,0:T(8,128)(2,1)S(1)} %get-tuple-element.15.pick_ref, f32[256,128]{1,0:T(8,128)S(1)} %get-tuple-element.13.limit_ref, bf16[10,2,641,128]{3,2,1,0:T(8,128)(2,1)S(1)} %copy.13.spec_ref, ...), custom_call_target="tpu_custom_call" | custom-call | tf_op jit(solution)/shard_map/legendre_sums/pallas_call | solution.py:201
  55.2 3.6 %legendre_sums.3 = bf16[5120,128]{1,0:T(8,128)(2,1)} custom-call(s32[2]{0:T(128)S(1)} %pad_add_fusion.2.place_ref, s32[640]{0:T(1024)S(1)} %copy-done.1, bf16[256,256]{1,0:T(8,128)(2,1)S(1)} %get-tuple-element.12.pick_ref, f32[256,128]{1,0:T(8,128)S(1)} %get-tuple-element.13.limit_ref, bf16[10,2,641,128]{3,2,1,0:T(8,128)(2,1)S(1)} %copy.13.spec_ref, ...), custom_call_target="tpu_custom_call" | custom-call | tf_op jit(solution)/shard_map/legendre_sums/pallas_call | solution.py:201
  58.8 13.5 %all-to-all-start = ((bf16[64,80,128]{2,1,0:T(8,128)(2,1)}), bf16[64,80,128]{2,1,0:T(8,128)(2,1)S(1)}, u32[]{:S(2)}, u32[]{:S(2)}) async-start(bf16[64,80,128]{2,1,0:T(8,128)(2,1)} %bitcast.5), calls=%async_computation | async-start | bytes 2621440 | tf_op jit(solution)/shard_map/all_to_all | solution.py:288
  72.3 0.1 stack_reshape.3
  72.4 0.1 copy.14
  72.5 0.1 copy.15
  72.6 0.1 copy.16
  72.7 0.1 reshape.36
  72.8 0.1 reshape.37
  72.9 33.6 %all-to-all-done.received_ref = bf16[64,80,128]{2,1,0:T(8,128)(2,1)S(1)} async-done(((bf16[64,80,128]{2,1,0:T(8,128)(2,1)}), bf16[64,80,128]{2,1,0:T(8,128)(2,1)S(1)}, u32[]{:S(2)}, u32[]{:S(2)}) %all-to-all-start) | async-done | bytes 1310752 | tf_op jit(solution)/shard_map/all_to_all | solution.py:288
  106.5 2.8 %place_waves.1 = bf16[4,1280,128]{2,1,0:T(8,128)(2,1)} custom-call(s32[1,1280]{1,0:T(1,128)S(1)} %reshape.38.waves_ref, bf16[64,80,128]{2,1,0:T(8,128)(2,1)S(1)} %all-to-all-done.received_ref), custom_call_target="tpu_custom_call" | custom-call | tf_op jit(solution)/shard_map/place_waves/pallas_call | solution.py:241
  (16 shorter events, 0.2 us)
Async XLA Ops:
  0.0 1.0 copy-start
  1.1 13.7 %collective-permute-start.4 = (bf16[51,16,128]{2,1,0:T(8,128)(2,1)S(1)}, bf16[51,16,128]{2,1,0:T(8,128)(2,1)S(1)}, u32[]{:S(2)}, u32[]{:S(2)}) collective-permute-start(bf16[51,16,128]{2,1,0:T(8,128)(2,1)S(1)} %get-tuple-element.16.refs_0_), channel_id=1, source_target_pairs={{0,1},{1,0},{2,3},{3,2},{4,5},{5,4},{6,7},{7,6},{8,9},{9,8},{10,11... | collective-permute-start | bytes 626696 | tf_op jit(solution)/shard_map/ppermute | solution.py:266
  6.0 14.6 %collective-permute-start = (bf16[51,16,128]{2,1,0:T(8,128)(2,1)S(1)}, bf16[51,16,128]{2,1,0:T(8,128)(2,1)S(1)}, u32[]{:S(2)}, u32[]{:S(2)}) collective-permute-start(bf16[51,16,128]{2,1,0:T(8,128)(2,1)S(1)} %get-tuple-element.14.refs_0_), channel_id=1, source_target_pairs={{0,7},{1,2},{2,1},{3,4},{4,3},{5,6},{6,5},{7,0},{8,15},{9,10},{10,... | collective-permute-start | bytes 626696 | tf_op jit(solution)/shard_map/ppermute | solution.py:266
  14.9 14.1 %collective-permute-start.5 = (bf16[102,16,128]{2,1,0:T(8,128)(2,1)S(1)}, bf16[102,16,128]{2,1,0:T(8,128)(2,1)S(1)}, u32[]{:S(2)}, u32[]{:S(2)}) collective-permute-start(bf16[102,16,128]{2,1,0:T(8,128)(2,1)S(1)} %pad_maximum_fusion.1), channel_id=1, source_target_pairs={{0,7},{1,2},{2,1},{3,4},{4,3},{5,6},{6,5},{7,0},{8,15},{9,10},{10,... | collective-permute-start | bytes 1253384 | tf_op jit(solution)/shard_map/ppermute | solution.py:266
  20.7 11.2 %collective-permute-start.1 = (bf16[102,16,128]{2,1,0:T(8,128)(2,1)S(1)}, bf16[102,16,128]{2,1,0:T(8,128)(2,1)S(1)}, u32[]{:S(2)}, u32[]{:S(2)}) collective-permute-start(bf16[102,16,128]{2,1,0:T(8,128)(2,1)S(1)} %pad_maximum_fusion), channel_id=1, source_target_pairs={{0,1},{1,0},{2,3},{3,2},{4,5},{5,4},{6,7},{7,6},{8,9},{9,8},{10,11... | collective-permute-start | bytes 1253384 | tf_op jit(solution)/shard_map/ppermute | solution.py:266
  29.0 12.1 %collective-permute-start.6 = (bf16[102,16,128]{2,1,0:T(8,128)(2,1)S(1)}, bf16[102,16,128]{2,1,0:T(8,128)(2,1)S(1)}, u32[]{:S(2)}, u32[]{:S(2)}) collective-permute-start(bf16[102,16,128]{2,1,0:T(8,128)(2,1)S(1)} %collective-permute-done.5.refs_2_), channel_id=1, source_target_pairs={{0,1},{1,0},{2,3},{3,2},{4,5},{5,4},{6,7},{7,6},{8,9},{9,8},{10,11... | collective-permute-start | bytes 1253384 | tf_op jit(solution)/shard_map/ppermute | solution.py:266
  31.9 12.0 %collective-permute-start.2 = (bf16[102,16,128]{2,1,0:T(8,128)(2,1)S(1)}, bf16[102,16,128]{2,1,0:T(8,128)(2,1)S(1)}, u32[]{:S(2)}, u32[]{:S(2)}) collective-permute-start(bf16[102,16,128]{2,1,0:T(8,128)(2,1)S(1)} %collective-permute-done.1.refs_2_), channel_id=1, source_target_pairs={{0,7},{1,2},{2,1},{3,4},{4,3},{5,6},{6,5},{7,0},{8,15},{9,10},{10,... | collective-permute-start | bytes 1253384 | tf_op jit(solution)/shard_map/ppermute | solution.py:266
  41.1 11.7 %collective-permute-start.7 = (bf16[102,16,128]{2,1,0:T(8,128)(2,1)S(1)}, bf16[102,16,128]{2,1,0:T(8,128)(2,1)S(1)}, u32[]{:S(2)}, u32[]{:S(2)}) collective-permute-start(bf16[102,16,128]{2,1,0:T(8,128)(2,1)S(1)} %collective-permute-done.6.refs_3_), channel_id=1, source_target_pairs={{0,7},{1,2},{2,1},{3,4},{4,3},{5,6},{6,5},{7,0},{8,15},{9,10},{10,... | collective-permute-start | bytes 1253384 | tf_op jit(solution)/shard_map/ppermute | solution.py:266
  43.8 11.3 %collective-permute-start.3 = (bf16[102,16,128]{2,1,0:T(8,128)(2,1)S(1)}, bf16[102,16,128]{2,1,0:T(8,128)(2,1)S(1)}, u32[]{:S(2)}, u32[]{:S(2)}) collective-permute-start(bf16[102,16,128]{2,1,0:T(8,128)(2,1)S(1)} %collective-permute-done.2.refs_3_), channel_id=1, source_target_pairs={{0,1},{1,0},{2,3},{3,2},{4,5},{5,4},{6,7},{7,6},{8,9},{9,8},{10,11... | collective-permute-start | bytes 1253384 | tf_op jit(solution)/shard_map/ppermute | solution.py:266
  45.8 2.5 %copy-start.2 = (s32[256]{0:T(256)S(1)}, s32[256]{0:T(256)}, u32[]{:S(2)}) copy-start(s32[256]{0:T(256)} %param.8) | copy-start | bytes 3076
  45.8 2.5 %copy-start.3 = (s32[128]{0:T(128)S(1)}, s32[128]{0:T(128)}, u32[]{:S(2)}) copy-start(s32[128]{0:T(128)} %param.9) | copy-start | bytes 1540
  45.8 7.0 %copy-start.1 = (s32[640]{0:T(1024)S(1)}, s32[640]{0:T(1024)}, u32[]{:S(2)}) copy-start(s32[640]{0:T(1024)} %lower_ref.3) | copy-start | bytes 7684
  58.8 47.7 %all-to-all-start = ((bf16[64,80,128]{2,1,0:T(8,128)(2,1)}), bf16[64,80,128]{2,1,0:T(8,128)(2,1)S(1)}, u32[]{:S(2)}, u32[]{:S(2)}) async-start(bf16[64,80,128]{2,1,0:T(8,128)(2,1)} %bitcast.5), calls=%async_computation | async-start | bytes 2621440 | tf_op jit(solution)/shard_map/all_to_all | solution.py:288

commit v8 on v6

--- a/solution.py
+++ b/solution.py
@@ -47,7 +47,7 @@
             out_specs=VMEM,
             out_shape=jax.ShapeDtypeStruct((length, rows, LANES), BF),
             scratch_shapes=[pltpu.VMEM((group, 2, rows, half_slots), BF), pltpu.SemaphoreType.DMA],
-            compiler_params=pltpu.CompilerParams(vmem_limit_bytes=60 * 1024 * 1024),
+            compiler_params=PARAMS,
             name="pack_table",
         )(table)
         for g in range(groups)

time: 113 us -> 110 us (0.973)
  Pallas kernels: 13.1 us -> 10.5 us
  other arithmetic: 2.06 us -> 0.2 us
    pallas_call x2, Pallas kernels: 3.43 us -> 0.85 us  [pack_table(): pl.pallas_call(functools.partial(pack_kernel, g * group), in_specs=[pl.Bl...]
    concatenate x2, other arithmetic: 1.94 us -> 0.08 us  [gather_table(): sent = jnp.concatenate(parts, axis=0) if step == 1 else parts[-1]]
    unnamed x11 -> x9, local copies, waits for them, and re-layouts: 2.43 us -> 3.42 us
  transfers between devices with their start and end apart: 9 -> 9, of which waited for: 5 -> 5; matrix products, arithmetic and copies ran while one was open for 4% -> 3% of each run, Pallas kernels for 4% -> 3%
where the time goes in v8:
time: 110 us
  waiting for transfers between devices  50.3 us (46%)
  starting transfers between devices  44.4 us (40%)
  Pallas kernels  10.5 us (10%)
  local copies, waits for them, and re-layouts  3.97 us (4%)
    all_to_all x1, waiting for transfers between devices, on_device(): lax.all_to_all(sent, 'wave', split_axis=0, concat_axis=0, tiled=True)  33.6 us
    ppermute x8, starting transfers between devices, gather_table(): parts.append(lax.ppermute(sent, 'fld', kinds[(first + step) % 2]))  30.8 us
    ppermute x8, waiting for transfers between devices, gather_table(): parts.append(lax.ppermute(sent, 'fld', kinds[(first + step) % 2]))  16.8 us
    all_to_all x1, starting transfers between devices, on_device(): lax.all_to_all(sent, 'wave', split_axis=0, concat_axis=0, tiled=True)  13.5 us
    pallas_call x2, Pallas kernels, legendre_sums(): pl.pallas_call(functools.partial(sums_kernel, truncation, n_wave, first_p...  5.95 us
    unnamed x9, local copies, waits for them, and re-layouts  3.42 us
    pallas_call x1, Pallas kernels, place_waves(): pl.pallas_call(place_kernel, out_specs=pl.BlockSpec(memory_space=pltpu.HB...  2.76 us
  transfers between devices with their start and end apart: 9, of which 5 were waited for; matrix products, arithmetic and copies ran while one was open for 3% of the time, Pallas kernels for 3%

profile of v8, /device:TPU:1, one launch (start us, length us, event | category | flops | bytes accessed | tf_op | source)
XLA Modules:
  0.0 109.6 jit_solution(11686197040514598230)
XLA Ops:
  0.0 1.0 copy-done
  1.0 0.4 pack_table.3.refs_0_
  1.4 4.8 %collective-permute-start.4 = (bf16[51,16,128]{2,1,0:T(8,128)(2,1)S(1)}, bf16[51,16,128]{2,1,0:T(8,128)(2,1)S(1)}, u32[]{:S(2)}, u32[]{:S(2)}) collective-permute-start(bf16[51,16,128]{2,1,0:T(8,128)(2,1)S(1)} %pack_table.3.refs_0_), channel_id=1, source_target_pairs={{0,1},{1,0},{2,3},{3,2},{4,5},{5,4},{6,7},{7,6},{8,9},{9,8},{10,11... | collective-permute-start | bytes 626696 | tf_op jit(solution)/shard_map/ppermute | solution.py:269
  6.3 0.4 pack_table.2.refs_0_
  6.7 8.8 %collective-permute-start = (bf16[51,16,128]{2,1,0:T(8,128)(2,1)S(1)}, bf16[51,16,128]{2,1,0:T(8,128)(2,1)S(1)}, u32[]{:S(2)}, u32[]{:S(2)}) collective-permute-start(bf16[51,16,128]{2,1,0:T(8,128)(2,1)S(1)} %pack_table.2.refs_0_), channel_id=1, source_target_pairs={{0,7},{1,2},{2,1},{3,4},{4,3},{5,6},{6,5},{7,0},{8,15},{9,10},{10,... | collective-permute-start | bytes 626696 | tf_op jit(solution)/shard_map/ppermute | solution.py:269
  15.7 5.3 %collective-permute-start.5 = (bf16[102,16,128]{2,1,0:T(8,128)(2,1)S(1)}, bf16[102,16,128]{2,1,0:T(8,128)(2,1)S(1)}, u32[]{:S(2)}, u32[]{:S(2)}) collective-permute-start(bf16[102,16,128]{2,1,0:T(8,128)(2,1)S(1)} %pad_maximum_fusion.1), channel_id=1, source_target_pairs={{0,7},{1,2},{2,1},{3,4},{4,3},{5,6},{6,5},{7,0},{8,15},{9,10},{10,... | collective-permute-start | bytes 1253384 | tf_op jit(solution)/shard_map/ppermute | solution.py:269
  21.0 1.9 %collective-permute-start.1 = (bf16[102,16,128]{2,1,0:T(8,128)(2,1)S(1)}, bf16[102,16,128]{2,1,0:T(8,128)(2,1)S(1)}, u32[]{:S(2)}, u32[]{:S(2)}) collective-permute-start(bf16[102,16,128]{2,1,0:T(8,128)(2,1)S(1)} %pad_maximum_fusion), channel_id=1, source_target_pairs={{0,1},{1,0},{2,3},{3,2},{4,5},{5,4},{6,7},{7,6},{8,9},{9,8},{10,11... | collective-permute-start | bytes 1253384 | tf_op jit(solution)/shard_map/ppermute | solution.py:269
  22.9 6.4 %collective-permute-done.5.refs_2_ = bf16[102,16,128]{2,1,0:T(8,128)(2,1)S(1)} collective-permute-done((bf16[102,16,128]{2,1,0:T(8,128)(2,1)S(1)}, bf16[102,16,128]{2,1,0:T(8,128)(2,1)S(1)}, u32[]{:S(2)}, u32[]{:S(2)}) %collective-permute-start.5) | collective-permute-done | bytes 417824 | tf_op jit(solution)/shard_map/ppermute | solution.py:269
  29.3 1.9 %collective-permute-start.6 = (bf16[102,16,128]{2,1,0:T(8,128)(2,1)S(1)}, bf16[102,16,128]{2,1,0:T(8,128)(2,1)S(1)}, u32[]{:S(2)}, u32[]{:S(2)}) collective-permute-start(bf16[102,16,128]{2,1,0:T(8,128)(2,1)S(1)} %collective-permute-done.5.refs_2_), channel_id=1, source_target_pairs={{0,1},{1,0},{2,3},{3,2},{4,5},{5,4},{6,7},{7,6},{8,9},{9,8},{10,11... | collective-permute-start | bytes 1253384 | tf_op jit(solution)/shard_map/ppermute | solution.py:269
  31.2 1.0 collective-permute-done.1.refs_2_
  32.2 3.4 %collective-permute-start.2 = (bf16[102,16,128]{2,1,0:T(8,128)(2,1)S(1)}, bf16[102,16,128]{2,1,0:T(8,128)(2,1)S(1)}, u32[]{:S(2)}, u32[]{:S(2)}) collective-permute-start(bf16[102,16,128]{2,1,0:T(8,128)(2,1)S(1)} %collective-permute-done.1.refs_2_), channel_id=1, source_target_pairs={{0,7},{1,2},{2,1},{3,4},{4,3},{5,6},{6,5},{7,0},{8,15},{9,10},{10,... | collective-permute-start | bytes 1253384 | tf_op jit(solution)/shard_map/ppermute | solution.py:269
  35.6 5.8 %collective-permute-done.6.refs_3_ = bf16[102,16,128]{2,1,0:T(8,128)(2,1)S(1)} collective-permute-done((bf16[102,16,128]{2,1,0:T(8,128)(2,1)S(1)}, bf16[102,16,128]{2,1,0:T(8,128)(2,1)S(1)}, u32[]{:S(2)}, u32[]{:S(2)}) %collective-permute-start.6) | collective-permute-done | bytes 417824 | tf_op jit(solution)/shard_map/ppermute | solution.py:269
  41.4 2.7 %collective-permute-start.7 = (bf16[102,16,128]{2,1,0:T(8,128)(2,1)S(1)}, bf16[102,16,128]{2,1,0:T(8,128)(2,1)S(1)}, u32[]{:S(2)}, u32[]{:S(2)}) collective-permute-start(bf16[102,16,128]{2,1,0:T(8,128)(2,1)S(1)} %collective-permute-done.6.refs_3_), channel_id=1, source_target_pairs={{0,7},{1,2},{2,1},{3,4},{4,3},{5,6},{6,5},{7,0},{8,15},{9,10},{10,... | collective-permute-start | bytes 1253384 | tf_op jit(solution)/shard_map/ppermute | solution.py:269
  44.2 1.9 %collective-permute-start.3 = (bf16[102,16,128]{2,1,0:T(8,128)(2,1)S(1)}, bf16[102,16,128]{2,1,0:T(8,128)(2,1)S(1)}, u32[]{:S(2)}, u32[]{:S(2)}) collective-permute-start(bf16[102,16,128]{2,1,0:T(8,128)(2,1)S(1)} %collective-permute-done.2.refs_3_), channel_id=1, source_target_pairs={{0,1},{1,0},{2,3},{3,2},{4,5},{5,4},{6,7},{7,6},{8,9},{9,8},{10,11... | collective-permute-start | bytes 1253384 | tf_op jit(solution)/shard_map/ppermute | solution.py:269
  46.1 0.0 copy-start.2
  46.1 0.0 copy-start.3
  46.1 0.0 copy-start.1
  46.1 2.4 %copy.13.spec_ref = bf16[10,2,641,128]{3,2,1,0:T(8,128)(2,1)S(1)} copy(bf16[10,2,641,128]{3,1,2,0:T(2,128)(2,1)} %param.5) | data formatting | bytes 6563840 | tf_op args[0]
  48.5 0.1 pad_add_fusion.2.place_ref
  48.6 0.9 row_order.1
  49.5 3.6 %collective-permute-done.7.refs_4_ = bf16[102,16,128]{2,1,0:T(8,128)(2,1)S(1)} collective-permute-done((bf16[102,16,128]{2,1,0:T(8,128)(2,1)S(1)}, bf16[102,16,128]{2,1,0:T(8,128)(2,1)S(1)}, u32[]{:S(2)}, u32[]{:S(2)}) %collective-permute-start.7) | collective-permute-done | bytes 417824 | tf_op jit(solution)/shard_map/ppermute | solution.py:269
  53.2 2.3 %legendre_sums.2.refs_5_ = f32[5120,128]{1,0:T(8,128)S(1)} custom-call(s32[2]{0:T(128)S(1)} %pad_add_fusion.2.place_ref, s32[640]{0:T(1024)S(1)} %copy-done.1, bf16[256,256]{1,0:T(8,128)(2,1)S(1)} %get-tuple-element.12.pick_ref, f32[256,128]{1,0:T(8,128)S(1)} %get-tuple-element.11.limit_ref, bf16[10,2,641,128]{3,2,1,0:T(8,128)(2,1)S(1)} %copy.13.spec_ref, ...), custom_call_target="tpu_custom_call" | custom-call | tf_op jit(solution)/shard_map/legendre_sums/pallas_call | solution.py:204
  55.5 3.6 %legendre_sums.3 = bf16[5120,128]{1,0:T(8,128)(2,1)} custom-call(s32[2]{0:T(128)S(1)} %pad_add_fusion.2.place_ref, s32[640]{0:T(1024)S(1)} %copy-done.1, bf16[256,256]{1,0:T(8,128)(2,1)S(1)} %get-tuple-element.10.pick_ref, f32[256,128]{1,0:T(8,128)S(1)} %get-tuple-element.11.limit_ref, bf16[10,2,641,128]{3,2,1,0:T(8,128)(2,1)S(1)} %copy.13.spec_ref, ...), custom_call_target="tpu_custom_call" | custom-call | tf_op jit(solution)/shard_map/legendre_sums/pallas_call | solution.py:204
  59.1 13.5 %all-to-all-start = ((bf16[64,80,128]{2,1,0:T(8,128)(2,1)}), bf16[64,80,128]{2,1,0:T(8,128)(2,1)S(1)}, u32[]{:S(2)}, u32[]{:S(2)}) async-start(bf16[64,80,128]{2,1,0:T(8,128)(2,1)} %bitcast.5), calls=%async_computation | async-start | bytes 2621440 | tf_op jit(solution)/shard_map/all_to_all | solution.py:291
  72.7 0.1 stack_reshape.3
  72.8 0.1 copy.14
  72.9 0.1 copy.15
  73.0 0.1 copy.16
  73.1 0.1 reshape.36
  73.2 0.1 reshape.37
  73.3 33.6 %all-to-all-done.received_ref = bf16[64,80,128]{2,1,0:T(8,128)(2,1)S(1)} async-done(((bf16[64,80,128]{2,1,0:T(8,128)(2,1)}), bf16[64,80,128]{2,1,0:T(8,128)(2,1)S(1)}, u32[]{:S(2)}, u32[]{:S(2)}) %all-to-all-start) | async-done | bytes 1310752 | tf_op jit(solution)/shard_map/all_to_all | solution.py:291
  106.8 2.8 %place_waves.1 = bf16[4,1280,128]{2,1,0:T(8,128)(2,1)} custom-call(s32[1,1280]{1,0:T(1,128)S(1)} %reshape.38.waves_ref, bf16[64,80,128]{2,1,0:T(8,128)(2,1)S(1)} %all-to-all-done.received_ref), custom_call_target="tpu_custom_call" | custom-call | tf_op jit(solution)/shard_map/place_waves/pallas_call | solution.py:244
  (17 shorter events, 0.2 us)
Async XLA Ops:
  0.0 1.0 copy-start
  1.4 14.2 %collective-permute-start.4 = (bf16[51,16,128]{2,1,0:T(8,128)(2,1)S(1)}, bf16[51,16,128]{2,1,0:T(8,128)(2,1)S(1)}, u32[]{:S(2)}, u32[]{:S(2)}) collective-permute-start(bf16[51,16,128]{2,1,0:T(8,128)(2,1)S(1)} %pack_table.3.refs_0_), channel_id=1, source_target_pairs={{0,1},{1,0},{2,3},{3,2},{4,5},{5,4},{6,7},{7,6},{8,9},{9,8},{10,11... | collective-permute-start | bytes 626696 | tf_op jit(solution)/shard_map/ppermute | solution.py:269
  6.7 14.2 %collective-permute-start = (bf16[51,16,128]{2,1,0:T(8,128)(2,1)S(1)}, bf16[51,16,128]{2,1,0:T(8,128)(2,1)S(1)}, u32[]{:S(2)}, u32[]{:S(2)}) collective-permute-start(bf16[51,16,128]{2,1,0:T(8,128)(2,1)S(1)} %pack_table.2.refs_0_), channel_id=1, source_target_pairs={{0,7},{1,2},{2,1},{3,4},{4,3},{5,6},{6,5},{7,0},{8,15},{9,10},{10,... | collective-permute-start | bytes 626696 | tf_op jit(solution)/shard_map/ppermute | solution.py:269
  15.7 13.7 %collective-permute-start.5 = (bf16[102,16,128]{2,1,0:T(8,128)(2,1)S(1)}, bf16[102,16,128]{2,1,0:T(8,128)(2,1)S(1)}, u32[]{:S(2)}, u32[]{:S(2)}) collective-permute-start(bf16[102,16,128]{2,1,0:T(8,128)(2,1)S(1)} %pad_maximum_fusion.1), channel_id=1, source_target_pairs={{0,7},{1,2},{2,1},{3,4},{4,3},{5,6},{6,5},{7,0},{8,15},{9,10},{10,... | collective-permute-start | bytes 1253384 | tf_op jit(solution)/shard_map/ppermute | solution.py:269
  21.0 11.2 %collective-permute-start.1 = (bf16[102,16,128]{2,1,0:T(8,128)(2,1)S(1)}, bf16[102,16,128]{2,1,0:T(8,128)(2,1)S(1)}, u32[]{:S(2)}, u32[]{:S(2)}) collective-permute-start(bf16[102,16,128]{2,1,0:T(8,128)(2,1)S(1)} %pad_maximum_fusion), channel_id=1, source_target_pairs={{0,1},{1,0},{2,3},{3,2},{4,5},{5,4},{6,7},{7,6},{8,9},{9,8},{10,11... | collective-permute-start | bytes 1253384 | tf_op jit(solution)/shard_map/ppermute | solution.py:269
  29.3 12.1 %collective-permute-start.6 = (bf16[102,16,128]{2,1,0:T(8,128)(2,1)S(1)}, bf16[102,16,128]{2,1,0:T(8,128)(2,1)S(1)}, u32[]{:S(2)}, u32[]{:S(2)}) collective-permute-start(bf16[102,16,128]{2,1,0:T(8,128)(2,1)S(1)} %collective-permute-done.5.refs_2_), channel_id=1, source_target_pairs={{0,1},{1,0},{2,3},{3,2},{4,5},{5,4},{6,7},{7,6},{8,9},{9,8},{10,11... | collective-permute-start | bytes 1253384 | tf_op jit(solution)/shard_map/ppermute | solution.py:269
  32.2 12.0 %collective-permute-start.2 = (bf16[102,16,128]{2,1,0:T(8,128)(2,1)S(1)}, bf16[102,16,128]{2,1,0:T(8,128)(2,1)S(1)}, u32[]{:S(2)}, u32[]{:S(2)}) collective-permute-start(bf16[102,16,128]{2,1,0:T(8,128)(2,1)S(1)} %collective-permute-done.1.refs_2_), channel_id=1, source_target_pairs={{0,7},{1,2},{2,1},{3,4},{4,3},{5,6},{6,5},{7,0},{8,15},{9,10},{10,... | collective-permute-start | bytes 1253384 | tf_op jit(solution)/shard_map/ppermute | solution.py:269
  41.4 11.7 %collective-permute-start.7 = (bf16[102,16,128]{2,1,0:T(8,128)(2,1)S(1)}, bf16[102,16,128]{2,1,0:T(8,128)(2,1)S(1)}, u32[]{:S(2)}, u32[]{:S(2)}) collective-permute-start(bf16[102,16,128]{2,1,0:T(8,128)(2,1)S(1)} %collective-permute-done.6.refs_3_), channel_id=1, source_target_pairs={{0,7},{1,2},{2,1},{3,4},{4,3},{5,6},{6,5},{7,0},{8,15},{9,10},{10,... | collective-permute-start | bytes 1253384 | tf_op jit(solution)/shard_map/ppermute | solution.py:269
  44.2 11.3 %collective-permute-start.3 = (bf16[102,16,128]{2,1,0:T(8,128)(2,1)S(1)}, bf16[102,16,128]{2,1,0:T(8,128)(2,1)S(1)}, u32[]{:S(2)}, u32[]{:S(2)}) collective-permute-start(bf16[102,16,128]{2,1,0:T(8,128)(2,1)S(1)} %collective-permute-done.2.refs_3_), channel_id=1, source_target_pairs={{0,1},{1,0},{2,3},{3,2},{4,5},{5,4},{6,7},{7,6},{8,9},{9,8},{10,11... | collective-permute-start | bytes 1253384 | tf_op jit(solution)/shard_map/ppermute | solution.py:269
  46.1 2.5 %copy-start.2 = (s32[256]{0:T(256)S(1)}, s32[256]{0:T(256)}, u32[]{:S(2)}) copy-start(s32[256]{0:T(256)} %param.8) | copy-start | bytes 3076
  46.1 2.5 %copy-start.3 = (s32[128]{0:T(128)S(1)}, s32[128]{0:T(128)}, u32[]{:S(2)}) copy-start(s32[128]{0:T(128)} %param.9) | copy-start | bytes 1540
  46.1 7.0 %copy-start.1 = (s32[640]{0:T(1024)S(1)}, s32[640]{0:T(1024)}, u32[]{:S(2)}) copy-start(s32[640]{0:T(1024)} %lower_ref.3) | copy-start | bytes 7684
  59.1 47.7 %all-to-all-start = ((bf16[64,80,128]{2,1,0:T(8,128)(2,1)}), bf16[64,80,128]{2,1,0:T(8,128)(2,1)S(1)}, u32[]{:S(2)}, u32[]{:S(2)}) async-start(bf16[64,80,128]{2,1,0:T(8,128)(2,1)} %bitcast.5), calls=%async_computation | async-start | bytes 2621440 | tf_op jit(solution)/shard_map/all_to_all | solution.py:291
